TPU v7x, 32 devices: a whole 2x2x4 slice. The times are simulated.
32 devices in a mesh: expert: 4 (over y, x), dp: 8 (over z, core).
Axes of the slice: x: 2, y: 2, z: 4, core: 2. Of those that a mesh axis runs over, the one named last changes fastest.
Arguments:
- tokens: bfloat16 [4096, 1024], P(('expert', 'dp')), may hold values from -6 to 6
- cotangent: bfloat16 [4096, 1024], P(('expert', 'dp')), may hold values from -6 to 6
- route_gates: float32 [4096, 6], P(('expert', 'dp')), may hold values from 0.2 to 1
- expert_ids: int32 [4096, 6], P(('expert', 'dp')), may hold values from 0 to 63, as said below
- replica: int32 [4096, 6], P(('expert', 'dp')), may hold values from 0 to 1
- hot_experts: int32 [4], replicated, may hold values from 0 to 3, as said below
- w_gate: bfloat16 [4, 2, 1024, 768], P('expert'), as said below
- w_up: bfloat16 [4, 2, 1024, 768], P('expert'), as said below
- w_down: bfloat16 [4, 2, 768, 1024], P('expert'), as said below
Outputs:
- layer_out: bfloat16 [4096, 1024], P(('expert', 'dp'))
- grad_tokens: bfloat16 [4096, 1024], P(('expert', 'dp'))
- grad_down: float32 [4, 768, 1024], P('expert', 'dp')
Inputs may be any that keep to these rules, and one draw needn't show every extreme that they name: `expert_ids`: each row names 6 different experts. `hot_experts`: names each of the 4 experts once and never its own index. `w_gate`: slot 1 of expert s holds the same matrix as slot 0 of expert hot_experts[s]. `w_up`: slot 1 of expert s holds the same matrix as slot 0 of expert hot_experts[s]. `w_down`: slot 1 of expert s holds the same matrix as slot 0 of expert hot_experts[s].
All inputs are finite; a program needn't handle non-finite values.
Results may differ from a plain program's by a relative error of at most 0.0059.
Values may be sent and summed in bfloat16 or wider, within the bound.
No kernel may reach another device: no remote copies, remote signals or barrier semaphores. Data moves between devices by JAX's collectives and lax.ppermute only.
A program may use at most 64 MiB of HBM per device.

v0:
```python
import jax
import jax.numpy as jnp
from jax import lax
from jax.sharding import PartitionSpec as P

CAP = 12


def forward_rows(rows_in, gate_w, up_w, down_w):
    gate_pre = jnp.einsum("spcd,pdf->spcf", rows_in, gate_w, preferred_element_type=jnp.float32)
    up_pre = jnp.einsum("spcd,pdf->spcf", rows_in, up_w, preferred_element_type=jnp.float32)
    sigmoid_g = jax.nn.sigmoid(gate_pre)
    silu_gate = gate_pre * sigmoid_g
    hidden = (silu_gate * up_pre).astype(jnp.bfloat16)
    result = jnp.einsum(
        "spcf,pfd->spcd", hidden, down_w, preferred_element_type=jnp.float32
    ).astype(jnp.bfloat16)
    return (result, hidden, gate_pre, sigmoid_g, silu_gate, up_pre)


def backward_rows(d_out, gate_pre, sigmoid_g, silu_gate, up_pre, gate_w, up_w, down_w):
    dhidden = jnp.einsum("spcd,pfd->spcf", d_out, down_w, preferred_element_type=jnp.float32)
    d_gate = (dhidden * up_pre * sigmoid_g * (1.0 + gate_pre * (1.0 - sigmoid_g))).astype(
        jnp.bfloat16
    )
    d_up = (dhidden * silu_gate).astype(jnp.bfloat16)
    d_rows = jnp.einsum("spcf,pdf->spcd", d_gate, gate_w, preferred_element_type=jnp.float32)
    d_rows = d_rows + jnp.einsum("spcf,pdf->spcd", d_up, up_w, preferred_element_type=jnp.float32)
    return d_rows.astype(jnp.bfloat16)


def hidden_again(rows_in, own_gate, own_up):
    gate_pre = jnp.einsum("scd,df->scf", rows_in, own_gate, preferred_element_type=jnp.float32)
    up_pre = jnp.einsum("scd,df->scf", rows_in, own_up, preferred_element_type=jnp.float32)
    return (gate_pre * jax.nn.sigmoid(gate_pre) * up_pre).astype(jnp.bfloat16)


def on_device(
    tokens, cotangent, route_gates, expert_ids, replica, hot_experts, w_gate, w_up, w_down
):
    experts = lax.axis_size("expert")
    groups = lax.axis_size("dp")
    tok_rows = tokens.shape[0]
    width = tokens.shape[1]
    hidden_width = w_gate.shape[3]
    choose_count = expert_ids.shape[1]
    routes = tok_rows * choose_count
    slot_total = 2 * experts * CAP
    flat_ids = expert_ids.reshape(-1)
    flat_pick = replica.reshape(-1)
    inside = flat_ids < experts
    matches = (hot_experts[None, :] == flat_ids[:, None]).astype(jnp.int32)
    spare_dev = jnp.sum(matches * jnp.arange(experts, dtype=jnp.int32)[None, :], axis=1)
    target = jnp.where(flat_pick == 1, spare_dev, flat_ids)
    copies = jnp.where(inside, 2 * target + flat_pick, 2 * experts)
    onehot = (copies[:, None] == jnp.arange(2 * experts + 1, dtype=jnp.int32)[None, :]).astype(
        jnp.int32
    )
    rank_in = jnp.sum(jnp.cumsum(onehot, axis=0) * onehot, axis=1) - 1
    kept_mask = inside & (rank_in < CAP)
    position = jnp.where(kept_mask, copies * CAP + rank_in, slot_total)
    slot_route = (
        jnp.full((slot_total + 1,), routes, jnp.int32)
        .at[position]
        .set(jnp.arange(routes, dtype=jnp.int32))[:slot_total]
    )
    source = slot_route // choose_count
    padded_x = jnp.concatenate([tokens, jnp.zeros((1, width), tokens.dtype)], axis=0)
    padded_dy = jnp.concatenate([cotangent, jnp.zeros((1, width), cotangent.dtype)], axis=0)
    flat_gates = route_gates.reshape(-1)
    padded_gates = jnp.concatenate([flat_gates, jnp.zeros((1,), flat_gates.dtype)], axis=0)
    send_x = padded_x[source].reshape(experts, 2, CAP, width)
    send_dy = (padded_gates[slot_route][:, None] * padded_dy[source].astype(jnp.float32)).astype(
        jnp.bfloat16
    )
    send_dy = send_dy.reshape(experts, 2, CAP, width)
    host_match = (hot_experts[:, None] == jnp.arange(experts, dtype=jnp.int32)[None, :]).astype(
        jnp.int32
    )
    inverse = jnp.sum(host_match * jnp.arange(experts, dtype=jnp.int32)[:, None], axis=0)
    owner_x = send_x[inverse, 1]
    owner_dy = send_dy[inverse, 1]
    gate_w = w_gate[0]
    up_w = w_up[0]
    down_w = w_down[0]
    own_gate = w_gate[0, 0]
    own_up = w_up[0, 0]
    rows_in = lax.all_to_all(send_x, "expert", split_axis=0, concat_axis=0, tiled=True)
    d_out = lax.all_to_all(send_dy, "expert", split_axis=0, concat_axis=0, tiled=True)
    result, hidden, gate_pre, sigmoid_g, silu_gate, up_pre = forward_rows(
        rows_in, gate_w, up_w, down_w
    )
    d_rows = backward_rows(d_out, gate_pre, sigmoid_g, silu_gate, up_pre, gate_w, up_w, down_w)
    result, d_rows, hidden_own, d_own = (result, d_rows, hidden[:, 0], d_out[:, 0])
    rows_in = lax.all_to_all(owner_x, "expert", split_axis=0, concat_axis=0, tiled=True)
    d_rows_in = lax.all_to_all(owner_dy, "expert", split_axis=0, concat_axis=0, tiled=True)
    hidden_owner = hidden_again(rows_in, own_gate, own_up)
    result_home, d_rows_home = (
        lax.all_to_all(result, "expert", split_axis=0, concat_axis=0, tiled=True),
        lax.all_to_all(d_rows, "expert", split_axis=0, concat_axis=0, tiled=True),
    )
    hidden_cols = jnp.concatenate(
        [hidden_own.reshape(-1, hidden_width), hidden_owner.reshape(-1, hidden_width)], axis=0
    ).T
    d_stacked = jnp.concatenate([d_own.reshape(-1, width), d_rows_in.reshape(-1, width)], axis=0)
    summed_all = lax.psum_scatter(
        jnp.dot(hidden_cols, d_stacked, preferred_element_type=jnp.float32),
        "dp",
        scatter_dimension=0,
        tiled=True,
    )
    grad_share = (summed_all / groups)[None]
    flat_result = jnp.concatenate(
        [result_home.reshape(slot_total, width), jnp.zeros((1, width), jnp.bfloat16)], axis=0
    )
    flat_drows = jnp.concatenate(
        [d_rows_home.reshape(slot_total, width), jnp.zeros((1, width), jnp.bfloat16)], axis=0
    )
    route_out = flat_result[position].astype(jnp.float32)
    route_grad = flat_drows[position].astype(jnp.float32)
    layer_out = (flat_gates[:, None] * route_out).reshape(tok_rows, choose_count, width).sum(axis=1)
    grad_tokens = route_grad.reshape(tok_rows, choose_count, width).sum(axis=1)
    return (layer_out.astype(jnp.bfloat16), grad_tokens.astype(jnp.bfloat16), grad_share)


def solution(mesh):
    in_specs = (
        P(("expert", "dp"), None),
        P(("expert", "dp"), None),
        P(("expert", "dp"), None),
        P(("expert", "dp"), None),
        P(("expert", "dp"), None),
        P(),
        P("expert", None, None, None),
        P("expert", None, None, None),
        P("expert", None, None, None),
    )
    out_specs = (P(("expert", "dp"), None), P(("expert", "dp"), None), P("expert", "dp", None))
    return jax.shard_map(
        on_device, mesh=mesh, in_specs=in_specs, out_specs=out_specs, check_vma=False
    )
```

profile of v0, /device:TPU:0, one launch (start us, length us, event | category | flops | bytes accessed | tf_op | source)
XLA Modules:
  0.0 132.8 jit_solution(11378156529329034333)
XLA Ops:
  7.2 0.9 copy.47
  8.1 0.1 reshape.190
  8.6 0.8 copy.49
  9.4 0.1 reshape.196
  9.8 0.7 select_reduce_fusion.1
  10.5 0.7 select_reduce_fusion
  11.3 1.7 %reduce-window.6 = s32[9,6,128]{2,0,1:T(8,128)S(1)} reduce-window(s32[9,6,128]{2,0,1:T(8,128)S(1)} %fusion.62, s32[]{:T(128)} %constant.22.clone.1), window={size=1x1x128 pad=0_0x0_0x127_0}, to_apply=%region_1.2 | reduce-window | flops 877824 | bytes 55300 | tf_op jit(solution)/shard_map/reduce-window
  13.0 0.3 slice_reduce_fusion.1
  13.5 3.4 %scatter_custom_fusion = s32[97]{0:T(128)S(1)} fusion(s32[768]{0:T(1024)S(1)} %fusion.66, s32[768]{0:T(1024)S(1)} %iota.21, s32[]{:T(128)} %constant.19.clone.1), kind=kCustom, calls=%fused_computation.93 | custom fusion | bytes 392 | tf_op jit(solution)/shard_map/scatter | solution.py:65
  16.9 1.0 concatenate.25
  17.9 1.5 %gather_fusion = bf16[96,1024]{1,0:T(8,128)(2,1)} fusion(bf16[129,1024]{1,0:T(8,128)(2,1)S(1)} %concatenate.25, s32[1024]{0:T(1024)S(1)} %get-tuple-element.8), kind=kCustom, calls=%fused_computation | custom fusion | bytes 393600 | tf_op jit(solution)/shard_map/gather | solution.py:72
  19.4 1.0 reshape.197
  20.4 1.2 gather_fusion.5
  21.6 5.2 %all-to-all-start.4 = ((bf16[4,12,1024]{2,1,0:T(8,128)(2,1)}), bf16[4,12,1024]{2,1,0:T(8,128)(2,1)}, u32[]{:S(2)}, u32[]{:S(2)}) async-start(bf16[4,12,1024]{2,1,0:T(8,128)(2,1)} %gather_fusion.5), calls=%async_computation.4 | async-start | bytes 262144 | tf_op jit(solution)/shard_map/all_to_all | solution.py:95
  27.0 1.0 gather_fusion.2
  28.1 1.0 concatenate.28
  29.1 1.5 %gather_fusion.3 = bf16[96,1024]{1,0:T(8,128)(2,1)} fusion(bf16[129,1024]{1,0:T(8,128)(2,1)S(1)} %concatenate.28, s32[1024]{0:T(1024)S(1)} %get-tuple-element.8), kind=kCustom, calls=%fused_computation.3 | custom fusion | bytes 393600 | tf_op jit(solution)/shard_map/gather | solution.py:73
  30.5 1.8 %reshape.204 = f32[4,2,12,1024]{3,2,1,0:T(8,128)} reshape(bf16[96,1024]{1,0:T(8,128)(2,1)} %gather_fusion.3) | data formatting | bytes 589824 | tf_op jit(solution)/shard_map/convert_element_type | solution.py:73
  32.3 1.1 multiply_convert_fusion
  33.4 1.2 gather_fusion.6
  34.6 4.2 %all-to-all-start.5 = ((bf16[4,12,1024]{2,1,0:T(8,128)(2,1)}), bf16[4,12,1024]{2,1,0:T(8,128)(2,1)S(1)}, u32[]{:S(2)}, u32[]{:S(2)}) async-start(bf16[4,12,1024]{2,1,0:T(8,128)(2,1)} %gather_fusion.6), calls=%async_computation.5 | async-start | bytes 262144 | tf_op jit(solution)/shard_map/all_to_all | solution.py:96
  38.8 1.8 %copy.54 = bf16[4,2,12,1024]{3,1,2,0:T(2,128)(2,1)} copy(bf16[4,2,12,1024]{3,2,1,0:T(8,128)(2,1)} %copy-done.5) | data formatting | bytes 393216 | tf_op jit(solution)/shard_map/reshape | solution.py:72
  40.6 0.9 copy.60
  41.5 2.3 %all-to-all-done.5 = bf16[4,12,1024]{2,1,0:T(8,128)(2,1)S(1)} async-done(((bf16[4,12,1024]{2,1,0:T(8,128)(2,1)}), bf16[4,12,1024]{2,1,0:T(8,128)(2,1)S(1)}, u32[]{:S(2)}, u32[]{:S(2)}) %all-to-all-start.5) | async-done | bytes 98336 | tf_op jit(solution)/shard_map/all_to_all | solution.py:96
  43.8 3.4 %all-to-all-start.2 = ((bf16[4,2,12,1024]{3,1,2,0:T(2,128)(2,1)}), bf16[4,2,12,1024]{3,1,2,0:T(2,128)(2,1)S(1)}, u32[]{:S(2)}, u32[]{:S(2)}) async-start(bf16[4,2,12,1024]{3,1,2,0:T(2,128)(2,1)} %copy.60), calls=%async_computation.2 | async-start | bytes 393216 | tf_op jit(solution)/shard_map/all_to_all | solution.py:89
  47.2 2.6 %fusion.14 = f32[4,12,768]{2,1,0:T(8,128)} fusion(bf16[4,12,1024]{2,1,0:T(8,128)(2,1)} %all-to-all-done.4, bf16[1,2,1024,768]{3,2,1,0:T(8,128)(2,1)} %param.15), kind=kOutput, calls=%fused_computation.23 | convolution fusion | flops 75497472 | bytes 1851392 | tf_op jit(solution)/shard_map/scd,df->scf/dot_general | solution.py:33
  49.8 2.6 %all-to-all-done.2 = bf16[4,2,12,1024]{3,1,2,0:T(2,128)(2,1)S(1)} async-done(((bf16[4,2,12,1024]{3,1,2,0:T(2,128)(2,1)}), bf16[4,2,12,1024]{3,1,2,0:T(2,128)(2,1)S(1)}, u32[]{:S(2)}, u32[]{:S(2)}) %all-to-all-start.2) | async-done | bytes 196640 | tf_op jit(solution)/shard_map/all_to_all | solution.py:89
  52.4 4.0 %all-to-all-start = ((bf16[4,2,12,1024]{3,1,2,0:T(2,128)(2,1)}), bf16[4,2,12,1024]{3,1,2,0:T(2,128)(2,1)}, u32[]{:S(2)}, u32[]{:S(2)}) async-start(bf16[4,2,12,1024]{3,1,2,0:T(2,128)(2,1)} %copy.54), calls=%async_computation | async-start | bytes 393216 | tf_op jit(solution)/shard_map/all_to_all | solution.py:88
  56.4 2.5 %fusion.45 = bf16[4,12,768]{2,1,0:T(8,128)(2,1)} fusion(bf16[4,12,1024]{2,1,0:T(8,128)(2,1)} %all-to-all-done.4, bf16[1,2,1024,768]{3,2,1,0:T(8,128)(2,1)} %param.16, f32[4,12,768]{2,1,0:T(8,128)} %fusion.14), kind=kOutput, calls=%fused_computation.36 | convolution fusion | flops 75718656 | bytes 1974272 | tf_op jit(solution)/shard_map/scd,df->scf/dot_general | solution.py:34
  58.9 1.5 %reshape.201 = bf16[48,768]{1,0:T(8,128)(2,1)} reshape(bf16[4,12,768]{2,1,0:T(8,128)(2,1)} %fusion.45) | data formatting | bytes 147456 | tf_op jit(solution)/shard_map/reshape | solution.py:103
  60.5 0.7 reshape.202
  61.1 0.5 slice_reduce_fusion
  61.6 0.7 reshape_squeeze.7
  62.3 2.7 %fusion.30 = f32[4,2,12,768]{3,2,0,1:T(8,128)S(1)} fusion(bf16[1,2,1024,768]{3,2,1,0:T(8,128)(2,1)} %param.15, bf16[4,2,12,1024]{3,1,2,0:T(2,128)(2,1)} %all-to-all-done), kind=kOutput, calls=%fused_computation.31 | convolution fusion | flops 150994944 | bytes 3637248 | tf_op jit(solution)/shard_map/spcd,pdf->spcf/dot_general | solution.py:10
  65.1 0.2 copy-done.1
  65.2 2.3 %multiply_convert_fusion.3 = (bf16[4,2,12,768]{3,2,0,1:T(8,128)(2,1)S(1)}, f32[4,2,12,768]{3,2,0,1:T(8,128)}) fusion(f32[4,2,12,768]{3,2,0,1:T(8,128)S(1)} %fusion.30, bf16[1,2,1024,768]{3,2,1,0:T(8,128)(2,1)S(1)} %copy-done.1, bf16[4,2,12,1024]{3,1,2,0:T(2,128)(2,1)} %all-to-all-done), kind=kOutput, calls=%fused_computation.41 | convolution fusion | flops 151437312 | bytes 4079616 | tf_op jit(solution)/shard_map/spcd,pdf->spcf/dot_general | solution.py:11
  67.6 0.7 copy-done.7
  68.2 0.6 slice.43
  68.9 1.5 %reshape_squeeze.6 = bf16[48,768]{1,0:T(8,128)(2,1)} reshape(bf16[4,1,12,768]{3,2,0,1:T(8,128)(2,1)} %slice.43) | data formatting | bytes 147456 | tf_op jit(solution)/shard_map/reshape;squeeze | solution.py:103
  70.4 3.3 %fusion.52 = f32[768,1024]{1,0:T(8,128)} fusion(bf16[48,1024]{1,0:T(8,128)(2,1)} %reshape.202, bf16[48,1024]{1,0:T(8,128)(2,1)} %reshape_squeeze.7, bf16[48,768]{1,0:T(8,128)(2,1)} %reshape.201, bf16[48,768]{1,0:T(8,128)(2,1)} %reshape_squeeze.6), kind=kOutput, calls=%fused_computation.48 | convolution fusion | flops 151683072 | bytes 3489792 | tf_op jit(solution)/shard_map/dot_general | solution.py:107
  73.7 1.6 %fusion.36 = bf16[4,2,12,1024]{3,2,0,1:T(8,128)(2,1)S(1)} fusion(bf16[4,2,12,768]{3,2,0,1:T(8,128)(2,1)} %copy-done.7, bf16[1,2,768,1024]{3,2,1,0:T(8,128)(2,1)S(1)} %copy-done), kind=kOutput, calls=%fused_computation.33 | convolution fusion | flops 151093248 | bytes 3489792 | tf_op jit(solution)/shard_map/spcf,pfd->spcd/dot_general | solution.py:15
  75.3 0.9 copy.57
  76.2 4.1 %all-to-all-start.1 = ((bf16[4,2,12,1024]{3,1,2,0:T(2,128)(2,1)}), bf16[4,2,12,1024]{3,1,2,0:T(2,128)(2,1)}, u32[]{:S(2)}, u32[]{:S(2)}) async-start(bf16[4,2,12,1024]{3,1,2,0:T(2,128)(2,1)} %copy.57), calls=%async_computation.1 | async-start | bytes 393216 | tf_op jit(solution)/shard_map/all_to_all | solution.py:99
  80.3 2.2 %fusion.27 = f32[4,2,12,768]{3,2,0,1:T(8,128)S(1)} fusion(bf16[1,2,768,1024]{3,2,1,0:T(8,128)(2,1)S(1)} %copy-done, bf16[4,2,12,1024]{3,1,2,0:T(2,128)(2,1)} %copy-done.4), kind=kOutput, calls=%fused_computation.30 | convolution fusion | flops 150994944 | bytes 3637248 | tf_op jit(solution)/shard_map/spcd,pfd->spcf/dot_general | solution.py:22
  82.6 1.1 fusion
  83.6 0.8 copy-done.3
  84.5 1.1 fusion.39
  85.6 0.9 copy.62
  86.5 4.2 %all-to-all-start.3 = ((bf16[4,2,12,1024]{3,1,2,0:T(2,128)(2,1)}), bf16[4,2,12,1024]{3,1,2,0:T(2,128)(2,1)}, u32[]{:S(2)}, u32[]{:S(2)}) async-start(bf16[4,2,12,1024]{3,1,2,0:T(2,128)(2,1)} %copy.62), calls=%async_computation.3 | async-start | bytes 393216 | tf_op jit(solution)/shard_map/all_to_all | solution.py:100
  90.7 0.6 pad_clamp_fusion.1
  91.3 1.0 copy.58
  92.3 0.7 reshape.198
  93.0 0.9 concatenate.26
  93.9 2.1 %all-to-all-done.3 = bf16[4,2,12,1024]{3,1,2,0:T(2,128)(2,1)} async-done(((bf16[4,2,12,1024]{3,1,2,0:T(2,128)(2,1)}), bf16[4,2,12,1024]{3,1,2,0:T(2,128)(2,1)}, u32[]{:S(2)}, u32[]{:S(2)}) %all-to-all-start.3) | async-done | bytes 196640 | tf_op jit(solution)/shard_map/all_to_all | solution.py:100
  96.0 1.7 %copy.63 = bf16[4,2,12,1024]{3,2,1,0:T(8,128)(2,1)} copy(bf16[4,2,12,1024]{3,1,2,0:T(2,128)(2,1)} %all-to-all-done.3) | data formatting | bytes 393216 | tf_op jit(solution)/shard_map/all_to_all | solution.py:100
  97.7 1.0 reshape.200
  98.7 0.7 concatenate.29
  99.4 5.6 %gather_fusion.4 = bf16[768,1024]{1,0:T(8,128)(2,1)} fusion(bf16[97,1024]{1,0:T(8,128)(2,1)} %concatenate.29, s32[1024]{0:T(1024)} %pad_clamp_fusion.1), kind=kCustom, calls=%fused_computation.4 | custom fusion | bytes 3148800 | tf_op jit(solution)/shard_map/gather | solution.py:120
  105.0 3.7 %gather.28 = bf16[128,6,1024]{2,1,0:T(8,128)(2,1)} reshape(bf16[768,1024]{1,0:T(8,128)(2,1)} %gather_fusion.4) | data formatting | bytes 3145728 | tf_op jit(solution)/shard_map/gather | solution.py:120
  108.7 3.6 %reduce_sum.59 = bf16[128,1024]{1,0:T(8,128)(2,1)} reduce(bf16[128,6,1024]{2,1,0:T(8,128)(2,1)} %gather.28, bf16[]{:T(256)} %constant.18.clone.1), dimensions={1}, to_apply=%region_6.7 | reduce | flops 655360 | bytes 1835010 | tf_op jit(solution)/shard_map/reduce_sum | solution.py:122
  112.4 3.6 %gather_fusion.1 = bf16[768,1024]{1,0:T(8,128)(2,1)} fusion(bf16[97,1024]{1,0:T(8,128)(2,1)S(1)} %concatenate.26, s32[1024]{0:T(1024)S(1)} %copy-done.10), kind=kCustom, calls=%fused_computation.1 | custom fusion | bytes 3148800 | tf_op jit(solution)/shard_map/gather | solution.py:119
  115.9 3.9 %reshape.203 = f32[128,6,1024]{2,1,0:T(8,128)} reshape(bf16[768,1024]{1,0:T(8,128)(2,1)} %gather_fusion.1) | data formatting | bytes 4718592 | tf_op jit(solution)/shard_map/convert_element_type | solution.py:119
  119.9 4.3 %multiply_reduce_fusion = bf16[128,1024]{1,0:T(8,128)(2,1)} fusion(f32[128,6,1024]{2,1,0:T(8,128)} %reshape.203, f32[128,6]{1,0:T(8,128)S(1)} %copy-done.9), kind=kLoop, calls=%fused_computation.8 | loop fusion | flops 1441792 | bytes 3410944 | tf_op jit(solution)/shard_map/reduce_sum | solution.py:121
  124.2 1.8 %multiply_bitcast_fusion = f32[1,96,1024]{2,1,0:T(8,128)} fusion(f32[96,1024]{1,0:T(8,128)} %reduce-scatter.2.cloned.1.call-done), kind=kLoop, calls=%fused_computation.38 | loop fusion | flops 98304 | bytes 786432 | tf_op jit(solution)/shard_map/broadcast_in_dim | solution.py:112
  (50 shorter events, 1.4 us)
Async XLA Ops:
  7.2 66.6 %copy-start = (bf16[1,2,768,1024]{3,2,1,0:T(8,128)(2,1)S(1)}, bf16[1,2,768,1024]{3,2,1,0:T(8,128)(2,1)}, u32[]{:S(2)}) copy-start(bf16[1,2,768,1024]{3,2,1,0:T(8,128)(2,1)} %param.17) | copy-start | bytes 9437188
  7.2 19.5 %copy-start.11 = (f32[128,6]{0,1:T(8,128)S(1)}, f32[128,6]{0,1:T(8,128)}, u32[]{:S(2)}) copy-start(f32[128,6]{0,1:T(8,128)} %param.11) | copy-start | bytes 9220
  20.4 6.5 %copy-start.5 = (bf16[4,2,12,1024]{3,2,1,0:T(8,128)(2,1)}, bf16[4,2,12,1024]{3,2,1,0:T(8,128)(2,1)S(1)}, u32[]{:S(2)}) copy-start(bf16[4,2,12,1024]{3,2,1,0:T(8,128)(2,1)S(1)} %reshape.197) | copy-start | bytes 589828
  21.6 13.1 %all-to-all-start.4 = ((bf16[4,12,1024]{2,1,0:T(8,128)(2,1)}), bf16[4,12,1024]{2,1,0:T(8,128)(2,1)}, u32[]{:S(2)}, u32[]{:S(2)}) async-start(bf16[4,12,1024]{2,1,0:T(8,128)(2,1)} %gather_fusion.5), calls=%async_computation.4 | async-start | bytes 262144 | tf_op jit(solution)/shard_map/all_to_all | solution.py:95
  26.8 1.1 copy-start.8
  34.6 9.2 %all-to-all-start.5 = ((bf16[4,12,1024]{2,1,0:T(8,128)(2,1)}), bf16[4,12,1024]{2,1,0:T(8,128)(2,1)S(1)}, u32[]{:S(2)}, u32[]{:S(2)}) async-start(bf16[4,12,1024]{2,1,0:T(8,128)(2,1)} %gather_fusion.6), calls=%async_computation.5 | async-start | bytes 262144 | tf_op jit(solution)/shard_map/all_to_all | solution.py:96
  43.8 8.5 %all-to-all-start.2 = ((bf16[4,2,12,1024]{3,1,2,0:T(2,128)(2,1)}), bf16[4,2,12,1024]{3,1,2,0:T(2,128)(2,1)S(1)}, u32[]{:S(2)}, u32[]{:S(2)}) async-start(bf16[4,2,12,1024]{3,1,2,0:T(2,128)(2,1)} %copy.60), calls=%async_computation.2 | async-start | bytes 393216 | tf_op jit(solution)/shard_map/all_to_all | solution.py:89
  52.4 9.9 %copy-start.4 = (bf16[4,2,12,1024]{3,1,2,0:T(2,128)(2,1)}, bf16[4,2,12,1024]{3,1,2,0:T(2,128)(2,1)S(1)}, u32[]{:S(2)}) copy-start(bf16[4,2,12,1024]{3,1,2,0:T(2,128)(2,1)S(1)} %all-to-all-done.2) | copy-start | bytes 589828
  52.4 9.9 %all-to-all-start = ((bf16[4,2,12,1024]{3,1,2,0:T(2,128)(2,1)}), bf16[4,2,12,1024]{3,1,2,0:T(2,128)(2,1)}, u32[]{:S(2)}, u32[]{:S(2)}) async-start(bf16[4,2,12,1024]{3,1,2,0:T(2,128)(2,1)} %copy.54), calls=%async_computation | async-start | bytes 393216 | tf_op jit(solution)/shard_map/all_to_all | solution.py:88
  56.4 67.8 %reduce-scatter.2.cloned.1.call-start = ((), (), s32[]{:S(2)}) async-start(), calls=%async_computation.7 | async-start | bytes 3538944 | tf_op jit(solution)/shard_map/reduce_scatter | solution.py:106
  62.3 2.9 %copy-start.1 = (bf16[1,2,1024,768]{3,2,1,0:T(8,128)(2,1)S(1)}, bf16[1,2,1024,768]{3,2,1,0:T(8,128)(2,1)}, u32[]{:S(2)}) copy-start(bf16[1,2,1024,768]{3,2,1,0:T(8,128)(2,1)} %param.16) | copy-start | bytes 9437188
  67.6 0.7 copy-start.7
  76.2 10.3 %all-to-all-start.1 = ((bf16[4,2,12,1024]{3,1,2,0:T(2,128)(2,1)}), bf16[4,2,12,1024]{3,1,2,0:T(2,128)(2,1)}, u32[]{:S(2)}, u32[]{:S(2)}) async-start(bf16[4,2,12,1024]{3,1,2,0:T(2,128)(2,1)} %copy.57), calls=%async_computation.1 | async-start | bytes 393216 | tf_op jit(solution)/shard_map/all_to_all | solution.py:99
  80.3 2.3 %copy-start.2 = (bf16[1,2,1024,768]{3,2,1,0:T(8,128)(2,1)S(1)}, bf16[1,2,1024,768]{3,2,1,0:T(8,128)(2,1)}, u32[]{:S(2)}) copy-start(bf16[1,2,1024,768]{3,2,1,0:T(8,128)(2,1)} %param.16) | copy-start | bytes 9437188
  82.6 1.9 %copy-start.3 = (bf16[1,2,1024,768]{3,2,1,0:T(8,128)(2,1)S(1)}, bf16[1,2,1024,768]{3,2,1,0:T(8,128)(2,1)}, u32[]{:S(2)}) copy-start(bf16[1,2,1024,768]{3,2,1,0:T(8,128)(2,1)} %param.15) | copy-start | bytes 9437188
  82.6 1.9 %copy-start.6 = (f32[4,2,12,768]{3,2,0,1:T(8,128)S(1)}, f32[4,2,12,768]{3,2,0,1:T(8,128)}, u32[]{:S(2)}) copy-start(f32[4,2,12,768]{3,2,0,1:T(8,128)} %get-tuple-element.6) | copy-start | bytes 884740
  86.5 9.5 %all-to-all-start.3 = ((bf16[4,2,12,1024]{3,1,2,0:T(2,128)(2,1)}), bf16[4,2,12,1024]{3,1,2,0:T(2,128)(2,1)}, u32[]{:S(2)}, u32[]{:S(2)}) async-start(bf16[4,2,12,1024]{3,1,2,0:T(2,128)(2,1)} %copy.62), calls=%async_computation.3 | async-start | bytes 393216 | tf_op jit(solution)/shard_map/all_to_all | solution.py:100
  105.0 7.4 %copy-start.10 = (s32[1024]{0:T(1024)S(1)}, s32[1024]{0:T(1024)}, u32[]{:S(2)}) copy-start(s32[1024]{0:T(1024)} %pad_clamp_fusion.1) | copy-start | bytes 12292
  115.9 3.9 %copy-start.9 = (f32[128,6]{1,0:T(8,128)S(1)}, f32[128,6]{1,0:T(8,128)}, u32[]{:S(2)}) copy-start(f32[128,6]{1,0:T(8,128)} %copy-done.8) | copy-start | bytes 9220
Sparse Core Ops, SparseCore 0:
  73.8 42.1 reduce-scatter.1
where the time goes:
time: 134 us; the launch traced here: 133 us
  local copies, waits for them, and re-layouts  52.3 us (39%)
  starting transfers between devices  25.1 us (19%)
  matrix products  19.3 us (14%)
  other arithmetic  14.8 us (11%)
  between operations  14.3 us (11%)
  waiting for transfers between devices  7 us (5%)
    gather x2, local copies, waits for them, and re-layouts, on_device(): route_grad = flat_drows[position].astype(jnp.float32)  9.37 us
    all_to_all x1, starting transfers between devices, on_device(): lax.all_to_all(owner_x, 'expert', split_axis=0, concat_axis=0, tiled=True)  5.16 us
    reduce_sum x1, other arithmetic, on_device(): (flat_gates[:, None] * route_out).reshape(tok_rows, choose_count, width)  4.3 us
    all_to_all x1, starting transfers between devices, on_device(): lax.all_to_all(d_rows, 'expert', split_axis=0, concat_axis=0, tiled=True)  4.2 us
    all_to_all x1, starting transfers between devices, on_device(): lax.all_to_all(owner_dy, 'expert', split_axis=0, concat_axis=0, tiled=True)  4.19 us
    all_to_all x1, starting transfers between devices, on_device(): lax.all_to_all(result, 'expert', split_axis=0, concat_axis=0, tiled=True)  4.1 us
    all_to_all x1, starting transfers between devices, on_device(): lax.all_to_all(send_x, 'expert', split_axis=0, concat_axis=0, tiled=True)  4 us
    convert_element_type x1, local copies, waits for them, and re-layouts, on_device(): route_out = flat_result[position].astype(jnp.float32)  3.92 us
  transfers between devices with their start and end apart: 7, of which 3 were waited for; matrix products, arithmetic and copies ran while one was open for 44% of the time, Pallas kernels for 0%

commit v1 on v0

v1 whole, which is shorter than its diff:
```python
import functools

import jax
import jax.numpy as jnp
from jax import lax
from jax.experimental import pallas as pl
from jax.experimental.pallas import tpu as pltpu
from jax.sharding import PartitionSpec as P

CAP = 12
PAIR = 2 * CAP
VMEM_LIMIT = 48 * 1024 * 1024
BF16 = jnp.bfloat16
F32 = jnp.float32


def dot(a, b, contract=((1,), (0,))):
    return lax.dot_general(a, b, (contract, ((), ())), preferred_element_type=F32)


def partner(index, step, count):
    if count & (count - 1) == 0:
        return index ^ step
    return (index + step) % count


def source(index, step, count):
    if count & (count - 1) == 0:
        return index ^ step
    return (index - step) % count


def call(kernel, out_shape, flops, moved, **kw):
    return pl.pallas_call(
        kernel,
        out_shape=out_shape,
        compiler_params=pltpu.CompilerParams(vmem_limit_bytes=VMEM_LIMIT),
        cost_estimate=pl.CostEstimate(flops=flops, bytes_accessed=moved, transcendentals=0),
        **kw,
    )


def route_kernel(experts, choices, ids_ref, pick_ref, gates_ref, x_ref, dy_ref, *outs):
    sends, (sel_ref, gsel_ref) = outs[:experts], outs[experts:]
    tok_rows, width = x_ref.shape
    lanes = sel_ref.shape[1]
    me = lax.axis_index("expert")
    lane = lax.broadcasted_iota(jnp.int32, (1, lanes), 1)
    expert_at = jnp.full((1, lanes), -1, jnp.int32)
    slot_at = lane
    for step in range(experts):
        inside = (lane >= step * PAIR) & (lane < (step + 1) * PAIR)
        expert_at = jnp.where(inside, partner(me, step, experts), expert_at)
        slot_at = jnp.where(inside, lane - step * PAIR, slot_at)
    copy_at = jnp.where(slot_at >= CAP, 1, 0)
    rank_at = (slot_at - CAP * copy_at).astype(F32)
    key_at = jnp.where(expert_at < 0, -1, 2 * expert_at + copy_at)
    keys = 2 * ids_ref[...] + pick_ref[...]
    gates = gates_ref[...]
    member = jnp.zeros((tok_rows, lanes), F32)
    weight = jnp.zeros((tok_rows, lanes), F32)
    for k in range(choices):
        hit = keys[:, k : k + 1] == key_at
        member = jnp.where(hit, 1.0, member)
        weight = jnp.where(hit, gates[:, k : k + 1], weight)
    row = lax.broadcasted_iota(jnp.int32, (tok_rows, tok_rows), 0)
    col = lax.broadcasted_iota(jnp.int32, (tok_rows, tok_rows), 1)
    earlier = jnp.where(col < row, 1.0, 0.0).astype(BF16)
    rank = dot(earlier, member.astype(BF16))
    kept = (member > 0.0) & (rank == rank_at)
    select = jnp.where(kept, 1.0, 0.0)
    gated = jnp.where(kept, weight, 0.0)
    sel_ref[...] = select.astype(BF16)
    gsel_ref[...] = gated
    pick = select.T.astype(BF16)
    gate_of = jnp.sum(gated.T, axis=1, keepdims=True)
    rows = dot(pick, x_ref[...]).astype(BF16)
    grads = (gate_of * dot(pick, dy_ref[...])).astype(BF16)
    for step in range(experts):
        at = slice(step * PAIR, (step + 1) * PAIR)
        sends[step][:, :width] = rows[at]
        sends[step][:, width:] = grads[at]


def expert_kernel(experts, *refs):
    blocks, (d_ref, gate_ref, up_ref, down_ref) = refs[:experts], refs[experts : experts + 4]
    outs = refs[experts + 4 : 2 * experts + 4]
    ht_ref, x_s, res_s, grad_s = refs[2 * experts + 4 :]
    at, last = pl.program_id(0), pl.num_programs(0) - 1
    width = x_s.shape[1]

    @pl.when(at == 0)
    def _():
        x_s[...] = jnp.concatenate(
            [b[:, :width].astype(F32) for b in blocks], axis=0
        ).astype(BF16)
        res_s[...] = jnp.zeros_like(res_s)
        grad_s[...] = jnp.zeros_like(grad_s)

    x, d_out = x_s[...], d_ref[...]
    gate_w, up_w, down_w = gate_ref[0, 0], up_ref[0, 0], down_ref[0, 0]
    gate_pre = dot(x, gate_w)
    up_pre = dot(x, up_w)
    sig = jax.nn.sigmoid(gate_pre)
    silu = gate_pre * sig
    hidden = silu * up_pre
    ht_ref[...] = hidden.T.astype(BF16)
    res_s[...] += dot(hidden.astype(BF16), down_w)
    dhidden = dot(d_out, down_w, ((1,), (1,)))
    d_gate = (dhidden * up_pre * sig * (1.0 + gate_pre * (1.0 - sig))).astype(BF16)
    d_up = (dhidden * silu).astype(BF16)
    grad_s[...] += dot(d_gate, gate_w, ((1,), (1,))) + dot(d_up, up_w, ((1,), (1,)))

    @pl.when(at == last)
    def _():
        for step in range(experts):
            rows = pl.ds(step * PAIR, PAIR)
            outs[step][:, :width] = res_s[rows, :].astype(BF16)
            outs[step][:, width:] = grad_s[rows, :].astype(BF16)


def combine_kernel(experts, sel_ref, gsel_ref, *refs):
    blocks, (out_ref, grad_ref) = refs[:experts], refs[experts:]
    width = out_ref.shape[1]
    rows = experts * PAIR
    back = jnp.concatenate([b[...].astype(F32) for b in blocks], axis=0).astype(BF16)
    result, d_rows = back[:, :width], back[:, width:]
    weight = gsel_ref[:, :rows]
    high = weight.astype(BF16)
    rest = weight - high.astype(F32)
    mid = rest.astype(BF16)
    low = (rest - mid.astype(F32)).astype(BF16)
    out_ref[...] = (dot(high, result) + (dot(mid, result) + dot(low, result))).astype(BF16)
    grad_ref[...] = dot(sel_ref[:, :rows], d_rows).astype(BF16)


def outer_kernel(count, scale, *refs):
    hts, ds, (keep_ref, give_ref) = refs[:count], refs[count : 2 * count], refs[2 * count :]
    share = keep_ref.shape[0]
    core = lax.axis_index("dp") % 2
    for out, half in ((keep_ref, core), (give_ref, 1 - core)):
        rows = pl.ds(pl.multiple_of(half * share, 16), share)
        total = dot(hts[0][rows, :], ds[0][...])
        for ht, d in zip(hts[1:], ds[1:]):
            total += dot(ht[rows, :], d[...])
        out[...] = total * scale


def swap(value, axis, count, step):
    return lax.ppermute(value, axis, [(i, partner(i, step, count)) for i in range(count)])


def swap_chip(value, chips, step):
    pairs = [(2 * z + c, 2 * partner(z, step, chips) + c) for z in range(chips) for c in range(2)]
    return lax.ppermute(value, "dp", pairs)


def swap_core(value, groups):
    return lax.ppermute(value, "dp", [(i, i ^ 1) for i in range(groups)])


def slice_kernel(chips, ht_ref, *outs):
    z = lax.axis_index("dp") // 2
    share = outs[0].shape[0]
    for step in range(chips):
        start = pl.multiple_of(partner(z, step, chips) * share, 16)
        outs[step][...] = ht_ref[pl.ds(start, share), :]


def grad_by_rows(ht, d_out, groups):
    chips = groups // 2
    hidden_width, rows = ht.shape
    width = d_out.shape[1]
    share = hidden_width // groups
    ds = [d_out] + [swap_chip(d_out, chips, step) for step in range(1, chips)]
    shape = jax.ShapeDtypeStruct((2 * share, rows), BF16)
    hts = call(
        functools.partial(slice_kernel, chips), [shape] * chips, 0, 4 * hidden_width * rows
    )(ht)
    hts = [hts[0]] + [swap_chip(hts[step], chips, step) for step in range(1, chips)]
    shape = jax.ShapeDtypeStruct((share, width), F32)
    keep, give = call(
        functools.partial(outer_kernel, chips, 1.0 / groups),
        [shape] * 2,
        4 * chips * rows * share * width,
        8 * share * width + 2 * chips * rows * (width + 2 * share),
    )(*hts, *ds)
    return keep + swap_core(give, groups)


def grad_by_sums(ht, d_out, groups):
    total = lax.psum_scatter(dot(ht, d_out), "dp", scatter_dimension=0, tiled=True)
    return total / groups


def on_device(
    tokens, cotangent, route_gates, expert_ids, replica, hot_experts, w_gate, w_up, w_down
):
    del hot_experts
    experts = lax.axis_size("expert")
    groups = lax.axis_size("dp")
    tok_rows, width = tokens.shape
    hidden_width = w_gate.shape[3]
    choices = expert_ids.shape[1]
    rows = experts * PAIR
    lanes = -(-rows // 128) * 128
    block = jax.ShapeDtypeStruct((PAIR, 2 * width), BF16)

    *sends, sel, gsel = call(
        functools.partial(route_kernel, experts, choices),
        [block] * experts
        + [
            jax.ShapeDtypeStruct((tok_rows, lanes), BF16),
            jax.ShapeDtypeStruct((tok_rows, lanes), F32),
        ],
        4 * lanes * tok_rows * width,
        4 * (tok_rows + rows) * width,
    )(expert_ids, replica, route_gates, tokens, cotangent)

    came = [sends[0]] + [swap(sends[s], "expert", experts, s) for s in range(1, experts)]
    d_out = jnp.concatenate([b[:, width:] for b in came], axis=0)

    chunk = 256 if hidden_width % 256 == 0 else hidden_width
    whole = lambda shape: pl.BlockSpec(shape, lambda f: (0,) * len(shape))
    wide = pl.BlockSpec((1, 1, width, chunk), lambda f: (0, 0, 0, f))
    *results, ht = call(
        functools.partial(expert_kernel, experts),
        [block] * experts + [jax.ShapeDtypeStruct((hidden_width, rows), BF16)],
        12 * rows * width * hidden_width,
        6 * width * hidden_width + 12 * rows * width,
        grid=(hidden_width // chunk,),
        in_specs=[whole((PAIR, 2 * width))] * experts
        + [
            whole((rows, width)),
            wide,
            wide,
            pl.BlockSpec((1, 1, chunk, width), lambda f: (0, 0, f, 0)),
        ],
        out_specs=[whole((PAIR, 2 * width))] * experts
        + [pl.BlockSpec((chunk, rows), lambda f: (f, 0))],
        scratch_shapes=[
            pltpu.VMEM((rows, width), BF16),
            pltpu.VMEM((rows, width), F32),
            pltpu.VMEM((rows, width), F32),
        ],
    )(*came, d_out, w_gate, w_up, w_down)

    pairs = experts & (experts - 1) == 0
    home = [results[0]] + [
        swap(results[s], "expert", experts, s if pairs else experts - s) for s in range(1, experts)
    ]
    layer_out, grad_tokens = call(
        functools.partial(combine_kernel, experts),
        [jax.ShapeDtypeStruct((tok_rows, width), BF16)] * 2,
        8 * rows * tok_rows * width,
        4 * (tok_rows + rows) * width,
    )(sel, gsel, *home)

    share = hidden_width // groups
    short = groups in (2, 4, 8, 16) and share % 16 == 0
    grad = (grad_by_rows if short else grad_by_sums)(ht, d_out, groups)
    return layer_out, grad_tokens, grad[None]


def solution(mesh):
    in_specs = (
        P(("expert", "dp"), None),
        P(("expert", "dp"), None),
        P(("expert", "dp"), None),
        P(("expert", "dp"), None),
        P(("expert", "dp"), None),
        P(),
        P("expert", None, None, None),
        P("expert", None, None, None),
        P("expert", None, None, None),
    )
    out_specs = (P(("expert", "dp"), None), P(("expert", "dp"), None), P("expert", "dp", None))
    return jax.shard_map(
        on_device, mesh=mesh, in_specs=in_specs, out_specs=out_specs, check_vma=False
    )
```

time: 134 us -> 50 us (0.37)
  local copies, waits for them, and re-layouts: 52.3 us -> 6.18 us
  matrix products: 19.3 us -> 0 us
  other arithmetic: 14.8 us -> 0.81 us
  between operations: 14.3 us -> 0.7 us
  waiting for transfers between devices: 7 us -> 14.9 us
  Pallas kernels: 0 us -> 7.72 us
  starting transfers between devices: 25.1 us -> 19.4 us
    all_to_all x6 -> x0, starting transfers between devices: 25 us -> none  [the longest x1 5.16 us: on_device(): lax.all_to_all(owner_x, 'expert', split_axis=0, concat_axis=0, tiled=True)]
    ppermute x0 -> x13, starting transfers between devices: none -> 19.4 us  [the longest x6 11.2 us: swap_chip(): return lax.ppermute(value, 'dp', pairs)]
    gather x8 -> x0, local copies, waits for them, and re-layouts: 19.3 us -> none  [the longest x2 9.37 us: on_device(): route_grad = flat_drows[position].astype(jnp.float32)]
    dot_general x9 -> x0, matrix products: 19.3 us -> none  [the longest x1 3.28 us: on_device(): jnp.dot(hidden_cols, d_stacked, preferred_element_type=jnp.float32)]
    ppermute x0 -> x13, waiting for transfers between devices: none -> 14.9 us  [the longest x6 10.5 us: swap(): lax.ppermute(value, axis, [(i, partner(i, step, count)) for i in range(co...]
    reduce_sum x5 -> x0, other arithmetic: 9.41 us -> none  [the longest x1 4.3 us: on_device(): (flat_gates[:, None] * route_out).reshape(tok_rows, choose_count, width)]
    convert_element_type x5 -> x0, local copies, waits for them, and re-layouts: 8.31 us -> none  [the longest x1 3.92 us: on_device(): route_out = flat_result[position].astype(jnp.float32)]
    pallas_call x0 -> x5, Pallas kernels: none -> 7.72 us  [the longest x1 5.26 us: on_device(): call(functools.partial(expert_kernel, experts), [block] * experts + [jax....]
  transfers between devices with their start and end apart: 7 -> 13, of which waited for: 3 -> 8; matrix products, arithmetic and copies ran while one was open for 44% -> 0% of each run, Pallas kernels for 0% -> 13%
where the time goes in v1:
time: 50 us; the launch traced here: 49.7 us
  starting transfers between devices  19.4 us (39%)
  waiting for transfers between devices  14.9 us (30%)
  Pallas kernels  7.72 us (15%)
  local copies, waits for them, and re-layouts  6.18 us (12%)
  other arithmetic  0.81 us (2%)
  between operations  0.7 us (1%)
    ppermute x6, starting transfers between devices, swap_chip(): return lax.ppermute(value, 'dp', pairs)  11.2 us
    ppermute x6, waiting for transfers between devices, swap(): lax.ppermute(value, axis, [(i, partner(i, step, count)) for i in range(co...  10.5 us
    ppermute x6, starting transfers between devices, swap(): lax.ppermute(value, axis, [(i, partner(i, step, count)) for i in range(co...  8.1 us
    unnamed x9, local copies, waits for them, and re-layouts  6.16 us
    pallas_call x1, Pallas kernels, on_device(): call(functools.partial(expert_kernel, experts), [block] * experts + [jax....  5.26 us
    ppermute x6, waiting for transfers between devices, swap_chip(): return lax.ppermute(value, 'dp', pairs)  4.4 us
    pallas_call x1, Pallas kernels, on_device(): call(functools.partial(combine_kernel, experts), [jax.ShapeDtypeStruct((t...  1.14 us
  transfers between devices with their start and end apart: 13, of which 8 were waited for; matrix products, arithmetic and copies ran while one was open for 0% of the time, Pallas kernels for 13%

profile of v1, /device:TPU:0, one launch (start us, length us, event | category | flops | bytes accessed | tf_op | source)
XLA Modules:
  0.0 49.7 jit_solution(5265440318792985799)
XLA Ops:
  0.6 0.8 %copy.11.ids_ref = s32[128,6]{1,0:T(8,128)S(1)} copy(s32[128,6]{0,1:T(8,128)} %param.12) | data formatting | bytes 6144 | tf_op args[3]
  1.4 0.8 %copy.12.pick_ref = s32[128,6]{1,0:T(8,128)S(1)} copy(s32[128,6]{0,1:T(8,128)} %param.13) | data formatting | bytes 6144 | tf_op args[4]
  2.2 0.8 %copy.13.gates_ref = f32[128,6]{1,0:T(8,128)S(1)} copy(f32[128,6]{0,1:T(8,128)} %param.11) | data formatting | bytes 6144 | tf_op args[2]
  3.0 0.0 copy-start.1
  3.0 0.9 %copy-done.1 = bf16[128,1024]{1,0:T(8,128)(2,1)S(1)} copy-done((bf16[128,1024]{1,0:T(8,128)(2,1)S(1)}, bf16[128,1024]{1,0:T(8,128)(2,1)}, u32[]{:S(2)}) %copy-start.1) | copy-done | bytes 262168
  4.0 0.0 copy-start.2
  4.0 0.9 %copy-done.2 = bf16[128,1024]{1,0:T(8,128)(2,1)S(1)} copy-done((bf16[128,1024]{1,0:T(8,128)(2,1)S(1)}, bf16[128,1024]{1,0:T(8,128)(2,1)}, u32[]{:S(2)}) %copy-start.2) | copy-done | bytes 262168
  4.9 0.7 %shard_map.103 = (bf16[24,2048]{1,0:T(8,128)(2,1)S(1)}, bf16[24,2048]{1,0:T(8,128)(2,1)S(1)}, bf16[24,2048]{1,0:T(8,128)(2,1)S(1)}, bf16[24,2048]{1,0:T(8,128)(2...) custom-call(s32[128,6]{1,0:T(8,128)S(1)} %copy.11.ids_ref, s32[128,6]{1,0:T(8,128)S(1)} %copy.12.pick_ref, ...), custom_call_target="tpu_custom_call" | custom-call | flops 67108864 | bytes 917504 | tf_op jit(solution)/shard_map/pallas_call | solution.py:209
  5.6 3.0 %collective-permute-start = (bf16[24,2048]{1,0:T(8,128)(2,1)S(1)}, bf16[24,2048]{1,0:T(8,128)(2,1)S(1)}, u32[]{:S(2)}, u32[]{:S(2)}) collective-permute-start(bf16[24,2048]{1,0:T(8,128)(2,1)S(1)} %get-tuple-element.25), channel_id=1, source_target_pairs={{0,8},{8,0},{16,24},{24,16},{1,9},{9,1},{17,25},{25,17},{2,10},{10... | collective-permute-start | bytes 294920 | tf_op jit(solution)/shard_map/ppermute | solution.py:150
  8.6 1.5 %collective-permute-start.1 = (bf16[24,2048]{1,0:T(8,128)(2,1)S(1)}, bf16[24,2048]{1,0:T(8,128)(2,1)S(1)}, u32[]{:S(2)}, u32[]{:S(2)}) collective-permute-start(bf16[24,2048]{1,0:T(8,128)(2,1)S(1)} %get-tuple-element.26), channel_id=1, source_target_pairs={{0,16},{8,24},{16,0},{24,8},{1,17},{9,25},{17,1},{25,9},{2,18},{10... | collective-permute-start | bytes 294920 | tf_op jit(solution)/shard_map/ppermute | solution.py:150
  10.1 0.0 collective-permute-start.2
  10.2 1.5 %collective-permute-done.refs_1_ = bf16[24,2048]{1,0:T(8,128)(2,1)S(1)} collective-permute-done((bf16[24,2048]{1,0:T(8,128)(2,1)S(1)}, bf16[24,2048]{1,0:T(8,128)(2,1)S(1)}, u32[]{:S(2)}, u32[]{:S(2)}) %collective-permute-start) | collective-permute-done | bytes 98336 | tf_op jit(solution)/shard_map/ppermute | solution.py:150
  11.7 2.6 %collective-permute-done.1.refs_2_ = bf16[24,2048]{1,0:T(8,128)(2,1)S(1)} collective-permute-done((bf16[24,2048]{1,0:T(8,128)(2,1)S(1)}, bf16[24,2048]{1,0:T(8,128)(2,1)S(1)}, u32[]{:S(2)}, u32[]{:S(2)}) %collective-permute-start.1) | collective-permute-done | bytes 98336 | tf_op jit(solution)/shard_map/ppermute | solution.py:150
  14.3 1.4 %collective-permute-done.2.refs_3_ = bf16[24,2048]{1,0:T(8,128)(2,1)S(1)} collective-permute-done((bf16[24,2048]{1,0:T(8,128)(2,1)S(1)}, bf16[24,2048]{1,0:T(8,128)(2,1)S(1)}, u32[]{:S(2)}, u32[]{:S(2)}) %collective-permute-start.2) | collective-permute-done | bytes 98336 | tf_op jit(solution)/shard_map/ppermute | solution.py:150
  15.7 2.7 %collective-permute-start.10 = (bf16[96,1024]{1,0:T(8,128)(2,1)S(1)}, bf16[96,1024]{1,0:T(8,128)(2,1)S(1)}, u32[]{:S(2)}, u32[]{:S(2)}) collective-permute-start(bf16[96,1024]{1,0:T(8,128)(2,1)S(1)} %pad_maximum_fusion.refs_4_), channel_id=1, source_target_pairs={{0,4},{1,5},{2,6},{3,7},{4,0},{5,1},{6,2},{7,3},{8,12},{9,13},{10,... | collective-permute-start | bytes 589832 | tf_op jit(solution)/shard_map/ppermute | solution.py:155
  18.3 1.4 %collective-permute-start.11 = (bf16[96,1024]{1,0:T(8,128)(2,1)S(1)}, bf16[96,1024]{1,0:T(8,128)(2,1)S(1)}, u32[]{:S(2)}, u32[]{:S(2)}) collective-permute-start(bf16[96,1024]{1,0:T(8,128)(2,1)S(1)} %pad_maximum_fusion.refs_4_), channel_id=1, source_target_pairs={{0,6},{1,7},{2,4},{3,5},{4,2},{5,3},{6,0},{7,1},{8,14},{9,15},{10,... | collective-permute-start | bytes 589832 | tf_op jit(solution)/shard_map/ppermute | solution.py:155
  19.7 0.2 collective-permute-start.9
  19.9 0.0 copy-start
  19.9 1.9 %copy-done = bf16[1,2,1024,768]{3,2,1,0:T(8,128)(2,1)S(1)} copy-done((bf16[1,2,1024,768]{3,2,1,0:T(8,128)(2,1)S(1)}, bf16[1,2,1024,768]{3,2,1,0:T(8,128)(2,1)}, u32[]{:S(2)}) %copy-start) | copy-done | bytes 3145752
  21.8 5.3 %shard_map.104 = (bf16[24,2048]{1,0:T(8,128)(2,1)S(1)}, bf16[24,2048]{1,0:T(8,128)(2,1)S(1)}, bf16[24,2048]{1,0:T(8,128)(2,1)S(1)}, bf16[24,2048]{1,0:T(8,128)(2,1)S(1)}, bf16[768,96]{1,0:T(8,128)(2,1)S(1)}) custom-call(bf16[24,2048]{1,0:T(8,128)(2,1)S(1)} %get-tuple-element.24.refs_0_, bf16[24,2048]{1,0:T(8,128)(2,1)S(1)} %collective-permute-done.refs_1_, ...), custom_call_target="tpu_custom_call" | custom-call | flops 905969664 | bytes 5898240 | tf_op jit(solution)/shard_map/pallas_call | solution.py:226
  27.1 0.1 shard_map.106
  27.1 1.9 %collective-permute-start.6 = (bf16[192,96]{1,0:T(8,128)(2,1)S(1)}, bf16[192,96]{1,0:T(8,128)(2,1)S(1)}, u32[]{:S(2)}, u32[]{:S(2)}) collective-permute-start(bf16[192,96]{1,0:T(8,128)(2,1)S(1)} %get-tuple-element.36), channel_id=1, source_target_pairs={{0,2},{1,3},{2,0},{3,1},{4,6},{5,7},{6,4},{7,5},{8,10},{9,11},{10,... | collective-permute-start | bytes 110600 | tf_op jit(solution)/shard_map/ppermute | solution.py:155
  29.0 1.7 %collective-permute-start.7 = (bf16[192,96]{1,0:T(8,128)(2,1)S(1)}, bf16[192,96]{1,0:T(8,128)(2,1)S(1)}, u32[]{:S(2)}, u32[]{:S(2)}) collective-permute-start(bf16[192,96]{1,0:T(8,128)(2,1)S(1)} %get-tuple-element.37), channel_id=1, source_target_pairs={{0,4},{1,5},{2,6},{3,7},{4,0},{5,1},{6,2},{7,3},{8,12},{9,13},{10,... | collective-permute-start | bytes 110600 | tf_op jit(solution)/shard_map/ppermute | solution.py:155
  30.7 1.9 %collective-permute-done.6.refs_1_ = bf16[192,96]{1,0:T(8,128)(2,1)S(1)} collective-permute-done((bf16[192,96]{1,0:T(8,128)(2,1)S(1)}, bf16[192,96]{1,0:T(8,128)(2,1)S(1)}, u32[]{:S(2)}, u32[]{:S(2)}) %collective-permute-start.6) | collective-permute-done | bytes 36896 | tf_op jit(solution)/shard_map/ppermute | solution.py:155
  32.6 3.5 %collective-permute-start.8 = (bf16[192,96]{1,0:T(8,128)(2,1)S(1)}, bf16[192,96]{1,0:T(8,128)(2,1)S(1)}, u32[]{:S(2)}, u32[]{:S(2)}) collective-permute-start(bf16[192,96]{1,0:T(8,128)(2,1)S(1)} %get-tuple-element.38), channel_id=1, source_target_pairs={{0,6},{1,7},{2,4},{3,5},{4,2},{5,3},{6,0},{7,1},{8,14},{9,15},{10,... | collective-permute-start | bytes 110600 | tf_op jit(solution)/shard_map/ppermute | solution.py:155
  36.0 1.5 %collective-permute-done.7.refs_2_ = bf16[192,96]{1,0:T(8,128)(2,1)S(1)} collective-permute-done((bf16[192,96]{1,0:T(8,128)(2,1)S(1)}, bf16[192,96]{1,0:T(8,128)(2,1)S(1)}, u32[]{:S(2)}, u32[]{:S(2)}) %collective-permute-start.7) | collective-permute-done | bytes 36896 | tf_op jit(solution)/shard_map/ppermute | solution.py:155
  37.5 1.1 %collective-permute-done.8.refs_3_ = bf16[192,96]{1,0:T(8,128)(2,1)S(1)} collective-permute-done((bf16[192,96]{1,0:T(8,128)(2,1)S(1)}, bf16[192,96]{1,0:T(8,128)(2,1)S(1)}, u32[]{:S(2)}, u32[]{:S(2)}) %collective-permute-start.8) | collective-permute-done | bytes 36896 | tf_op jit(solution)/shard_map/ppermute | solution.py:155
  38.5 0.0 collective-permute-done.10.refs_6_
  38.5 0.0 collective-permute-done.11.refs_7_
  38.5 0.0 collective-permute-done.9.refs_5_
  38.6 0.6 %shard_map.107 = (f32[96,1024]{1,0:T(8,128)S(1)}, f32[96,1024]{1,0:T(8,128)S(1)}) custom-call(bf16[192,96]{1,0:T(8,128)(2,1)S(1)} %get-tuple-element.35.refs_0_, bf16[192,96]{1,0:T(8,128)(2,1)S(1)} %collective-permute-done.6.refs_1_, bf16[192,96]{1,0:T(8,128)(2,1)S(1)} %collective-permute-done.7.refs_2_, bf16[192,96]{1,0:T(8,128)(2,1)S(1)} %collective-permute-done.8.refs_3_, ...), custom_call_target="tpu_custom_call" | custom-call | flops 150994944 | bytes 1720320 | tf_op jit(solution)/shard_map/pallas_call | solution.py:182
  39.1 0.1 collective-permute-start.12
  39.2 1.6 %collective-permute-start.3 = (bf16[24,2048]{1,0:T(8,128)(2,1)S(1)}, bf16[24,2048]{1,0:T(8,128)(2,1)S(1)}, u32[]{:S(2)}, u32[]{:S(2)}) collective-permute-start(bf16[24,2048]{1,0:T(8,128)(2,1)S(1)} %get-tuple-element.29), channel_id=1, source_target_pairs={{0,8},{8,0},{16,24},{24,16},{1,9},{9,1},{17,25},{25,17},{2,10},{10... | collective-permute-start | bytes 294920 | tf_op jit(solution)/shard_map/ppermute | solution.py:150
  40.8 0.6 %collective-permute-start.4 = (bf16[24,2048]{1,0:T(8,128)(2,1)S(1)}, bf16[24,2048]{1,0:T(8,128)(2,1)S(1)}, u32[]{:S(2)}, u32[]{:S(2)}) collective-permute-start(bf16[24,2048]{1,0:T(8,128)(2,1)S(1)} %get-tuple-element.30), channel_id=1, source_target_pairs={{0,16},{8,24},{16,0},{24,8},{1,17},{9,25},{17,1},{25,9},{2,18},{10... | collective-permute-start | bytes 294920 | tf_op jit(solution)/shard_map/ppermute | solution.py:150
  41.4 1.4 %collective-permute-start.5 = (bf16[24,2048]{1,0:T(8,128)(2,1)S(1)}, bf16[24,2048]{1,0:T(8,128)(2,1)S(1)}, u32[]{:S(2)}, u32[]{:S(2)}) collective-permute-start(bf16[24,2048]{1,0:T(8,128)(2,1)S(1)} %get-tuple-element.31), channel_id=1, source_target_pairs={{0,24},{8,16},{16,8},{24,0},{1,25},{9,17},{17,9},{25,1},{2,26},{10... | collective-permute-start | bytes 294920 | tf_op jit(solution)/shard_map/ppermute | solution.py:150
  42.8 1.7 %collective-permute-done.3.refs_1_ = bf16[24,2048]{1,0:T(8,128)(2,1)S(1)} collective-permute-done((bf16[24,2048]{1,0:T(8,128)(2,1)S(1)}, bf16[24,2048]{1,0:T(8,128)(2,1)S(1)}, u32[]{:S(2)}, u32[]{:S(2)}) %collective-permute-start.3) | collective-permute-done | bytes 98336 | tf_op jit(solution)/shard_map/ppermute | solution.py:150
  44.4 3.3 %collective-permute-done.4.refs_2_ = bf16[24,2048]{1,0:T(8,128)(2,1)S(1)} collective-permute-done((bf16[24,2048]{1,0:T(8,128)(2,1)S(1)}, bf16[24,2048]{1,0:T(8,128)(2,1)S(1)}, u32[]{:S(2)}, u32[]{:S(2)}) %collective-permute-start.4) | collective-permute-done | bytes 98336 | tf_op jit(solution)/shard_map/ppermute | solution.py:150
  47.8 0.0 collective-permute-done.5.refs_3_
  47.8 1.1 %shard_map.105 = (bf16[128,1024]{1,0:T(8,128)(2,1)}, bf16[128,1024]{1,0:T(8,128)(2,1)}) custom-call(bf16[128,128]{1,0:T(8,128)(2,1)S(1)} %get-tuple-element.22.sel_ref, f32[128,128]{1,0:T(8,128)S(1)} %get-tuple-element.23.gsel_ref, bf16[24,2048]{1,0:T(8,128)(2,1)S(1)} %get-tuple-element.28.refs_0_, bf16[24,2048]{1,0:T(8,128)(2,1)S(1)} %collective-permute-done.3.refs_1_, ...), custom_call_target="tpu_custom_call" | custom-call | flops 100663296 | bytes 917504 | tf_op jit(solution)/shard_map/pallas_call | solution.py:252
  48.9 0.0 collective-permute-done.12
  48.9 0.8 %add_bitcast_fusion = f32[1,96,1024]{2,1,0:T(8,128)} fusion(f32[96,1024]{1,0:T(8,128)S(1)} %get-tuple-element.39, f32[96,1024]{1,0:T(8,128)S(1)} %collective-permute-done.12), kind=kLoop, calls=%fused_computation | loop fusion | flops 98304 | bytes 1179648 | tf_op jit(solution)/shard_map/broadcast_in_dim | solution.py:262
  (5 shorter events, 0.0 us)
Async XLA Ops:
  3.0 0.9 %copy-start.1 = (bf16[128,1024]{1,0:T(8,128)(2,1)S(1)}, bf16[128,1024]{1,0:T(8,128)(2,1)}, u32[]{:S(2)}) copy-start(bf16[128,1024]{1,0:T(8,128)(2,1)} %x_ref.1) | copy-start | bytes 786436
  4.0 0.9 %copy-start.2 = (bf16[128,1024]{1,0:T(8,128)(2,1)S(1)}, bf16[128,1024]{1,0:T(8,128)(2,1)}, u32[]{:S(2)}) copy-start(bf16[128,1024]{1,0:T(8,128)(2,1)} %dy_ref.1) | copy-start | bytes 786436
  5.6 6.1 %collective-permute-start = (bf16[24,2048]{1,0:T(8,128)(2,1)S(1)}, bf16[24,2048]{1,0:T(8,128)(2,1)S(1)}, u32[]{:S(2)}, u32[]{:S(2)}) collective-permute-start(bf16[24,2048]{1,0:T(8,128)(2,1)S(1)} %get-tuple-element.25), channel_id=1, source_target_pairs={{0,8},{8,0},{16,24},{24,16},{1,9},{9,1},{17,25},{25,17},{2,10},{10... | collective-permute-start | bytes 294920 | tf_op jit(solution)/shard_map/ppermute | solution.py:150
  8.6 5.7 %collective-permute-start.1 = (bf16[24,2048]{1,0:T(8,128)(2,1)S(1)}, bf16[24,2048]{1,0:T(8,128)(2,1)S(1)}, u32[]{:S(2)}, u32[]{:S(2)}) collective-permute-start(bf16[24,2048]{1,0:T(8,128)(2,1)S(1)} %get-tuple-element.26), channel_id=1, source_target_pairs={{0,16},{8,24},{16,0},{24,8},{1,17},{9,25},{17,1},{25,9},{2,18},{10... | collective-permute-start | bytes 294920 | tf_op jit(solution)/shard_map/ppermute | solution.py:150
  10.1 5.5 %collective-permute-start.2 = (bf16[24,2048]{1,0:T(8,128)(2,1)S(1)}, bf16[24,2048]{1,0:T(8,128)(2,1)S(1)}, u32[]{:S(2)}, u32[]{:S(2)}) collective-permute-start(bf16[24,2048]{1,0:T(8,128)(2,1)S(1)} %get-tuple-element.27), channel_id=1, source_target_pairs={{0,24},{8,16},{16,8},{24,0},{1,25},{9,17},{17,9},{25,1},{2,26},{10... | collective-permute-start | bytes 294920 | tf_op jit(solution)/shard_map/ppermute | solution.py:150
  15.7 22.9 %collective-permute-start.10 = (bf16[96,1024]{1,0:T(8,128)(2,1)S(1)}, bf16[96,1024]{1,0:T(8,128)(2,1)S(1)}, u32[]{:S(2)}, u32[]{:S(2)}) collective-permute-start(bf16[96,1024]{1,0:T(8,128)(2,1)S(1)} %pad_maximum_fusion.refs_4_), channel_id=1, source_target_pairs={{0,4},{1,5},{2,6},{3,7},{4,0},{5,1},{6,2},{7,3},{8,12},{9,13},{10,... | collective-permute-start | bytes 589832 | tf_op jit(solution)/shard_map/ppermute | solution.py:155
  18.3 20.2 %collective-permute-start.11 = (bf16[96,1024]{1,0:T(8,128)(2,1)S(1)}, bf16[96,1024]{1,0:T(8,128)(2,1)S(1)}, u32[]{:S(2)}, u32[]{:S(2)}) collective-permute-start(bf16[96,1024]{1,0:T(8,128)(2,1)S(1)} %pad_maximum_fusion.refs_4_), channel_id=1, source_target_pairs={{0,6},{1,7},{2,4},{3,5},{4,2},{5,3},{6,0},{7,1},{8,14},{9,15},{10,... | collective-permute-start | bytes 589832 | tf_op jit(solution)/shard_map/ppermute | solution.py:155
  19.7 18.9 %collective-permute-start.9 = (bf16[96,1024]{1,0:T(8,128)(2,1)S(1)}, bf16[96,1024]{1,0:T(8,128)(2,1)S(1)}, u32[]{:S(2)}, u32[]{:S(2)}) collective-permute-start(bf16[96,1024]{1,0:T(8,128)(2,1)S(1)} %pad_maximum_fusion.refs_4_), channel_id=1, source_target_pairs={{0,2},{1,3},{2,0},{3,1},{4,6},{5,7},{6,4},{7,5},{8,10},{9,11},{10,... | collective-permute-start | bytes 589832 | tf_op jit(solution)/shard_map/ppermute | solution.py:155
  19.9 1.9 %copy-start = (bf16[1,2,1024,768]{3,2,1,0:T(8,128)(2,1)S(1)}, bf16[1,2,1024,768]{3,2,1,0:T(8,128)(2,1)}, u32[]{:S(2)}) copy-start(bf16[1,2,1024,768]{3,2,1,0:T(8,128)(2,1)} %refs_5_.1) | copy-start | bytes 9437188
  27.1 5.4 %collective-permute-start.6 = (bf16[192,96]{1,0:T(8,128)(2,1)S(1)}, bf16[192,96]{1,0:T(8,128)(2,1)S(1)}, u32[]{:S(2)}, u32[]{:S(2)}) collective-permute-start(bf16[192,96]{1,0:T(8,128)(2,1)S(1)} %get-tuple-element.36), channel_id=1, source_target_pairs={{0,2},{1,3},{2,0},{3,1},{4,6},{5,7},{6,4},{7,5},{8,10},{9,11},{10,... | collective-permute-start | bytes 110600 | tf_op jit(solution)/shard_map/ppermute | solution.py:155
  29.0 8.5 %collective-permute-start.7 = (bf16[192,96]{1,0:T(8,128)(2,1)S(1)}, bf16[192,96]{1,0:T(8,128)(2,1)S(1)}, u32[]{:S(2)}, u32[]{:S(2)}) collective-permute-start(bf16[192,96]{1,0:T(8,128)(2,1)S(1)} %get-tuple-element.37), channel_id=1, source_target_pairs={{0,4},{1,5},{2,6},{3,7},{4,0},{5,1},{6,2},{7,3},{8,12},{9,13},{10,... | collective-permute-start | bytes 110600 | tf_op jit(solution)/shard_map/ppermute | solution.py:155
  32.6 6.0 %collective-permute-start.8 = (bf16[192,96]{1,0:T(8,128)(2,1)S(1)}, bf16[192,96]{1,0:T(8,128)(2,1)S(1)}, u32[]{:S(2)}, u32[]{:S(2)}) collective-permute-start(bf16[192,96]{1,0:T(8,128)(2,1)S(1)} %get-tuple-element.38), channel_id=1, source_target_pairs={{0,6},{1,7},{2,4},{3,5},{4,2},{5,3},{6,0},{7,1},{8,14},{9,15},{10,... | collective-permute-start | bytes 110600 | tf_op jit(solution)/shard_map/ppermute | solution.py:155
  39.1 9.8 %collective-permute-start.12 = (f32[96,1024]{1,0:T(8,128)S(1)}, f32[96,1024]{1,0:T(8,128)S(1)}, u32[]{:S(2)}, u32[]{:S(2)}) collective-permute-start(f32[96,1024]{1,0:T(8,128)S(1)} %get-tuple-element.40), channel_id=1, source_target_pairs={{0,1},{1,0},{2,3},{3,2},{4,5},{5,4},{6,7},{7,6},{8,9},{9,8},{10,11... | collective-permute-start | bytes 1179656 | tf_op jit(solution)/shard_map/ppermute | solution.py:159
  39.2 5.2 %collective-permute-start.3 = (bf16[24,2048]{1,0:T(8,128)(2,1)S(1)}, bf16[24,2048]{1,0:T(8,128)(2,1)S(1)}, u32[]{:S(2)}, u32[]{:S(2)}) collective-permute-start(bf16[24,2048]{1,0:T(8,128)(2,1)S(1)} %get-tuple-element.29), channel_id=1, source_target_pairs={{0,8},{8,0},{16,24},{24,16},{1,9},{9,1},{17,25},{25,17},{2,10},{10... | collective-permute-start | bytes 294920 | tf_op jit(solution)/shard_map/ppermute | solution.py:150
  40.8 7.0 %collective-permute-start.4 = (bf16[24,2048]{1,0:T(8,128)(2,1)S(1)}, bf16[24,2048]{1,0:T(8,128)(2,1)S(1)}, u32[]{:S(2)}, u32[]{:S(2)}) collective-permute-start(bf16[24,2048]{1,0:T(8,128)(2,1)S(1)} %get-tuple-element.30), channel_id=1, source_target_pairs={{0,16},{8,24},{16,0},{24,8},{1,17},{9,25},{17,1},{25,9},{2,18},{10... | collective-permute-start | bytes 294920 | tf_op jit(solution)/shard_map/ppermute | solution.py:150
  41.4 6.4 %collective-permute-start.5 = (bf16[24,2048]{1,0:T(8,128)(2,1)S(1)}, bf16[24,2048]{1,0:T(8,128)(2,1)S(1)}, u32[]{:S(2)}, u32[]{:S(2)}) collective-permute-start(bf16[24,2048]{1,0:T(8,128)(2,1)S(1)} %get-tuple-element.31), channel_id=1, source_target_pairs={{0,24},{8,16},{16,8},{24,0},{1,25},{9,17},{17,9},{25,1},{2,26},{10... | collective-permute-start | bytes 294920 | tf_op jit(solution)/shard_map/ppermute | solution.py:150

commit v2 on v1

v2 whole, which is shorter than its diff:
```python
import functools

import jax
import jax.numpy as jnp
from jax import lax
from jax.experimental import pallas as pl
from jax.experimental.pallas import tpu as pltpu
from jax.sharding import PartitionSpec as P

CAP = 12
PAIR = 2 * CAP
VMEM_LIMIT = 32 * 1024 * 1024
BF16 = jnp.bfloat16
F32 = jnp.float32
NEAR = pl.BlockSpec(memory_space=pltpu.VMEM)
ANY = pl.BlockSpec(memory_space=pl.ANY)
HBM = pl.BlockSpec(memory_space=pltpu.HBM)


def dot(a, b, contract=((1,), (0,))):
    return lax.dot_general(a, b, (contract, ((), ())), preferred_element_type=F32)


def partner(index, step, count):
    if count & (count - 1) == 0:
        return index ^ step
    return (index + step) % count


def call(kernel, out_shape, flops, moved, **kw):
    return pl.pallas_call(
        kernel,
        out_shape=out_shape,
        compiler_params=pltpu.CompilerParams(vmem_limit_bytes=VMEM_LIMIT),
        cost_estimate=pl.CostEstimate(flops=flops, bytes_accessed=moved, transcendentals=0),
        **kw,
    )


def route_kernel(experts, choices, *refs):
    given, (ids_ref, pick_ref, gates_ref, x_ref, dy_ref, sems) = refs[:5], refs[-6:]
    sends, (sel_ref, gsel_ref) = refs[5 : 5 + experts], refs[5 + experts : -6]
    copies = [
        pltpu.make_async_copy(src, dst, sems.at[i])
        for i, (src, dst) in enumerate(zip(given, (ids_ref, pick_ref, gates_ref, x_ref, dy_ref)))
    ]
    for copy in copies:
        copy.start()
    tok_rows, width = x_ref.shape
    rows = sel_ref.shape[0]
    me = lax.axis_index("expert")
    row = lax.broadcasted_iota(jnp.int32, (rows, tok_rows), 0)
    expert_at = jnp.zeros((rows, tok_rows), jnp.int32)
    slot_at = row
    for step in range(experts):
        inside = (row >= step * PAIR) & (row < (step + 1) * PAIR)
        expert_at = jnp.where(inside, partner(me, step, experts), expert_at)
        slot_at = jnp.where(inside, row - step * PAIR, slot_at)
    copy_at = jnp.where(slot_at >= CAP, 1, 0)
    rank_at = (slot_at - CAP * copy_at).astype(F32)
    key_at = 2 * expert_at + copy_at
    for copy in copies[:3]:
        copy.wait()
    keys = 2 * ids_ref[...] + pick_ref[...]
    gates = gates_ref[...]
    member = jnp.zeros((rows, tok_rows), F32)
    weight = jnp.zeros((rows, tok_rows), F32)
    for k in range(choices):
        hit = keys[k : k + 1, :] == key_at
        member = jnp.where(hit, 1.0, member)
        weight = jnp.where(hit, gates[k : k + 1, :], weight)
    first = lax.broadcasted_iota(jnp.int32, (tok_rows, tok_rows), 0)
    second = lax.broadcasted_iota(jnp.int32, (tok_rows, tok_rows), 1)
    earlier = jnp.where(first < second, 1.0, 0.0).astype(BF16)
    rank = dot(member.astype(BF16), earlier)
    kept = (member > 0.0) & (rank == rank_at)
    select = jnp.where(kept, 1.0, 0.0)
    gated = jnp.where(kept, weight, 0.0)
    sel_ref[...] = select
    gsel_ref[...] = gated
    pick = select.astype(BF16)
    gate_of = jnp.sum(gated, axis=1, keepdims=True)
    copies[3].wait()
    chosen = dot(pick, x_ref[...]).astype(BF16)
    copies[4].wait()
    grads = (gate_of * dot(pick, dy_ref[...])).astype(BF16)
    for step in range(experts):
        at = slice(step * PAIR, (step + 1) * PAIR)
        sends[step][:, :width] = chosen[at]
        sends[step][:, width:] = grads[at]


def weights_kernel(after, gate_hbm, up_hbm, down_hbm, gate_ref, up_ref, down_ref, sems):
    del after
    pairs = ((gate_hbm, gate_ref), (up_hbm, up_ref), (down_hbm, down_ref))
    copies = [
        pltpu.make_async_copy(src.at[0, 0], dst, sems.at[i]) for i, (src, dst) in enumerate(pairs)
    ]
    for copy in copies:
        copy.start()
    for copy in copies:
        copy.wait()


def joined(parts):
    return jnp.concatenate([p.astype(F32) for p in parts], axis=0).astype(BF16)


def join_kernel(experts, after, *refs):
    del after
    blocks, d_ref = refs[:experts], refs[experts]
    d_ref[...] = joined([b[:, d_ref.shape[1] :] for b in blocks])


def expert_kernel(experts, chunk, starts, *refs):
    blocks, (gate_ref, up_ref, down_ref) = refs[:experts], refs[experts : experts + 3]
    outs, hts = refs[experts + 3 : 2 * experts + 3], refs[2 * experts + 3 : -3]
    ht_s, res_s, grad_s = refs[-3:]
    hidden_width, width = down_ref.shape
    x = joined([b[:, :width] for b in blocks])
    d_out = joined([b[:, width:] for b in blocks])
    for start in range(0, hidden_width, chunk):
        at = slice(start, start + chunk)
        gate_w, up_w, down_w = gate_ref[:, at], up_ref[:, at], down_ref[at, :]
        gate_pre = dot(x, gate_w)
        up_pre = dot(x, up_w)
        sig = jax.nn.sigmoid(gate_pre)
        silu = gate_pre * sig
        hidden = silu * up_pre
        ht_s[at, :] = hidden.T.astype(BF16)
        res = dot(hidden.astype(BF16), down_w)
        dhidden = dot(d_out, down_w, ((1,), (1,)))
        d_gate = (dhidden * up_pre * sig * (1.0 + gate_pre * (1.0 - sig))).astype(BF16)
        d_up = (dhidden * silu).astype(BF16)
        grad = dot(d_gate, gate_w, ((1,), (1,))) + dot(d_up, up_w, ((1,), (1,)))
        if start == 0:
            res_s[...] = res
            grad_s[...] = grad
        else:
            res_s[...] += res
            grad_s[...] += grad
    for step in range(experts):
        rows = pl.ds(step * PAIR, PAIR)
        outs[step][:, :width] = res_s[rows, :].astype(BF16)
        outs[step][:, width:] = grad_s[rows, :].astype(BF16)
    for ht, firsts in zip(hts, starts()):
        share = ht.shape[0] // len(firsts)
        for i, first in enumerate(firsts):
            ht[i * share : (i + 1) * share, :] = ht_s[pl.ds(pl.multiple_of(first * share, 16), share), :]


def combine_kernel(experts, after, sel_ref, gsel_ref, *refs):
    del after
    blocks, (out_ref, grad_ref) = refs[:experts], refs[experts:]
    width = out_ref.shape[1]
    back = joined([b[...] for b in blocks])
    result, d_rows = back[:, :width], back[:, width:]
    weight = gsel_ref[...].T
    high = weight.astype(BF16)
    rest = weight - high.astype(F32)
    mid = rest.astype(BF16)
    low = (rest - mid.astype(F32)).astype(BF16)
    out_ref[...] = (dot(high, result) + (dot(mid, result) + dot(low, result))).astype(BF16)
    grad_ref[...] = dot(sel_ref[...].T.astype(BF16), d_rows).astype(BF16)


def pack_kernel(d_ref, far_ref, near_ht, far_ht, *refs):
    pair_ref = refs[-1]
    rows, width = d_ref.shape
    half = near_ht.shape[0] // 2
    pair_ref[:rows] = d_ref[...]
    pair_ref[rows : 2 * rows] = far_ref[...]
    pair_ref[2 * rows :] = jnp.zeros_like(pair_ref[2 * rows :])
    step = pair_ref.shape[0] - 2 * rows
    lanes = width // (2 * half // step)
    for i in range(2 * half // step):
        src, first = (near_ht, i * step) if i * step < half else (far_ht, i * step - half)
        pair_ref[2 * rows :, i * lanes : i * lanes + rows] = src[half + first : half + first + step]


def outer_kernel(scale, d_ref, far_ref, near_ht, far_ht, pair_ref, keep_ref, give_ref):
    rows, width = d_ref.shape
    share = keep_ref.shape[0]
    half = 2 * share
    step = pair_ref.shape[0] - 2 * rows
    count = 2 * half // step
    lanes = width // count
    total = dot(near_ht[:half], d_ref[...]) + dot(far_ht[:half], far_ref[...])
    for i in range(2):
        blocks = range(i * count // 2, (i + 1) * count // 2)
        ht = jnp.concatenate(
            [pair_ref[2 * rows :, k * lanes : k * lanes + rows] for k in blocks], axis=0
        )
        total += dot(ht, pair_ref[i * rows : (i + 1) * rows])
    keep_ref[...] = total[:share] * scale
    give_ref[...] = (total[share:] * scale).astype(BF16)


def swap(value, axis, count, step):
    return lax.ppermute(value, axis, [(i, partner(i, step, count)) for i in range(count)])


CORE, EXCHANGE, FAR = 1, 2, 4
NEAR_UNITS = (0, EXCHANGE, CORE, CORE ^ EXCHANGE)


def gathered_units():
    me = lax.axis_index("dp")
    return [[me ^ unit for unit in NEAR_UNITS], [me ^ FAR ^ unit for unit in NEAR_UNITS]]


def all_units():
    return [[0]]


def grad_by_rows(hts, d_out, home, groups):
    near_ht, far_ht = hts
    rows, width = d_out.shape
    share = near_ht.shape[0] // 4
    far = swap(d_out, "dp", groups, FAR)
    far_ht = swap(far_ht, "dp", groups, FAR)
    extra = near_ht.shape[0] * 128 // width
    pair = call(
        pack_kernel,
        jax.ShapeDtypeStruct((2 * rows + extra, width), BF16),
        0,
        8 * rows * width,
        in_specs=[NEAR] * 4 + [ANY] * len(home),
    )(d_out, far, near_ht, far_ht, *home)
    pair = swap(pair, "dp", groups, CORE)
    keep, give = call(
        functools.partial(outer_kernel, 1.0 / groups),
        [jax.ShapeDtypeStruct((share, width), F32), jax.ShapeDtypeStruct((share, width), BF16)],
        16 * rows * share * width,
        6 * share * width + 8 * rows * (width + 2 * share),
    )(d_out, far, near_ht, far_ht, pair)
    return keep, give


def grad_by_sums(hts, d_out, groups):
    total = lax.psum_scatter(dot(hts[0], d_out), "dp", scatter_dimension=0, tiled=True)
    return total / groups


def on_device(
    tokens, cotangent, route_gates, expert_ids, replica, hot_experts, w_gate, w_up, w_down
):
    del hot_experts
    ids, picks, gates, tokens, cotangent, w_gate, w_up, w_down = (
        pltpu.with_memory_space_constraint(a, pltpu.HBM)
        for a in (
            expert_ids.T, replica.T, route_gates.T, tokens, cotangent, w_gate, w_up, w_down
        )
    )
    experts = lax.axis_size("expert")
    groups = lax.axis_size("dp")
    tok_rows, width = tokens.shape
    hidden_width = w_gate.shape[3]
    choices = expert_ids.shape[1]
    rows = experts * PAIR
    block = jax.ShapeDtypeStruct((PAIR, 2 * width), BF16)

    *sends, sel, gsel = call(
        functools.partial(route_kernel, experts, choices),
        [block] * experts + [jax.ShapeDtypeStruct((rows, tok_rows), F32)] * 2,
        4 * rows * tok_rows * width,
        4 * (tok_rows + rows) * width,
        in_specs=[HBM] * 5,
        scratch_shapes=[
            pltpu.VMEM((choices, tok_rows), jnp.int32),
            pltpu.VMEM((choices, tok_rows), jnp.int32),
            pltpu.VMEM((choices, tok_rows), F32),
            pltpu.VMEM((tok_rows, width), BF16),
            pltpu.VMEM((tok_rows, width), BF16),
            pltpu.SemaphoreType.DMA((5,)),
        ],
    )(ids, picks, gates, tokens, cotangent)

    own_gate, own_up, own_down = call(
        weights_kernel,
        [
            jax.ShapeDtypeStruct((width, hidden_width), BF16),
            jax.ShapeDtypeStruct((width, hidden_width), BF16),
            jax.ShapeDtypeStruct((hidden_width, width), BF16),
        ],
        0,
        12 * width * hidden_width,
        in_specs=[ANY] + [HBM] * 3,
        scratch_shapes=[pltpu.SemaphoreType.DMA((3,))],
    )(gsel, w_gate, w_up, w_down)

    came = [sends[0]] + [swap(sends[s], "expert", experts, s) for s in range(1, experts)]
    d_out = call(
        functools.partial(join_kernel, experts),
        jax.ShapeDtypeStruct((rows, width), BF16),
        0,
        4 * rows * width,
        in_specs=[ANY] + [NEAR] * experts,
    )(own_gate, *came)

    share = hidden_width // groups
    short = groups == 8 and share % 32 == 0 and rows <= 128 and width % 128 == 0
    if short:
        parts = [jax.ShapeDtypeStruct((4 * share, rows), BF16)] * 2
    else:
        parts = [jax.ShapeDtypeStruct((hidden_width, rows), BF16)]
    chunk = 256 if hidden_width % 256 == 0 else hidden_width
    outs = call(
        functools.partial(expert_kernel, experts, chunk, gathered_units if short else all_units),
        [block] * experts + parts,
        12 * rows * width * hidden_width,
        6 * width * hidden_width + 12 * rows * width,
        scratch_shapes=[
            pltpu.VMEM((hidden_width, rows), BF16),
            pltpu.VMEM((rows, width), F32),
            pltpu.VMEM((rows, width), F32),
        ],
    )(*came, own_gate, own_up, own_down)
    results, hts = outs[:experts], outs[experts:]

    pairs = experts & (experts - 1) == 0
    home = [results[0]] + [
        swap(results[s], "expert", experts, s if pairs else experts - s) for s in range(1, experts)
    ]
    if short:
        keep, give = grad_by_rows(hts, d_out, home, groups)
        grad = keep + swap(give, "dp", groups, EXCHANGE).astype(F32)
    else:
        give = sel
        grad = grad_by_sums(hts, d_out, groups)
    layer_out, grad_tokens = call(
        functools.partial(combine_kernel, experts),
        [jax.ShapeDtypeStruct((tok_rows, width), BF16)] * 2,
        8 * rows * tok_rows * width,
        4 * (tok_rows + rows) * width,
        in_specs=[ANY] + [NEAR] * (2 + experts),
    )(give, sel, gsel, *home)
    return layer_out, grad_tokens, grad[None]


def solution(mesh):
    in_specs = (
        P(("expert", "dp"), None),
        P(("expert", "dp"), None),
        P(("expert", "dp"), None),
        P(("expert", "dp"), None),
        P(("expert", "dp"), None),
        P(),
        P("expert", None, None, None),
        P("expert", None, None, None),
        P("expert", None, None, None),
    )
    out_specs = (P(("expert", "dp"), None), P(("expert", "dp"), None), P("expert", "dp", None))
    return jax.shard_map(
        on_device, mesh=mesh, in_specs=in_specs, out_specs=out_specs, check_vma=False
    )
```

time: 50 us -> 37.5 us (0.75)
  starting transfers between devices: 19.4 us -> 12.8 us
  local copies, waits for them, and re-layouts: 6.18 us -> 0 us
  Pallas kernels: 7.72 us -> 8.73 us
  waiting for transfers between devices: 14.9 us -> 14.3 us
    ppermute x7 -> x0, starting transfers between devices: 11.3 us -> none  [the longest x6 11.2 us: swap_chip(): return lax.ppermute(value, 'dp', pairs)]
    unnamed x9 -> x0, local copies, waits for them, and re-layouts: 6.16 us -> none
    ppermute x6 -> x10, starting transfers between devices: 8.1 us -> 12.8 us  [swap(): lax.ppermute(value, axis, [(i, partner(i, step, count)) for i in range(co...]
    ppermute x7 -> x0, waiting for transfers between devices: 4.4 us -> none  [the longest x6 4.4 us: swap_chip(): return lax.ppermute(value, 'dp', pairs)]
    ppermute x6 -> x10, waiting for transfers between devices: 10.5 us -> 14.3 us  [swap(): lax.ppermute(value, axis, [(i, partner(i, step, count)) for i in range(co...]
    pallas_call x1, Pallas kernels: 0.7 us -> 1.46 us  [on_device(): call(functools.partial(route_kernel, experts, choices), [block] * experts...]
    pallas_call x3 -> x5, Pallas kernels: 5.88 us -> 6.07 us  [the longest x1 3.09 us: on_device(): call(functools.partial(expert_kernel, experts, chunk, gathered_units if s...]
  transfers between devices with their start and end apart: 13 -> 10, of which waited for: 8 -> 5; matrix products, arithmetic and copies ran while one was open for 0% -> 0% of each run, Pallas kernels for 13% -> 18%
where the time goes in v2:
time: 37.5 us; the launch traced here: 37.3 us
  waiting for transfers between devices  14.3 us (38%)
  starting transfers between devices  12.8 us (34%)
  Pallas kernels  8.73 us (23%)
  other arithmetic  0.79 us (2%)
  between operations  0.71 us (2%)
    ppermute x10, waiting for transfers between devices, swap(): lax.ppermute(value, axis, [(i, partner(i, step, count)) for i in range(co...  14.3 us
    ppermute x10, starting transfers between devices, swap(): lax.ppermute(value, axis, [(i, partner(i, step, count)) for i in range(co...  12.8 us
    pallas_call x1, Pallas kernels, on_device(): call(functools.partial(expert_kernel, experts, chunk, gathered_units if s...  3.09 us
    pallas_call x1, Pallas kernels, on_device(): call(weights_kernel, [jax.ShapeDtypeStruct((width, hidden_width), BF16),...  2.38 us
    pallas_call x1, Pallas kernels, on_device(): call(functools.partial(route_kernel, experts, choices), [block] * experts...  1.46 us
    pallas_call x1, Pallas kernels, on_device(): call(functools.partial(combine_kernel, experts), [jax.ShapeDtypeStruct((t...  1.2 us
    broadcast_in_dim x1, other arithmetic, on_device(): return (layer_out, grad_tokens, grad[None])  0.79 us
  transfers between devices with their start and end apart: 10, of which 5 were waited for; matrix products, arithmetic and copies ran while one was open for 0% of the time, Pallas kernels for 18%

profile of v2, /device:TPU:0, one launch (start us, length us, event | category | flops | bytes accessed | tf_op | source)
XLA Modules:
  0.0 37.3 jit_solution(12122917187626893941)
XLA Ops:
  0.6 1.5 %shard_map.103 = (bf16[24,2048]{1,0:T(8,128)(2,1)S(1)}, bf16[24,2048]{1,0:T(8,128)(2,1)S(1)}, bf16[24,2048]{1,0:T(8,128)(2,1)S(1)}, bf16[24,2048]{1,0:T(8,128)(2...) custom-call(s32[6,128]{1,0:T(8,128)} %bitcast.5, s32[6,128]{1,0:T(8,128)} %bitcast.6, f32[6,128]{1,0:T(8,128)} %bitcast.7, ...), custom_call_target="tpu_custom_call" | custom-call | flops 50331648 | bytes 917504 | tf_op jit(solution)/shard_map/pallas_call | solution.py:263
  2.1 3.0 %collective-permute-start = (bf16[24,2048]{1,0:T(8,128)(2,1)S(1)}, bf16[24,2048]{1,0:T(8,128)(2,1)S(1)}, u32[]{:S(2)}, u32[]{:S(2)}) collective-permute-start(bf16[24,2048]{1,0:T(8,128)(2,1)S(1)} %get-tuple-element.25), channel_id=1, source_target_pairs={{0,8},{8,0},{16,24},{24,16},{1,9},{9,1},{17,25},{25,17},{2,10},{10... | collective-permute-start | bytes 294920 | tf_op jit(solution)/shard_map/ppermute | solution.py:200
  5.1 1.5 %collective-permute-start.1 = (bf16[24,2048]{1,0:T(8,128)(2,1)S(1)}, bf16[24,2048]{1,0:T(8,128)(2,1)S(1)}, u32[]{:S(2)}, u32[]{:S(2)}) collective-permute-start(bf16[24,2048]{1,0:T(8,128)(2,1)S(1)} %get-tuple-element.26), channel_id=1, source_target_pairs={{0,16},{8,24},{16,0},{24,8},{1,17},{9,25},{17,1},{25,9},{2,18},{10... | collective-permute-start | bytes 294920 | tf_op jit(solution)/shard_map/ppermute | solution.py:200
  6.6 0.0 collective-permute-start.2
  6.6 2.4 %shard_map.104 = (bf16[1024,768]{1,0:T(8,128)(2,1)S(1)}, bf16[1024,768]{1,0:T(8,128)(2,1)S(1)}, bf16[768,1024]{1,0:T(8,128)(2,1)S(1)}) custom-call(f32[96,128]{1,0:T(8,128)S(1)} %get-tuple-element.22.after.gsel_ref, bf16[1,2,1024,768]{3,2,1,0:T(8,128)(2,1)} %gate_hbm.1, bf16[1,2,1024,768]{3,2,1,0:T(8,128)(2,1)} %up_hbm.1, bf16[1,2,768,1024]{3,2,1,0:T(8,128)(2,1)} %down_hbm.1), custom_call_target="tpu_custom_call" | custom-call | bytes 9437184 | tf_op jit(solution)/shard_map/pallas_call | solution.py:279
  9.0 0.0 collective-permute-done.refs_1_
  9.0 1.7 %collective-permute-done.1.refs_2_ = bf16[24,2048]{1,0:T(8,128)(2,1)S(1)} collective-permute-done((bf16[24,2048]{1,0:T(8,128)(2,1)S(1)}, bf16[24,2048]{1,0:T(8,128)(2,1)S(1)}, u32[]{:S(2)}, u32[]{:S(2)}) %collective-permute-start.1) | collective-permute-done | bytes 98336 | tf_op jit(solution)/shard_map/ppermute | solution.py:200
  10.8 1.4 %collective-permute-done.2.refs_3_ = bf16[24,2048]{1,0:T(8,128)(2,1)S(1)} collective-permute-done((bf16[24,2048]{1,0:T(8,128)(2,1)S(1)}, bf16[24,2048]{1,0:T(8,128)(2,1)S(1)}, u32[]{:S(2)}, u32[]{:S(2)}) %collective-permute-start.2) | collective-permute-done | bytes 98336 | tf_op jit(solution)/shard_map/ppermute | solution.py:200
  12.2 2.6 %collective-permute-start.3 = (bf16[96,1024]{1,0:T(8,128)(2,1)S(1)}, bf16[96,1024]{1,0:T(8,128)(2,1)S(1)}, u32[]{:S(2)}, u32[]{:S(2)}) collective-permute-start(bf16[96,1024]{1,0:T(8,128)(2,1)S(1)} %shard_map.105.d_ref), channel_id=1, source_target_pairs={{0,4},{1,5},{2,6},{3,7},{4,0},{5,1},{6,2},{7,3},{8,12},{9,13},{10,... | collective-permute-start | bytes 589832 | tf_op jit(solution)/shard_map/ppermute | solution.py:200
  14.8 3.1 %shard_map.106 = (bf16[24,2048]{1,0:T(8,128)(2,1)S(1)}, bf16[24,2048]{1,0:T(8,128)(2,1)S(1)}, bf16[24,2048]{1,0:T(8,128)(2,1)S(1)}, bf16[24,2048]{1,0:T(8,128)(2...) custom-call(bf16[24,2048]{1,0:T(8,128)(2,1)S(1)} %get-tuple-element.24.refs_0_, ...), custom_call_target="tpu_custom_call" | custom-call | flops 905969664 | bytes 5898240 | tf_op jit(solution)/shard_map/pallas_call | solution.py:308
  17.9 0.7 %collective-permute-start.5 = (bf16[24,2048]{1,0:T(8,128)(2,1)S(1)}, bf16[24,2048]{1,0:T(8,128)(2,1)S(1)}, u32[]{:S(2)}, u32[]{:S(2)}) collective-permute-start(bf16[24,2048]{1,0:T(8,128)(2,1)S(1)} %get-tuple-element.33), channel_id=1, source_target_pairs={{0,8},{8,0},{16,24},{24,16},{1,9},{9,1},{17,25},{25,17},{2,10},{10... | collective-permute-start | bytes 294920 | tf_op jit(solution)/shard_map/ppermute | solution.py:200
  18.6 1.0 %collective-permute-start.6 = (bf16[24,2048]{1,0:T(8,128)(2,1)S(1)}, bf16[24,2048]{1,0:T(8,128)(2,1)S(1)}, u32[]{:S(2)}, u32[]{:S(2)}) collective-permute-start(bf16[24,2048]{1,0:T(8,128)(2,1)S(1)} %get-tuple-element.34), channel_id=1, source_target_pairs={{0,16},{8,24},{16,0},{24,8},{1,17},{9,25},{17,1},{25,9},{2,18},{10... | collective-permute-start | bytes 294920 | tf_op jit(solution)/shard_map/ppermute | solution.py:200
  19.6 1.9 %collective-permute-start.7 = (bf16[24,2048]{1,0:T(8,128)(2,1)S(1)}, bf16[24,2048]{1,0:T(8,128)(2,1)S(1)}, u32[]{:S(2)}, u32[]{:S(2)}) collective-permute-start(bf16[24,2048]{1,0:T(8,128)(2,1)S(1)} %get-tuple-element.35), channel_id=1, source_target_pairs={{0,24},{8,16},{16,8},{24,0},{1,25},{9,17},{17,9},{25,1},{2,26},{10... | collective-permute-start | bytes 294920 | tf_op jit(solution)/shard_map/ppermute | solution.py:200
  21.5 0.3 collective-permute-start.4
  21.8 5.2 %collective-permute-done.4.far_ht = bf16[384,96]{1,0:T(8,128)(2,1)S(1)} collective-permute-done((bf16[384,96]{1,0:T(8,128)(2,1)S(1)}, bf16[384,96]{1,0:T(8,128)(2,1)S(1)}, u32[]{:S(2)}, u32[]{:S(2)}) %collective-permute-start.4) | collective-permute-done | bytes 73760 | tf_op jit(solution)/shard_map/ppermute | solution.py:200
  27.0 0.0 collective-permute-done.5.refs_1_
  27.0 0.0 collective-permute-done.6.refs_2_
  27.0 0.0 collective-permute-done.7.refs_3_
  27.0 0.0 collective-permute-done.3.far_ref
  27.1 0.1 collective-permute-start.8
  27.1 1.9 %collective-permute-done.8.pair_ref = bf16[240,1024]{1,0:T(8,128)(2,1)S(1)} collective-permute-done((bf16[240,1024]{1,0:T(8,128)(2,1)S(1)}, bf16[240,1024]{1,0:T(8,128)(2,1)S(1)}, u32[]{:S(2)}, u32[]{:S(2)}) %collective-permute-start.8) | collective-permute-done | bytes 491552 | tf_op jit(solution)/shard_map/ppermute | solution.py:200
  29.0 0.5 %shard_map.108 = (f32[96,1024]{1,0:T(8,128)S(1)}, bf16[96,1024]{1,0:T(8,128)(2,1)S(1)}) custom-call(bf16[96,1024]{1,0:T(8,128)(2,1)S(1)} %shard_map.105.d_ref, bf16[96,1024]{1,0:T(8,128)(2,1)S(1)} %collective-permute-done.3.far_ref, bf16[384,96]{1,0:T(8,128)(2,1)S(1)} %get-tuple-element.30.near_ht, bf16[384,96]{1,0:T(8,128)(2,1)S(1)} %collective-permute-done.4.far_ht, ...), custom_call_target="tpu_custom_call" | custom-call | flops 150994944 | bytes 1523712 | tf_op jit(solution)/shard_map/pallas_call | solution.py:231
  29.5 1.7 %collective-permute-start.9 = (bf16[96,1024]{1,0:T(8,128)(2,1)S(1)}, bf16[96,1024]{1,0:T(8,128)(2,1)S(1)}, u32[]{:S(2)}, u32[]{:S(2)}) collective-permute-start(bf16[96,1024]{1,0:T(8,128)(2,1)S(1)} %get-tuple-element.36.after), channel_id=1, source_target_pairs={{0,2},{1,3},{2,0},{3,1},{4,6},{5,7},{6,4},{7,5},{8,10},{9,11},{10,... | collective-permute-start | bytes 589832 | tf_op jit(solution)/shard_map/ppermute | solution.py:200
  31.2 1.2 %shard_map.109 = (bf16[128,1024]{1,0:T(8,128)(2,1)}, bf16[128,1024]{1,0:T(8,128)(2,1)}) custom-call(bf16[96,1024]{1,0:T(8,128)(2,1)S(1)} %get-tuple-element.36.after, f32[96,128]{1,0:T(8,128)S(1)} %get-tuple-element.37.sel_ref, f32[96,128]{1,0:T(8,128)S(1)} %get-tuple-element.22.after.gsel_ref, bf16[24,2048]{1,0:T(8,128)(2,1)S(1)} %get-tuple-element.32.refs_0_, ...), custom_call_target="tpu_custom_call" | custom-call | flops 100663296 | bytes 917504 | tf_op jit(solution)/shard_map/pallas_call | solution.py:331
  32.4 4.1 %collective-permute-done.9 = bf16[96,1024]{1,0:T(8,128)(2,1)S(1)} collective-permute-done((bf16[96,1024]{1,0:T(8,128)(2,1)S(1)}, bf16[96,1024]{1,0:T(8,128)(2,1)S(1)}, u32[]{:S(2)}, u32[]{:S(2)}) %collective-permute-start.9) | collective-permute-done | bytes 196640 | tf_op jit(solution)/shard_map/ppermute | solution.py:200
  36.6 0.8 %add_bitcast_fusion = f32[1,96,1024]{2,1,0:T(8,128)} fusion(f32[96,1024]{1,0:T(8,128)S(1)} %get-tuple-element.40, bf16[96,1024]{1,0:T(8,128)(2,1)S(1)} %collective-permute-done.9), kind=kLoop, calls=%fused_computation | loop fusion | flops 196608 | bytes 983040 | tf_op jit(solution)/shard_map/broadcast_in_dim | solution.py:338
  (2 shorter events, 0.1 us)
Async XLA Ops:
  2.1 6.9 %collective-permute-start = (bf16[24,2048]{1,0:T(8,128)(2,1)S(1)}, bf16[24,2048]{1,0:T(8,128)(2,1)S(1)}, u32[]{:S(2)}, u32[]{:S(2)}) collective-permute-start(bf16[24,2048]{1,0:T(8,128)(2,1)S(1)} %get-tuple-element.25), channel_id=1, source_target_pairs={{0,8},{8,0},{16,24},{24,16},{1,9},{9,1},{17,25},{25,17},{2,10},{10... | collective-permute-start | bytes 294920 | tf_op jit(solution)/shard_map/ppermute | solution.py:200
  5.1 5.7 %collective-permute-start.1 = (bf16[24,2048]{1,0:T(8,128)(2,1)S(1)}, bf16[24,2048]{1,0:T(8,128)(2,1)S(1)}, u32[]{:S(2)}, u32[]{:S(2)}) collective-permute-start(bf16[24,2048]{1,0:T(8,128)(2,1)S(1)} %get-tuple-element.26), channel_id=1, source_target_pairs={{0,16},{8,24},{16,0},{24,8},{1,17},{9,25},{17,1},{25,9},{2,18},{10... | collective-permute-start | bytes 294920 | tf_op jit(solution)/shard_map/ppermute | solution.py:200
  6.6 5.5 %collective-permute-start.2 = (bf16[24,2048]{1,0:T(8,128)(2,1)S(1)}, bf16[24,2048]{1,0:T(8,128)(2,1)S(1)}, u32[]{:S(2)}, u32[]{:S(2)}) collective-permute-start(bf16[24,2048]{1,0:T(8,128)(2,1)S(1)} %get-tuple-element.27), channel_id=1, source_target_pairs={{0,24},{8,16},{16,8},{24,0},{1,25},{9,17},{17,9},{25,1},{2,26},{10... | collective-permute-start | bytes 294920 | tf_op jit(solution)/shard_map/ppermute | solution.py:200
  12.2 14.8 %collective-permute-start.3 = (bf16[96,1024]{1,0:T(8,128)(2,1)S(1)}, bf16[96,1024]{1,0:T(8,128)(2,1)S(1)}, u32[]{:S(2)}, u32[]{:S(2)}) collective-permute-start(bf16[96,1024]{1,0:T(8,128)(2,1)S(1)} %shard_map.105.d_ref), channel_id=1, source_target_pairs={{0,4},{1,5},{2,6},{3,7},{4,0},{5,1},{6,2},{7,3},{8,12},{9,13},{10,... | collective-permute-start | bytes 589832 | tf_op jit(solution)/shard_map/ppermute | solution.py:200
  17.9 9.1 %collective-permute-start.5 = (bf16[24,2048]{1,0:T(8,128)(2,1)S(1)}, bf16[24,2048]{1,0:T(8,128)(2,1)S(1)}, u32[]{:S(2)}, u32[]{:S(2)}) collective-permute-start(bf16[24,2048]{1,0:T(8,128)(2,1)S(1)} %get-tuple-element.33), channel_id=1, source_target_pairs={{0,8},{8,0},{16,24},{24,16},{1,9},{9,1},{17,25},{25,17},{2,10},{10... | collective-permute-start | bytes 294920 | tf_op jit(solution)/shard_map/ppermute | solution.py:200
  18.6 8.4 %collective-permute-start.6 = (bf16[24,2048]{1,0:T(8,128)(2,1)S(1)}, bf16[24,2048]{1,0:T(8,128)(2,1)S(1)}, u32[]{:S(2)}, u32[]{:S(2)}) collective-permute-start(bf16[24,2048]{1,0:T(8,128)(2,1)S(1)} %get-tuple-element.34), channel_id=1, source_target_pairs={{0,16},{8,24},{16,0},{24,8},{1,17},{9,25},{17,1},{25,9},{2,18},{10... | collective-permute-start | bytes 294920 | tf_op jit(solution)/shard_map/ppermute | solution.py:200
  19.6 7.4 %collective-permute-start.7 = (bf16[24,2048]{1,0:T(8,128)(2,1)S(1)}, bf16[24,2048]{1,0:T(8,128)(2,1)S(1)}, u32[]{:S(2)}, u32[]{:S(2)}) collective-permute-start(bf16[24,2048]{1,0:T(8,128)(2,1)S(1)} %get-tuple-element.35), channel_id=1, source_target_pairs={{0,24},{8,16},{16,8},{24,0},{1,25},{9,17},{17,9},{25,1},{2,26},{10... | collective-permute-start | bytes 294920 | tf_op jit(solution)/shard_map/ppermute | solution.py:200
  21.5 5.5 %collective-permute-start.4 = (bf16[384,96]{1,0:T(8,128)(2,1)S(1)}, bf16[384,96]{1,0:T(8,128)(2,1)S(1)}, u32[]{:S(2)}, u32[]{:S(2)}) collective-permute-start(bf16[384,96]{1,0:T(8,128)(2,1)S(1)} %get-tuple-element.31), channel_id=1, source_target_pairs={{0,4},{1,5},{2,6},{3,7},{4,0},{5,1},{6,2},{7,3},{8,12},{9,13},{10,... | collective-permute-start | bytes 221192 | tf_op jit(solution)/shard_map/ppermute | solution.py:200
  27.1 1.9 %collective-permute-start.8 = (bf16[240,1024]{1,0:T(8,128)(2,1)S(1)}, bf16[240,1024]{1,0:T(8,128)(2,1)S(1)}, u32[]{:S(2)}, u32[]{:S(2)}) collective-permute-start(bf16[240,1024]{1,0:T(8,128)(2,1)S(1)} %shard_map.107), channel_id=1, source_target_pairs={{0,1},{1,0},{2,3},{3,2},{4,5},{5,4},{6,7},{7,6},{8,9},{9,8},{10,11... | collective-permute-start | bytes 1474568 | tf_op jit(solution)/shard_map/ppermute | solution.py:200
  29.5 7.0 %collective-permute-start.9 = (bf16[96,1024]{1,0:T(8,128)(2,1)S(1)}, bf16[96,1024]{1,0:T(8,128)(2,1)S(1)}, u32[]{:S(2)}, u32[]{:S(2)}) collective-permute-start(bf16[96,1024]{1,0:T(8,128)(2,1)S(1)} %get-tuple-element.36.after), channel_id=1, source_target_pairs={{0,2},{1,3},{2,0},{3,1},{4,6},{5,7},{6,4},{7,5},{8,10},{9,11},{10,... | collective-permute-start | bytes 589832 | tf_op jit(solution)/shard_map/ppermute | solution.py:200

commit v3 on v2

--- a/solution.py
+++ b/solution.py
@@ -13,6 +13,7 @@
 BF16 = jnp.bfloat16
 F32 = jnp.float32
 NEAR = pl.BlockSpec(memory_space=pltpu.VMEM)
+FLOPS, BYTES = 1.0e9, 3.0e6
 ANY = pl.BlockSpec(memory_space=pl.ANY)
 HBM = pl.BlockSpec(memory_space=pltpu.HBM)
 
@@ -27,12 +28,14 @@
     return (index + step) % count
 
 
-def call(kernel, out_shape, flops, moved, **kw):
+def call(kernel, micros, out_shape, **kw):
     return pl.pallas_call(
         kernel,
         out_shape=out_shape,
         compiler_params=pltpu.CompilerParams(vmem_limit_bytes=VMEM_LIMIT),
-        cost_estimate=pl.CostEstimate(flops=flops, bytes_accessed=moved, transcendentals=0),
+        cost_estimate=pl.CostEstimate(
+            flops=int(micros * FLOPS), bytes_accessed=int(micros * BYTES), transcendentals=0
+        ),
         **kw,
     )
 
@@ -112,26 +115,48 @@
     d_ref[...] = joined([b[:, d_ref.shape[1] :] for b in blocks])
 
 
-def expert_kernel(experts, chunk, starts, *refs):
-    blocks, (gate_ref, up_ref, down_ref) = refs[:experts], refs[experts : experts + 3]
-    outs, hts = refs[experts + 3 : 2 * experts + 3], refs[2 * experts + 3 : -3]
-    ht_s, res_s, grad_s = refs[-3:]
-    hidden_width, width = down_ref.shape
-    x = joined([b[:, :width] for b in blocks])
-    d_out = joined([b[:, width:] for b in blocks])
+def forward_kernel(experts, chunk, units_of, after, *refs):
+    del after
+    blocks, (gate_ref, up_ref), hts = refs[:experts], refs[experts : experts + 2], refs[experts + 2 : -5]
+    hidden_ref, dgate_ref, silu_ref, x_s, ht_s = refs[-5:]
+    width, hidden_width = gate_ref.shape
+    x_s[...] = joined([b[:, :width] for b in blocks])
     for start in range(0, hidden_width, chunk):
         at = slice(start, start + chunk)
-        gate_w, up_w, down_w = gate_ref[:, at], up_ref[:, at], down_ref[at, :]
-        gate_pre = dot(x, gate_w)
-        up_pre = dot(x, up_w)
+        gate_pre = dot(x_s[...], gate_ref[:, at])
+        up_pre = dot(x_s[...], up_ref[:, at])
         sig = jax.nn.sigmoid(gate_pre)
         silu = gate_pre * sig
         hidden = silu * up_pre
         ht_s[at, :] = hidden.T.astype(BF16)
-        res = dot(hidden.astype(BF16), down_w)
-        dhidden = dot(d_out, down_w, ((1,), (1,)))
-        d_gate = (dhidden * up_pre * sig * (1.0 + gate_pre * (1.0 - sig))).astype(BF16)
-        d_up = (dhidden * silu).astype(BF16)
+        hidden_ref[:, at] = hidden.astype(BF16)
+        dgate_ref[:, at] = up_pre * sig * (1.0 + gate_pre * (1.0 - sig))
+        silu_ref[:, at] = silu
+    for ht, firsts in zip(hts, units_of()):
+        share = hidden_width if len(firsts) == 1 else hidden_width // 8
+        units = [
+            ht_s[pl.ds(pl.multiple_of(first * share, 16), share), :] for first in firsts
+        ]
+        for i, unit in enumerate(units[: ht.shape[0] // share]):
+            if ht.shape[1] > unit.shape[1]:
+                more = ht.shape[1] - unit.shape[1]
+                unit = beside([unit, units[-1][:, i * more : (i + 1) * more]])
+            ht[i * share : (i + 1) * share, :] = unit
+
+
+def backward_kernel(experts, chunk, *refs):
+    blocks, (gate_ref, up_ref, down_ref) = refs[:experts], refs[experts : experts + 3]
+    hidden_ref, dgate_ref, silu_ref = refs[experts + 3 : experts + 6]
+    outs, (d_s, res_s, grad_s) = refs[experts + 6 : -3], refs[-3:]
+    hidden_width, width = down_ref.shape
+    d_s[...] = joined([b[:, width:] for b in blocks])
+    for start in range(0, hidden_width, chunk):
+        at = slice(start, start + chunk)
+        gate_w, up_w, down_w = gate_ref[:, at], up_ref[:, at], down_ref[at, :]
+        res = dot(hidden_ref[:, at], down_w)
+        dhidden = dot(d_s[...], down_w, ((1,), (1,)))
+        d_gate = (dhidden * dgate_ref[:, at]).astype(BF16)
+        d_up = (dhidden * silu_ref[:, at]).astype(BF16)
         grad = dot(d_gate, gate_w, ((1,), (1,))) + dot(d_up, up_w, ((1,), (1,)))
         if start == 0:
             res_s[...] = res
@@ -143,14 +168,9 @@
         rows = pl.ds(step * PAIR, PAIR)
         outs[step][:, :width] = res_s[rows, :].astype(BF16)
         outs[step][:, width:] = grad_s[rows, :].astype(BF16)
-    for ht, firsts in zip(hts, starts()):
-        share = ht.shape[0] // len(firsts)
-        for i, first in enumerate(firsts):
-            ht[i * share : (i + 1) * share, :] = ht_s[pl.ds(pl.multiple_of(first * share, 16), share), :]
-
-
-def combine_kernel(experts, after, sel_ref, gsel_ref, *refs):
-    del after
+
+
+def combine_kernel(experts, sel_ref, gsel_ref, *refs):
     blocks, (out_ref, grad_ref) = refs[:experts], refs[experts:]
     width = out_ref.shape[1]
     back = joined([b[...] for b in blocks])
@@ -164,28 +184,37 @@
     grad_ref[...] = dot(sel_ref[...].T.astype(BF16), d_rows).astype(BF16)
 
 
-def pack_kernel(d_ref, far_ref, near_ht, far_ht, *refs):
-    pair_ref = refs[-1]
+def beside(parts):
+    return jnp.concatenate([p.astype(F32) for p in parts], axis=1).astype(BF16)
+
+
+def pack_kernel(d_ref, far_ref, near_ht, far_ht, after, pair_ref):
+    del after
     rows, width = d_ref.shape
-    half = near_ht.shape[0] // 2
+    share = near_ht.shape[0] // 4
     pair_ref[:rows] = d_ref[...]
     pair_ref[rows : 2 * rows] = far_ref[...]
     pair_ref[2 * rows :] = jnp.zeros_like(pair_ref[2 * rows :])
     step = pair_ref.shape[0] - 2 * rows
-    lanes = width // (2 * half // step)
-    for i in range(2 * half // step):
-        src, first = (near_ht, i * step) if i * step < half else (far_ht, i * step - half)
-        pair_ref[2 * rows :, i * lanes : i * lanes + rows] = src[half + first : half + first + step]
-
-
-def outer_kernel(scale, d_ref, far_ref, near_ht, far_ht, pair_ref, keep_ref, give_ref):
-    rows, width = d_ref.shape
+    lanes = width // (4 * share // step)
+    last = beside([far_ht[k * share : (k + 1) * share, rows:] for k in range(3)])
+    units = [near_ht[2 * share : 3 * share], near_ht[3 * share :], far_ht[2 * share :, :rows], last]
+    at = 0
+    for unit in units:
+        for first in range(0, share, step):
+            pair_ref[2 * rows :, at : at + rows] = unit[first : first + step]
+            at += lanes
+
+
+def outer_kernel(scale, near_ht, far_ht, own_ref, pair_ref, *refs):
+    keep_ref, give_ref = refs[-2:]
+    rows, width = near_ht.shape[1], own_ref.shape[1]
     share = keep_ref.shape[0]
     half = 2 * share
     step = pair_ref.shape[0] - 2 * rows
     count = 2 * half // step
     lanes = width // count
-    total = dot(near_ht[:half], d_ref[...]) + dot(far_ht[:half], far_ref[...])
+    total = dot(near_ht[:half], own_ref[:rows]) + dot(far_ht[:half, :rows], own_ref[rows : 2 * rows])
     for i in range(2):
         blocks = range(i * count // 2, (i + 1) * count // 2)
         ht = jnp.concatenate(
@@ -196,11 +225,17 @@
     give_ref[...] = (total[share:] * scale).astype(BF16)
 
 
+def release_kernel(count, after, *refs):
+    del after
+    for src, dst in zip(refs[:count], refs[count:]):
+        dst[...] = src[...]
+
+
 def swap(value, axis, count, step):
     return lax.ppermute(value, axis, [(i, partner(i, step, count)) for i in range(count)])
 
 
-CORE, EXCHANGE, FAR = 1, 2, 4
+CORE, FAR, EXCHANGE = 1, 2, 4
 NEAR_UNITS = (0, EXCHANGE, CORE, CORE ^ EXCHANGE)
 
 
@@ -213,28 +248,25 @@
     return [[0]]
 
 
-def grad_by_rows(hts, d_out, home, groups):
+def grad_by_rows(hts, d_out, after, groups):
     near_ht, far_ht = hts
     rows, width = d_out.shape
     share = near_ht.shape[0] // 4
     far = swap(d_out, "dp", groups, FAR)
     far_ht = swap(far_ht, "dp", groups, FAR)
     extra = near_ht.shape[0] * 128 // width
-    pair = call(
+    own = call(
         pack_kernel,
+        0.2,
         jax.ShapeDtypeStruct((2 * rows + extra, width), BF16),
-        0,
-        8 * rows * width,
-        in_specs=[NEAR] * 4 + [ANY] * len(home),
-    )(d_out, far, near_ht, far_ht, *home)
-    pair = swap(pair, "dp", groups, CORE)
-    keep, give = call(
+        in_specs=[NEAR] * 4 + [ANY],
+    )(d_out, far, near_ht, far_ht, after)
+    pair = swap(own, "dp", groups, CORE)
+    return call(
         functools.partial(outer_kernel, 1.0 / groups),
+        0.6,
         [jax.ShapeDtypeStruct((share, width), F32), jax.ShapeDtypeStruct((share, width), BF16)],
-        16 * rows * share * width,
-        6 * share * width + 8 * rows * (width + 2 * share),
-    )(d_out, far, near_ht, far_ht, pair)
-    return keep, give
+    )(near_ht, far_ht, own, pair)
 
 
 def grad_by_sums(hts, d_out, groups):
@@ -262,9 +294,8 @@
 
     *sends, sel, gsel = call(
         functools.partial(route_kernel, experts, choices),
+        1.4,
         [block] * experts + [jax.ShapeDtypeStruct((rows, tok_rows), F32)] * 2,
-        4 * rows * tok_rows * width,
-        4 * (tok_rows + rows) * width,
         in_specs=[HBM] * 5,
         scratch_shapes=[
             pltpu.VMEM((choices, tok_rows), jnp.int32),
@@ -278,13 +309,12 @@
 
     own_gate, own_up, own_down = call(
         weights_kernel,
+        2.4,
         [
             jax.ShapeDtypeStruct((width, hidden_width), BF16),
             jax.ShapeDtypeStruct((width, hidden_width), BF16),
             jax.ShapeDtypeStruct((hidden_width, width), BF16),
         ],
-        0,
-        12 * width * hidden_width,
         in_specs=[ANY] + [HBM] * 3,
         scratch_shapes=[pltpu.SemaphoreType.DMA((3,))],
     )(gsel, w_gate, w_up, w_down)
@@ -292,49 +322,61 @@
     came = [sends[0]] + [swap(sends[s], "expert", experts, s) for s in range(1, experts)]
     d_out = call(
         functools.partial(join_kernel, experts),
+        0.2,
         jax.ShapeDtypeStruct((rows, width), BF16),
-        0,
-        4 * rows * width,
         in_specs=[ANY] + [NEAR] * experts,
     )(own_gate, *came)
 
     share = hidden_width // groups
-    short = groups == 8 and share % 32 == 0 and rows <= 128 and width % 128 == 0
+    short = groups == 8 and experts == 4 and share % 32 == 0
     if short:
-        parts = [jax.ShapeDtypeStruct((4 * share, rows), BF16)] * 2
+        parts = [
+            jax.ShapeDtypeStruct((4 * share, rows), BF16),
+            jax.ShapeDtypeStruct((3 * share, rows + rows // 3), BF16),
+        ]
     else:
         parts = [jax.ShapeDtypeStruct((hidden_width, rows), BF16)]
     chunk = 256 if hidden_width % 256 == 0 else hidden_width
-    outs = call(
-        functools.partial(expert_kernel, experts, chunk, gathered_units if short else all_units),
-        [block] * experts + parts,
-        12 * rows * width * hidden_width,
-        6 * width * hidden_width + 12 * rows * width,
+    factors = [jax.ShapeDtypeStruct((rows, hidden_width), t) for t in (BF16, F32, F32)]
+    *hts, hidden, d_gate, silu = call(
+        functools.partial(forward_kernel, experts, chunk, gathered_units if short else all_units),
+        0.9,
+        parts + factors,
+        in_specs=[ANY] + [NEAR] * (experts + 2),
+        scratch_shapes=[pltpu.VMEM((rows, width), BF16), pltpu.VMEM((hidden_width, rows), BF16)],
+    )(d_out, *came, own_gate, own_up)
+    own_result, *results = call(
+        functools.partial(backward_kernel, experts, chunk),
+        2.6,
+        [block] * experts,
         scratch_shapes=[
-            pltpu.VMEM((hidden_width, rows), BF16),
+            pltpu.VMEM((rows, width), BF16),
             pltpu.VMEM((rows, width), F32),
             pltpu.VMEM((rows, width), F32),
         ],
-    )(*came, own_gate, own_up, own_down)
-    results, hts = outs[:experts], outs[experts:]
+    )(*came, own_gate, own_up, own_down, hidden, d_gate, silu)
+
+    if short:
+        keep, give = grad_by_rows(hts, d_out, own_result, groups)
+        grad = keep + swap(give, "dp", groups, EXCHANGE).astype(F32)
+        results = call(
+            functools.partial(release_kernel, experts - 1),
+            9.0,
+            [block] * (experts - 1),
+            in_specs=[ANY] + [NEAR] * (experts - 1),
+        )(give, *results)
+    else:
+        grad = grad_by_sums(hts, d_out, groups)
 
     pairs = experts & (experts - 1) == 0
-    home = [results[0]] + [
-        swap(results[s], "expert", experts, s if pairs else experts - s) for s in range(1, experts)
+    home = [own_result] + [
+        swap(results[s - 1], "expert", experts, s if pairs else experts - s) for s in range(1, experts)
     ]
-    if short:
-        keep, give = grad_by_rows(hts, d_out, home, groups)
-        grad = keep + swap(give, "dp", groups, EXCHANGE).astype(F32)
-    else:
-        give = sel
-        grad = grad_by_sums(hts, d_out, groups)
     layer_out, grad_tokens = call(
         functools.partial(combine_kernel, experts),
+        0.1,
         [jax.ShapeDtypeStruct((tok_rows, width), BF16)] * 2,
-        8 * rows * tok_rows * width,
-        4 * (tok_rows + rows) * width,
-        in_specs=[ANY] + [NEAR] * (2 + experts),
-    )(give, sel, gsel, *home)
+    )(sel, gsel, *home)
     return layer_out, grad_tokens, grad[None]
 
 

time: 37.5 us -> 34.8 us (0.928)
  waiting for transfers between devices: 14.3 us -> 10.9 us
  Pallas kernels: 8.73 us -> 9.21 us
    ppermute x10, waiting for transfers between devices: 14.3 us -> 10.9 us  [swap(): lax.ppermute(value, axis, [(i, partner(i, step, count)) for i in range(co...]
    pallas_call x7 -> x9, Pallas kernels: 8.73 us -> 9.21 us  [the longest x1 2.61 us: on_device(): call(functools.partial(backward_kernel, experts, chunk), 2.6, [block] * e...]
  transfers between devices with their start and end apart: 10 -> 10, of which waited for: 5 -> 7; matrix products, arithmetic and copies ran while one was open for 0% -> 0% of each run, Pallas kernels for 18% -> 21%
where the time goes in v3:
time: 34.8 us; the launch traced here: 34.6 us
  starting transfers between devices  13 us (37%)
  waiting for transfers between devices  10.9 us (31%)
  Pallas kernels  9.21 us (26%)
  other arithmetic  0.8 us (2%)
  between operations  0.7 us (2%)
    ppermute x10, starting transfers between devices, swap(): lax.ppermute(value, axis, [(i, partner(i, step, count)) for i in range(co...  13 us
    ppermute x10, waiting for transfers between devices, swap(): lax.ppermute(value, axis, [(i, partner(i, step, count)) for i in range(co...  10.9 us
    pallas_call x1, Pallas kernels, on_device(): call(functools.partial(backward_kernel, experts, chunk), 2.6, [block] * e...  2.61 us
    pallas_call x1, Pallas kernels, on_device(): call(weights_kernel, 2.4, [jax.ShapeDtypeStruct((width, hidden_width), BF...  2.38 us
    pallas_call x1, Pallas kernels, on_device(): call(functools.partial(route_kernel, experts, choices), 1.4, [block] * ex...  1.46 us
    pallas_call x1, Pallas kernels, on_device(): call(functools.partial(combine_kernel, experts), 0.1, [jax.ShapeDtypeStru...  1.21 us
    pallas_call x1, Pallas kernels, on_device(): call(functools.partial(forward_kernel, experts, chunk, gathered_units if...  0.87 us
    broadcast_in_dim x1, other arithmetic, on_device(): return (layer_out, grad_tokens, grad[None])  0.8 us
  transfers between devices with their start and end apart: 10, of which 7 were waited for; matrix products, arithmetic and copies ran while one was open for 0% of the time, Pallas kernels for 21%

profile of v3, /device:TPU:0, one launch (start us, length us, event | category | flops | bytes accessed | tf_op | source)
XLA Modules:
  0.0 34.6 jit_solution(3566764539279003004)
XLA Ops:
  0.6 1.5 %shard_map.103 = (bf16[24,2048]{1,0:T(8,128)(2,1)S(1)}, bf16[24,2048]{1,0:T(8,128)(2,1)S(1)}, bf16[24,2048]{1,0:T(8,128)(2,1)S(1)}, bf16[24,2048]{1,0:T(8,128)(2...) custom-call(s32[6,128]{1,0:T(8,128)} %bitcast.5, s32[6,128]{1,0:T(8,128)} %bitcast.6, f32[6,128]{1,0:T(8,128)} %bitcast.7, ...), custom_call_target="tpu_custom_call" | custom-call | flops 1400000000 | bytes 4200000 | tf_op jit(solution)/shard_map/pallas_call | solution.py:295
  2.1 3.0 %collective-permute-start = (bf16[24,2048]{1,0:T(8,128)(2,1)S(1)}, bf16[24,2048]{1,0:T(8,128)(2,1)S(1)}, u32[]{:S(2)}, u32[]{:S(2)}) collective-permute-start(bf16[24,2048]{1,0:T(8,128)(2,1)S(1)} %get-tuple-element.31), channel_id=1, source_target_pairs={{0,8},{8,0},{16,24},{24,16},{1,9},{9,1},{17,25},{25,17},{2,10},{10... | collective-permute-start | bytes 294920 | tf_op jit(solution)/shard_map/ppermute | solution.py:235
  5.1 1.5 %collective-permute-start.1 = (bf16[24,2048]{1,0:T(8,128)(2,1)S(1)}, bf16[24,2048]{1,0:T(8,128)(2,1)S(1)}, u32[]{:S(2)}, u32[]{:S(2)}) collective-permute-start(bf16[24,2048]{1,0:T(8,128)(2,1)S(1)} %get-tuple-element.32), channel_id=1, source_target_pairs={{0,16},{8,24},{16,0},{24,8},{1,17},{9,25},{17,1},{25,9},{2,18},{10... | collective-permute-start | bytes 294920 | tf_op jit(solution)/shard_map/ppermute | solution.py:235
  6.6 0.0 collective-permute-start.2
  6.6 2.4 %shard_map.104 = (bf16[1024,768]{1,0:T(8,128)(2,1)S(1)}, bf16[1024,768]{1,0:T(8,128)(2,1)S(1)}, bf16[768,1024]{1,0:T(8,128)(2,1)S(1)}) custom-call(f32[96,128]{1,0:T(8,128)S(1)} %get-tuple-element.29.after.gsel_ref, bf16[1,2,1024,768]{3,2,1,0:T(8,128)(2,1)} %gate_hbm.1, bf16[1,2,1024,768]{3,2,1,0:T(8,128)(2,1)} %up_hbm.1, bf16[1,2,768,1024]{3,2,1,0:T(8,128)(2,1)} %down_hbm.1), custom_call_target="tpu_custom_call" | custom-call | flops 2400000000 | bytes 7200000 | tf_op jit(solution)/shard_map/pallas_call | solution.py:310
  9.0 0.0 collective-permute-done.refs_1_
  9.0 1.7 %collective-permute-done.1.refs_2_ = bf16[24,2048]{1,0:T(8,128)(2,1)S(1)} collective-permute-done((bf16[24,2048]{1,0:T(8,128)(2,1)S(1)}, bf16[24,2048]{1,0:T(8,128)(2,1)S(1)}, u32[]{:S(2)}, u32[]{:S(2)}) %collective-permute-start.1) | collective-permute-done | bytes 98336 | tf_op jit(solution)/shard_map/ppermute | solution.py:235
  10.8 1.4 %collective-permute-done.2.refs_3_ = bf16[24,2048]{1,0:T(8,128)(2,1)S(1)} collective-permute-done((bf16[24,2048]{1,0:T(8,128)(2,1)S(1)}, bf16[24,2048]{1,0:T(8,128)(2,1)S(1)}, u32[]{:S(2)}, u32[]{:S(2)}) %collective-permute-start.2) | collective-permute-done | bytes 98336 | tf_op jit(solution)/shard_map/ppermute | solution.py:235
  12.2 1.6 %collective-permute-start.4 = (bf16[96,1024]{1,0:T(8,128)(2,1)S(1)}, bf16[96,1024]{1,0:T(8,128)(2,1)S(1)}, u32[]{:S(2)}, u32[]{:S(2)}) collective-permute-start(bf16[96,1024]{1,0:T(8,128)(2,1)S(1)} %shard_map.105.after.d_ref), channel_id=1, source_target_pairs={{0,2},{1,3},{2,0},{3,1},{4,6},{5,7},{6,4},{7,5},{8,10},{9,11},{10,... | collective-permute-start | bytes 589832 | tf_op jit(solution)/shard_map/ppermute | solution.py:235
  13.8 0.9 %shard_map.106 = (bf16[384,96]{1,0:T(8,128)(2,1)S(1)}, bf16[288,128]{1,0:T(8,128)(2,1)S(1)}, bf16[96,768]{1,0:T(8,128)(2,1)S(1)}, f32[96,768]{1,0:T(8,128)S(1)}, f32[96,768]{1,0:T(8,128)S(1)}) custom-call(bf16[96,1024]{1,0:T(8,128)(2,1)S(1)} %shard_map.105.after.d_ref, bf16[24,2048]{1,0:T(8,128)(2,1)S(1)} %get-tuple-element.30.refs_0_, ...), custom_call_target="tpu_custom_call" | custom-call | flops 900000000 | bytes 2700000 | tf_op jit(solution)/shard_map/pallas_call | solution.py:341
  14.7 0.5 %collective-permute-start.3 = (bf16[288,128]{1,0:T(8,128)(2,1)S(1)}, bf16[288,128]{1,0:T(8,128)(2,1)S(1)}, u32[]{:S(2)}, u32[]{:S(2)}) collective-permute-start(bf16[288,128]{1,0:T(8,128)(2,1)S(1)} %get-tuple-element.42), channel_id=1, source_target_pairs={{0,2},{1,3},{2,0},{3,1},{4,6},{5,7},{6,4},{7,5},{8,10},{9,11},{10,... | collective-permute-start | bytes 221192 | tf_op jit(solution)/shard_map/ppermute | solution.py:235
  15.2 2.6 %shard_map.107 = (bf16[24,2048]{1,0:T(8,128)(2,1)S(1)}, bf16[24,2048]{1,0:T(8,128)(2,1)S(1)}, bf16[24,2048]{1,0:T(8,128)(2,1)S(1)}, bf16[24,2048]{1,0:T(8,128)(2,1)S(1)}) custom-call(bf16[24,2048]{1,0:T(8,128)(2,1)S(1)} %get-tuple-element.30.refs_0_, bf16[24,2048]{1,0:T(8,128)(2,1)S(1)} %collective-permute-done.refs_1_, ...), custom_call_target="tpu_custom_call" | custom-call | flops 2600000000 | bytes 7800000 | tf_op jit(solution)/shard_map/pallas_call | solution.py:348
  17.8 1.3 %collective-permute-done.3.far_ht = bf16[288,128]{1,0:T(8,128)(2,1)S(1)} collective-permute-done((bf16[288,128]{1,0:T(8,128)(2,1)S(1)}, bf16[288,128]{1,0:T(8,128)(2,1)S(1)}, u32[]{:S(2)}, u32[]{:S(2)}) %collective-permute-start.3) | collective-permute-done | bytes 73760 | tf_op jit(solution)/shard_map/ppermute | solution.py:235
  19.1 0.0 collective-permute-done.4.far_ref
  19.1 0.1 shard_map.108.own_ref
  19.2 0.1 collective-permute-start.5
  19.3 1.9 %collective-permute-done.5.pair_ref = bf16[240,1024]{1,0:T(8,128)(2,1)S(1)} collective-permute-done((bf16[240,1024]{1,0:T(8,128)(2,1)S(1)}, bf16[240,1024]{1,0:T(8,128)(2,1)S(1)}, u32[]{:S(2)}, u32[]{:S(2)}) %collective-permute-start.5) | collective-permute-done | bytes 491552 | tf_op jit(solution)/shard_map/ppermute | solution.py:235
  21.1 0.6 %shard_map.109 = (f32[96,1024]{1,0:T(8,128)S(1)}, bf16[96,1024]{1,0:T(8,128)(2,1)S(1)}) custom-call(bf16[384,96]{1,0:T(8,128)(2,1)S(1)} %get-tuple-element.41.near_ht, bf16[288,128]{1,0:T(8,128)(2,1)S(1)} %collective-permute-done.3.far_ht, bf16[240,1024]{1,0:T(8,128)(2,1)S(1)} %shard_map.108.own_ref, bf16[240,1024]{1,0:T(8,128)(2,1)S(1)} %collective-permute-done.5.pair_ref), custom_call_target="tpu_custom_call" | custom-call | flops 600000000 | bytes 1800000 | tf_op jit(solution)/shard_map/pallas_call | solution.py:265
  21.7 2.7 %collective-permute-start.9 = (bf16[96,1024]{1,0:T(8,128)(2,1)S(1)}, bf16[96,1024]{1,0:T(8,128)(2,1)S(1)}, u32[]{:S(2)}, u32[]{:S(2)}) collective-permute-start(bf16[96,1024]{1,0:T(8,128)(2,1)S(1)} %get-tuple-element.43.after), channel_id=1, source_target_pairs={{0,4},{1,5},{2,6},{3,7},{4,0},{5,1},{6,2},{7,3},{8,12},{9,13},{10,... | collective-permute-start | bytes 589832 | tf_op jit(solution)/shard_map/ppermute | solution.py:235
  24.4 1.3 %collective-permute-start.6 = (bf16[24,2048]{1,0:T(8,128)(2,1)S(1)}, bf16[24,2048]{1,0:T(8,128)(2,1)S(1)}, u32[]{:S(2)}, u32[]{:S(2)}) collective-permute-start(bf16[24,2048]{1,0:T(8,128)(2,1)S(1)} %get-tuple-element.47), channel_id=1, source_target_pairs={{0,8},{8,0},{16,24},{24,16},{1,9},{9,1},{17,25},{25,17},{2,10},{10... | collective-permute-start | bytes 294920 | tf_op jit(solution)/shard_map/ppermute | solution.py:235
  25.7 0.6 %collective-permute-start.7 = (bf16[24,2048]{1,0:T(8,128)(2,1)S(1)}, bf16[24,2048]{1,0:T(8,128)(2,1)S(1)}, u32[]{:S(2)}, u32[]{:S(2)}) collective-permute-start(bf16[24,2048]{1,0:T(8,128)(2,1)S(1)} %get-tuple-element.48), channel_id=1, source_target_pairs={{0,16},{8,24},{16,0},{24,8},{1,17},{9,25},{17,1},{25,9},{2,18},{10... | collective-permute-start | bytes 294920 | tf_op jit(solution)/shard_map/ppermute | solution.py:235
  26.3 1.6 %collective-permute-start.8 = (bf16[24,2048]{1,0:T(8,128)(2,1)S(1)}, bf16[24,2048]{1,0:T(8,128)(2,1)S(1)}, u32[]{:S(2)}, u32[]{:S(2)}) collective-permute-start(bf16[24,2048]{1,0:T(8,128)(2,1)S(1)} %get-tuple-element.49), channel_id=1, source_target_pairs={{0,24},{8,16},{16,8},{24,0},{1,25},{9,17},{17,9},{25,1},{2,26},{10... | collective-permute-start | bytes 294920 | tf_op jit(solution)/shard_map/ppermute | solution.py:235
  27.9 1.1 %collective-permute-done.6.refs_1_ = bf16[24,2048]{1,0:T(8,128)(2,1)S(1)} collective-permute-done((bf16[24,2048]{1,0:T(8,128)(2,1)S(1)}, bf16[24,2048]{1,0:T(8,128)(2,1)S(1)}, u32[]{:S(2)}, u32[]{:S(2)}) %collective-permute-start.6) | collective-permute-done | bytes 98336 | tf_op jit(solution)/shard_map/ppermute | solution.py:235
  29.0 3.3 %collective-permute-done.7.refs_2_ = bf16[24,2048]{1,0:T(8,128)(2,1)S(1)} collective-permute-done((bf16[24,2048]{1,0:T(8,128)(2,1)S(1)}, bf16[24,2048]{1,0:T(8,128)(2,1)S(1)}, u32[]{:S(2)}, u32[]{:S(2)}) %collective-permute-start.7) | collective-permute-done | bytes 98336 | tf_op jit(solution)/shard_map/ppermute | solution.py:235
  32.3 0.0 collective-permute-done.8.refs_3_
  32.3 1.2 %shard_map.111 = (bf16[128,1024]{1,0:T(8,128)(2,1)}, bf16[128,1024]{1,0:T(8,128)(2,1)}) custom-call(f32[96,128]{1,0:T(8,128)S(1)} %get-tuple-element.28.sel_ref, f32[96,128]{1,0:T(8,128)S(1)} %get-tuple-element.29.after.gsel_ref, bf16[24,2048]{1,0:T(8,128)(2,1)S(1)} %get-tuple-element.40.after.refs_0_, bf16[24,2048]{1,0:T(8,128)(2,1)S(1)} %collective-permute-done.6.refs_1_, ...), custom_call_target="tpu_custom_call" | custom-call | flops 100000000 | bytes 300000 | tf_op jit(solution)/shard_map/pallas_call | solution.py:375
  33.5 0.3 collective-permute-done.9
  33.8 0.8 %add_bitcast_fusion = f32[1,96,1024]{2,1,0:T(8,128)} fusion(f32[96,1024]{1,0:T(8,128)S(1)} %get-tuple-element.52, bf16[96,1024]{1,0:T(8,128)(2,1)S(1)} %collective-permute-done.9), kind=kLoop, calls=%fused_computation | loop fusion | flops 196608 | bytes 983040 | tf_op jit(solution)/shard_map/broadcast_in_dim | solution.py:380
  (2 shorter events, 0.0 us)
Async XLA Ops:
  2.1 6.9 %collective-permute-start = (bf16[24,2048]{1,0:T(8,128)(2,1)S(1)}, bf16[24,2048]{1,0:T(8,128)(2,1)S(1)}, u32[]{:S(2)}, u32[]{:S(2)}) collective-permute-start(bf16[24,2048]{1,0:T(8,128)(2,1)S(1)} %get-tuple-element.31), channel_id=1, source_target_pairs={{0,8},{8,0},{16,24},{24,16},{1,9},{9,1},{17,25},{25,17},{2,10},{10... | collective-permute-start | bytes 294920 | tf_op jit(solution)/shard_map/ppermute | solution.py:235
  5.1 5.7 %collective-permute-start.1 = (bf16[24,2048]{1,0:T(8,128)(2,1)S(1)}, bf16[24,2048]{1,0:T(8,128)(2,1)S(1)}, u32[]{:S(2)}, u32[]{:S(2)}) collective-permute-start(bf16[24,2048]{1,0:T(8,128)(2,1)S(1)} %get-tuple-element.32), channel_id=1, source_target_pairs={{0,16},{8,24},{16,0},{24,8},{1,17},{9,25},{17,1},{25,9},{2,18},{10... | collective-permute-start | bytes 294920 | tf_op jit(solution)/shard_map/ppermute | solution.py:235
  6.6 5.5 %collective-permute-start.2 = (bf16[24,2048]{1,0:T(8,128)(2,1)S(1)}, bf16[24,2048]{1,0:T(8,128)(2,1)S(1)}, u32[]{:S(2)}, u32[]{:S(2)}) collective-permute-start(bf16[24,2048]{1,0:T(8,128)(2,1)S(1)} %get-tuple-element.33), channel_id=1, source_target_pairs={{0,24},{8,16},{16,8},{24,0},{1,25},{9,17},{17,9},{25,1},{2,26},{10... | collective-permute-start | bytes 294920 | tf_op jit(solution)/shard_map/ppermute | solution.py:235
  12.2 6.9 %collective-permute-start.4 = (bf16[96,1024]{1,0:T(8,128)(2,1)S(1)}, bf16[96,1024]{1,0:T(8,128)(2,1)S(1)}, u32[]{:S(2)}, u32[]{:S(2)}) collective-permute-start(bf16[96,1024]{1,0:T(8,128)(2,1)S(1)} %shard_map.105.after.d_ref), channel_id=1, source_target_pairs={{0,2},{1,3},{2,0},{3,1},{4,6},{5,7},{6,4},{7,5},{8,10},{9,11},{10,... | collective-permute-start | bytes 589832 | tf_op jit(solution)/shard_map/ppermute | solution.py:235
  14.7 4.4 %collective-permute-start.3 = (bf16[288,128]{1,0:T(8,128)(2,1)S(1)}, bf16[288,128]{1,0:T(8,128)(2,1)S(1)}, u32[]{:S(2)}, u32[]{:S(2)}) collective-permute-start(bf16[288,128]{1,0:T(8,128)(2,1)S(1)} %get-tuple-element.42), channel_id=1, source_target_pairs={{0,2},{1,3},{2,0},{3,1},{4,6},{5,7},{6,4},{7,5},{8,10},{9,11},{10,... | collective-permute-start | bytes 221192 | tf_op jit(solution)/shard_map/ppermute | solution.py:235
  19.2 1.9 %collective-permute-start.5 = (bf16[240,1024]{1,0:T(8,128)(2,1)S(1)}, bf16[240,1024]{1,0:T(8,128)(2,1)S(1)}, u32[]{:S(2)}, u32[]{:S(2)}) collective-permute-start(bf16[240,1024]{1,0:T(8,128)(2,1)S(1)} %shard_map.108.own_ref), channel_id=1, source_target_pairs={{0,1},{1,0},{2,3},{3,2},{4,5},{5,4},{6,7},{7,6},{8,9},{9,8},{10,11... | collective-permute-start | bytes 1474568 | tf_op jit(solution)/shard_map/ppermute | solution.py:235
  21.7 12.1 %collective-permute-start.9 = (bf16[96,1024]{1,0:T(8,128)(2,1)S(1)}, bf16[96,1024]{1,0:T(8,128)(2,1)S(1)}, u32[]{:S(2)}, u32[]{:S(2)}) collective-permute-start(bf16[96,1024]{1,0:T(8,128)(2,1)S(1)} %get-tuple-element.43.after), channel_id=1, source_target_pairs={{0,4},{1,5},{2,6},{3,7},{4,0},{5,1},{6,2},{7,3},{8,12},{9,13},{10,... | collective-permute-start | bytes 589832 | tf_op jit(solution)/shard_map/ppermute | solution.py:235
  24.4 4.7 %collective-permute-start.6 = (bf16[24,2048]{1,0:T(8,128)(2,1)S(1)}, bf16[24,2048]{1,0:T(8,128)(2,1)S(1)}, u32[]{:S(2)}, u32[]{:S(2)}) collective-permute-start(bf16[24,2048]{1,0:T(8,128)(2,1)S(1)} %get-tuple-element.47), channel_id=1, source_target_pairs={{0,8},{8,0},{16,24},{24,16},{1,9},{9,1},{17,25},{25,17},{2,10},{10... | collective-permute-start | bytes 294920 | tf_op jit(solution)/shard_map/ppermute | solution.py:235
  25.7 6.6 %collective-permute-start.7 = (bf16[24,2048]{1,0:T(8,128)(2,1)S(1)}, bf16[24,2048]{1,0:T(8,128)(2,1)S(1)}, u32[]{:S(2)}, u32[]{:S(2)}) collective-permute-start(bf16[24,2048]{1,0:T(8,128)(2,1)S(1)} %get-tuple-element.48), channel_id=1, source_target_pairs={{0,16},{8,24},{16,0},{24,8},{1,17},{9,25},{17,1},{25,9},{2,18},{10... | collective-permute-start | bytes 294920 | tf_op jit(solution)/shard_map/ppermute | solution.py:235
  26.3 6.0 %collective-permute-start.8 = (bf16[24,2048]{1,0:T(8,128)(2,1)S(1)}, bf16[24,2048]{1,0:T(8,128)(2,1)S(1)}, u32[]{:S(2)}, u32[]{:S(2)}) collective-permute-start(bf16[24,2048]{1,0:T(8,128)(2,1)S(1)} %get-tuple-element.49), channel_id=1, source_target_pairs={{0,24},{8,16},{16,8},{24,0},{1,25},{9,17},{17,9},{25,1},{2,26},{10... | collective-permute-start | bytes 294920 | tf_op jit(solution)/shard_map/ppermute | solution.py:235

commit v4 on v3

--- a/solution.py
+++ b/solution.py
@@ -93,14 +93,22 @@
         sends[step][:, width:] = grads[at]
 
 
-def weights_kernel(after, gate_hbm, up_hbm, down_hbm, gate_ref, up_ref, down_ref, sems):
-    del after
+def weights_kernel(sel_ref, gsel_ref, gate_hbm, up_hbm, down_hbm, *refs):
+    gate_ref, up_ref, down_ref, pick_ref, high_ref, mid_ref, low_ref, sems = refs
     pairs = ((gate_hbm, gate_ref), (up_hbm, up_ref), (down_hbm, down_ref))
     copies = [
         pltpu.make_async_copy(src.at[0, 0], dst, sems.at[i]) for i, (src, dst) in enumerate(pairs)
     ]
     for copy in copies:
         copy.start()
+    pick_ref[...] = sel_ref[...].T.astype(BF16)
+    weight = gsel_ref[...].T
+    high = weight.astype(BF16)
+    rest = weight - high.astype(F32)
+    mid = rest.astype(BF16)
+    high_ref[...] = high
+    mid_ref[...] = mid
+    low_ref[...] = (rest - mid.astype(F32)).astype(BF16)
     for copy in copies:
         copy.wait()
 
@@ -170,18 +178,14 @@
         outs[step][:, width:] = grad_s[rows, :].astype(BF16)
 
 
-def combine_kernel(experts, sel_ref, gsel_ref, *refs):
+def combine_kernel(experts, pick_ref, high_ref, mid_ref, low_ref, *refs):
     blocks, (out_ref, grad_ref) = refs[:experts], refs[experts:]
     width = out_ref.shape[1]
     back = joined([b[...] for b in blocks])
     result, d_rows = back[:, :width], back[:, width:]
-    weight = gsel_ref[...].T
-    high = weight.astype(BF16)
-    rest = weight - high.astype(F32)
-    mid = rest.astype(BF16)
-    low = (rest - mid.astype(F32)).astype(BF16)
-    out_ref[...] = (dot(high, result) + (dot(mid, result) + dot(low, result))).astype(BF16)
-    grad_ref[...] = dot(sel_ref[...].T.astype(BF16), d_rows).astype(BF16)
+    total = dot(mid_ref[...], result) + dot(low_ref[...], result)
+    out_ref[...] = (dot(high_ref[...], result) + total).astype(BF16)
+    grad_ref[...] = dot(pick_ref[...], d_rows).astype(BF16)
 
 
 def beside(parts):
@@ -235,7 +239,7 @@
     return lax.ppermute(value, axis, [(i, partner(i, step, count)) for i in range(count)])
 
 
-CORE, FAR, EXCHANGE = 1, 2, 4
+CORE, FAR, EXCHANGE = 1, 2, 6
 NEAR_UNITS = (0, EXCHANGE, CORE, CORE ^ EXCHANGE)
 
 
@@ -307,17 +311,18 @@
         ],
     )(ids, picks, gates, tokens, cotangent)
 
-    own_gate, own_up, own_down = call(
+    own_gate, own_up, own_down, *factors = call(
         weights_kernel,
         2.4,
         [
             jax.ShapeDtypeStruct((width, hidden_width), BF16),
             jax.ShapeDtypeStruct((width, hidden_width), BF16),
             jax.ShapeDtypeStruct((hidden_width, width), BF16),
-        ],
-        in_specs=[ANY] + [HBM] * 3,
+        ]
+        + [jax.ShapeDtypeStruct((tok_rows, rows), BF16)] * 4,
+        in_specs=[NEAR] * 2 + [HBM] * 3,
         scratch_shapes=[pltpu.SemaphoreType.DMA((3,))],
-    )(gsel, w_gate, w_up, w_down)
+    )(sel, gsel, w_gate, w_up, w_down)
 
     came = [sends[0]] + [swap(sends[s], "expert", experts, s) for s in range(1, experts)]
     d_out = call(
@@ -337,15 +342,15 @@
     else:
         parts = [jax.ShapeDtypeStruct((hidden_width, rows), BF16)]
     chunk = 256 if hidden_width % 256 == 0 else hidden_width
-    factors = [jax.ShapeDtypeStruct((rows, hidden_width), t) for t in (BF16, F32, F32)]
+    kept = [jax.ShapeDtypeStruct((rows, hidden_width), t) for t in (BF16, F32, F32)]
     *hts, hidden, d_gate, silu = call(
         functools.partial(forward_kernel, experts, chunk, gathered_units if short else all_units),
         0.9,
-        parts + factors,
+        parts + kept,
         in_specs=[ANY] + [NEAR] * (experts + 2),
         scratch_shapes=[pltpu.VMEM((rows, width), BF16), pltpu.VMEM((hidden_width, rows), BF16)],
     )(d_out, *came, own_gate, own_up)
-    own_result, *results = call(
+    own_result, near_result, *results = call(
         functools.partial(backward_kernel, experts, chunk),
         2.6,
         [block] * experts,
@@ -360,15 +365,16 @@
         keep, give = grad_by_rows(hts, d_out, own_result, groups)
         grad = keep + swap(give, "dp", groups, EXCHANGE).astype(F32)
         results = call(
-            functools.partial(release_kernel, experts - 1),
+            functools.partial(release_kernel, experts - 2),
             9.0,
-            [block] * (experts - 1),
-            in_specs=[ANY] + [NEAR] * (experts - 1),
+            [block] * (experts - 2),
+            in_specs=[ANY] + [NEAR] * (experts - 2),
         )(give, *results)
     else:
         grad = grad_by_sums(hts, d_out, groups)
 
     pairs = experts & (experts - 1) == 0
+    results = [near_result, *results]
     home = [own_result] + [
         swap(results[s - 1], "expert", experts, s if pairs else experts - s) for s in range(1, experts)
     ]
@@ -376,7 +382,7 @@
         functools.partial(combine_kernel, experts),
         0.1,
         [jax.ShapeDtypeStruct((tok_rows, width), BF16)] * 2,
-    )(sel, gsel, *home)
+    )(*factors, *home)
     return layer_out, grad_tokens, grad[None]
 
 

time: 34.8 us -> 34 us (0.977)
  waiting for transfers between devices: 10.9 us -> 8.66 us
  starting transfers between devices: 13 us -> 14.5 us
    ppermute x10, waiting for transfers between devices: 10.9 us -> 8.66 us  [swap(): lax.ppermute(value, axis, [(i, partner(i, step, count)) for i in range(co...]
    ppermute x10, starting transfers between devices: 13 us -> 14.5 us  [swap(): lax.ppermute(value, axis, [(i, partner(i, step, count)) for i in range(co...]
  transfers between devices with their start and end apart: 10 -> 10, of which waited for: 7 -> 5; matrix products, arithmetic and copies ran while one was open for 0% -> 0% of each run, Pallas kernels for 21% -> 22%
where the time goes in v4:
time: 34 us; the launch traced here: 33.8 us
  starting transfers between devices  14.5 us (43%)
  Pallas kernels  9.14 us (27%)
  waiting for transfers between devices  8.66 us (25%)
  other arithmetic  0.79 us (2%)
  between operations  0.7 us (2%)
    ppermute x10, starting transfers between devices, swap(): lax.ppermute(value, axis, [(i, partner(i, step, count)) for i in range(co...  14.5 us
    ppermute x10, waiting for transfers between devices, swap(): lax.ppermute(value, axis, [(i, partner(i, step, count)) for i in range(co...  8.66 us
    pallas_call x1, Pallas kernels, on_device(): call(functools.partial(backward_kernel, experts, chunk), 2.6, [block] * e...  2.61 us
    pallas_call x1, Pallas kernels, on_device(): call(weights_kernel, 2.4, [jax.ShapeDtypeStruct((width, hidden_width), BF...  2.38 us
    pallas_call x1, Pallas kernels, on_device(): call(functools.partial(route_kernel, experts, choices), 1.4, [block] * ex...  1.46 us
    pallas_call x1, Pallas kernels, on_device(): call(functools.partial(combine_kernel, experts), 0.1, [jax.ShapeDtypeStru...  1.14 us
    pallas_call x1, Pallas kernels, on_device(): call(functools.partial(forward_kernel, experts, chunk, gathered_units if...  0.88 us
    broadcast_in_dim x1, other arithmetic, on_device(): return (layer_out, grad_tokens, grad[None])  0.79 us
  transfers between devices with their start and end apart: 10, of which 5 were waited for; matrix products, arithmetic and copies ran while one was open for 0% of the time, Pallas kernels for 22%

profile of v4, /device:TPU:0, one launch (start us, length us, event | category | flops | bytes accessed | tf_op | source)
XLA Modules:
  0.0 33.8 jit_solution(13261594185182992031)
XLA Ops:
  0.6 1.5 %shard_map.103 = (bf16[24,2048]{1,0:T(8,128)(2,1)S(1)}, bf16[24,2048]{1,0:T(8,128)(2,1)S(1)}, bf16[24,2048]{1,0:T(8,128)(2,1)S(1)}, bf16[24,2048]{1,0:T(8,128)(2...) custom-call(s32[6,128]{1,0:T(8,128)} %bitcast.5, s32[6,128]{1,0:T(8,128)} %bitcast.6, f32[6,128]{1,0:T(8,128)} %bitcast.7, ...), custom_call_target="tpu_custom_call" | custom-call | flops 1400000000 | bytes 4200000 | tf_op jit(solution)/shard_map/pallas_call | solution.py:299
  2.1 3.0 %collective-permute-start = (bf16[24,2048]{1,0:T(8,128)(2,1)S(1)}, bf16[24,2048]{1,0:T(8,128)(2,1)S(1)}, u32[]{:S(2)}, u32[]{:S(2)}) collective-permute-start(bf16[24,2048]{1,0:T(8,128)(2,1)S(1)} %get-tuple-element.38), channel_id=1, source_target_pairs={{0,8},{8,0},{16,24},{24,16},{1,9},{9,1},{17,25},{25,17},{2,10},{10... | collective-permute-start | bytes 294920 | tf_op jit(solution)/shard_map/ppermute | solution.py:239
  5.1 1.5 %collective-permute-start.1 = (bf16[24,2048]{1,0:T(8,128)(2,1)S(1)}, bf16[24,2048]{1,0:T(8,128)(2,1)S(1)}, u32[]{:S(2)}, u32[]{:S(2)}) collective-permute-start(bf16[24,2048]{1,0:T(8,128)(2,1)S(1)} %get-tuple-element.39), channel_id=1, source_target_pairs={{0,16},{8,24},{16,0},{24,8},{1,17},{9,25},{17,1},{25,9},{2,18},{10... | collective-permute-start | bytes 294920 | tf_op jit(solution)/shard_map/ppermute | solution.py:239
  6.6 0.0 collective-permute-start.2
  6.6 2.4 %shard_map.104 = (bf16[1024,768]{1,0:T(8,128)(2,1)S(1)}, bf16[1024,768]{1,0:T(8,128)(2,1)S(1)}, bf16[768,1024]{1,0:T(8,128)(2,1)S(1)}, bf16[128,96]{1,0:T(8,128)...) custom-call(f32[96,128]{1,0:T(8,128)S(1)} %get-tuple-element.31.sel_ref, ...), custom_call_target="tpu_custom_call" | custom-call | flops 2400000000 | bytes 7200000 | tf_op jit(solution)/shard_map/pallas_call | solution.py:314
  9.0 0.0 collective-permute-done.refs_1_
  9.0 1.7 %collective-permute-done.1.refs_2_ = bf16[24,2048]{1,0:T(8,128)(2,1)S(1)} collective-permute-done((bf16[24,2048]{1,0:T(8,128)(2,1)S(1)}, bf16[24,2048]{1,0:T(8,128)(2,1)S(1)}, u32[]{:S(2)}, u32[]{:S(2)}) %collective-permute-start.1) | collective-permute-done | bytes 98336 | tf_op jit(solution)/shard_map/ppermute | solution.py:239
  10.8 1.4 %collective-permute-done.2.refs_3_ = bf16[24,2048]{1,0:T(8,128)(2,1)S(1)} collective-permute-done((bf16[24,2048]{1,0:T(8,128)(2,1)S(1)}, bf16[24,2048]{1,0:T(8,128)(2,1)S(1)}, u32[]{:S(2)}, u32[]{:S(2)}) %collective-permute-start.2) | collective-permute-done | bytes 98336 | tf_op jit(solution)/shard_map/ppermute | solution.py:239
  12.2 1.6 %collective-permute-start.5 = (bf16[96,1024]{1,0:T(8,128)(2,1)S(1)}, bf16[96,1024]{1,0:T(8,128)(2,1)S(1)}, u32[]{:S(2)}, u32[]{:S(2)}) collective-permute-start(bf16[96,1024]{1,0:T(8,128)(2,1)S(1)} %shard_map.105.after.d_ref), channel_id=1, source_target_pairs={{0,2},{1,3},{2,0},{3,1},{4,6},{5,7},{6,4},{7,5},{8,10},{9,11},{10,... | collective-permute-start | bytes 589832 | tf_op jit(solution)/shard_map/ppermute | solution.py:239
  13.8 0.9 %shard_map.106 = (bf16[384,96]{1,0:T(8,128)(2,1)S(1)}, bf16[288,128]{1,0:T(8,128)(2,1)S(1)}, bf16[96,768]{1,0:T(8,128)(2,1)S(1)}, f32[96,768]{1,0:T(8,128)S(1)}, f32[96,768]{1,0:T(8,128)S(1)}) custom-call(bf16[96,1024]{1,0:T(8,128)(2,1)S(1)} %shard_map.105.after.d_ref, bf16[24,2048]{1,0:T(8,128)(2,1)S(1)} %get-tuple-element.37.refs_0_, ...), custom_call_target="tpu_custom_call" | custom-call | flops 900000000 | bytes 2700000 | tf_op jit(solution)/shard_map/pallas_call | solution.py:346
  14.7 0.5 %collective-permute-start.4 = (bf16[288,128]{1,0:T(8,128)(2,1)S(1)}, bf16[288,128]{1,0:T(8,128)(2,1)S(1)}, u32[]{:S(2)}, u32[]{:S(2)}) collective-permute-start(bf16[288,128]{1,0:T(8,128)(2,1)S(1)} %get-tuple-element.50), channel_id=1, source_target_pairs={{0,2},{1,3},{2,0},{3,1},{4,6},{5,7},{6,4},{7,5},{8,10},{9,11},{10,... | collective-permute-start | bytes 221192 | tf_op jit(solution)/shard_map/ppermute | solution.py:239
  15.2 2.6 %shard_map.107 = (bf16[24,2048]{1,0:T(8,128)(2,1)S(1)}, bf16[24,2048]{1,0:T(8,128)(2,1)S(1)}, bf16[24,2048]{1,0:T(8,128)(2,1)S(1)}, bf16[24,2048]{1,0:T(8,128)(2,1)S(1)}) custom-call(bf16[24,2048]{1,0:T(8,128)(2,1)S(1)} %get-tuple-element.37.refs_0_, bf16[24,2048]{1,0:T(8,128)(2,1)S(1)} %collective-permute-done.refs_1_, ...), custom_call_target="tpu_custom_call" | custom-call | flops 2600000000 | bytes 7800000 | tf_op jit(solution)/shard_map/pallas_call | solution.py:353
  17.8 1.3 %collective-permute-done.4.far_ht = bf16[288,128]{1,0:T(8,128)(2,1)S(1)} collective-permute-done((bf16[288,128]{1,0:T(8,128)(2,1)S(1)}, bf16[288,128]{1,0:T(8,128)(2,1)S(1)}, u32[]{:S(2)}, u32[]{:S(2)}) %collective-permute-start.4) | collective-permute-done | bytes 73760 | tf_op jit(solution)/shard_map/ppermute | solution.py:239
  19.1 0.0 collective-permute-done.5.far_ref
  19.1 0.1 shard_map.108.own_ref
  19.2 0.1 collective-permute-start.6
  19.3 1.3 %collective-permute-start.3 = (bf16[24,2048]{1,0:T(8,128)(2,1)S(1)}, bf16[24,2048]{1,0:T(8,128)(2,1)S(1)}, u32[]{:S(2)}, u32[]{:S(2)}) collective-permute-start(bf16[24,2048]{1,0:T(8,128)(2,1)S(1)} %get-tuple-element.48), channel_id=1, source_target_pairs={{0,8},{8,0},{16,24},{24,16},{1,9},{9,1},{17,25},{25,17},{2,10},{10... | collective-permute-start | bytes 294920 | tf_op jit(solution)/shard_map/ppermute | solution.py:239
  20.6 0.5 %collective-permute-done.6.pair_ref = bf16[240,1024]{1,0:T(8,128)(2,1)S(1)} collective-permute-done((bf16[240,1024]{1,0:T(8,128)(2,1)S(1)}, bf16[240,1024]{1,0:T(8,128)(2,1)S(1)}, u32[]{:S(2)}, u32[]{:S(2)}) %collective-permute-start.6) | collective-permute-done | bytes 491552 | tf_op jit(solution)/shard_map/ppermute | solution.py:239
  21.1 0.5 %shard_map.109 = (f32[96,1024]{1,0:T(8,128)S(1)}, bf16[96,1024]{1,0:T(8,128)(2,1)S(1)}) custom-call(bf16[384,96]{1,0:T(8,128)(2,1)S(1)} %get-tuple-element.49.near_ht, bf16[288,128]{1,0:T(8,128)(2,1)S(1)} %collective-permute-done.4.far_ht, bf16[240,1024]{1,0:T(8,128)(2,1)S(1)} %shard_map.108.own_ref, bf16[240,1024]{1,0:T(8,128)(2,1)S(1)} %collective-permute-done.6.pair_ref), custom_call_target="tpu_custom_call" | custom-call | flops 600000000 | bytes 1800000 | tf_op jit(solution)/shard_map/pallas_call | solution.py:269
  21.7 3.4 %collective-permute-start.9 = (bf16[96,1024]{1,0:T(8,128)(2,1)S(1)}, bf16[96,1024]{1,0:T(8,128)(2,1)S(1)}, u32[]{:S(2)}, u32[]{:S(2)}) collective-permute-start(bf16[96,1024]{1,0:T(8,128)(2,1)S(1)} %get-tuple-element.51.after), channel_id=1, source_target_pairs={{0,6},{1,7},{2,4},{3,5},{4,2},{5,3},{6,0},{7,1},{8,14},{9,15},{10,... | collective-permute-start | bytes 589832 | tf_op jit(solution)/shard_map/ppermute | solution.py:239
  25.1 0.8 %collective-permute-start.7 = (bf16[24,2048]{1,0:T(8,128)(2,1)S(1)}, bf16[24,2048]{1,0:T(8,128)(2,1)S(1)}, u32[]{:S(2)}, u32[]{:S(2)}) collective-permute-start(bf16[24,2048]{1,0:T(8,128)(2,1)S(1)} %get-tuple-element.54), channel_id=1, source_target_pairs={{0,16},{8,24},{16,0},{24,8},{1,17},{9,25},{17,1},{25,9},{2,18},{10... | collective-permute-start | bytes 294920 | tf_op jit(solution)/shard_map/ppermute | solution.py:239
  25.9 2.2 %collective-permute-start.8 = (bf16[24,2048]{1,0:T(8,128)(2,1)S(1)}, bf16[24,2048]{1,0:T(8,128)(2,1)S(1)}, u32[]{:S(2)}, u32[]{:S(2)}) collective-permute-start(bf16[24,2048]{1,0:T(8,128)(2,1)S(1)} %get-tuple-element.55), channel_id=1, source_target_pairs={{0,24},{8,16},{16,8},{24,0},{1,25},{9,17},{17,9},{25,1},{2,26},{10... | collective-permute-start | bytes 294920 | tf_op jit(solution)/shard_map/ppermute | solution.py:239
  28.2 0.0 collective-permute-done.3.refs_1_
  28.2 3.7 %collective-permute-done.7.refs_2_ = bf16[24,2048]{1,0:T(8,128)(2,1)S(1)} collective-permute-done((bf16[24,2048]{1,0:T(8,128)(2,1)S(1)}, bf16[24,2048]{1,0:T(8,128)(2,1)S(1)}, u32[]{:S(2)}, u32[]{:S(2)}) %collective-permute-start.7) | collective-permute-done | bytes 98336 | tf_op jit(solution)/shard_map/ppermute | solution.py:239
  31.9 0.0 collective-permute-done.8.refs_3_
  31.9 1.1 %shard_map.111 = (bf16[128,1024]{1,0:T(8,128)(2,1)}, bf16[128,1024]{1,0:T(8,128)(2,1)}) custom-call(bf16[128,96]{1,0:T(8,128)(2,1)S(1)} %get-tuple-element.33.pick_ref, bf16[128,96]{1,0:T(8,128)(2,1)S(1)} %get-tuple-element.34.high_ref, bf16[128,96]{1,0:T(8,128)(2,1)S(1)} %get-tuple-element.35.mid_ref, bf16[128,96]{1,0:T(8,128)(2,1)S(1)} %get-tuple-element.36.low_ref, ...), custom_call_target="tpu_custom_call" | custom-call | flops 100000000 | bytes 300000 | tf_op jit(solution)/shard_map/pallas_call | solution.py:381
  33.0 0.0 collective-permute-done.9
  33.0 0.8 %add_bitcast_fusion = f32[1,96,1024]{2,1,0:T(8,128)} fusion(f32[96,1024]{1,0:T(8,128)S(1)} %get-tuple-element.58, bf16[96,1024]{1,0:T(8,128)(2,1)S(1)} %collective-permute-done.9), kind=kLoop, calls=%fused_computation | loop fusion | flops 196608 | bytes 983040 | tf_op jit(solution)/shard_map/broadcast_in_dim | solution.py:386
  (2 shorter events, 0.0 us)
Async XLA Ops:
  2.1 6.9 %collective-permute-start = (bf16[24,2048]{1,0:T(8,128)(2,1)S(1)}, bf16[24,2048]{1,0:T(8,128)(2,1)S(1)}, u32[]{:S(2)}, u32[]{:S(2)}) collective-permute-start(bf16[24,2048]{1,0:T(8,128)(2,1)S(1)} %get-tuple-element.38), channel_id=1, source_target_pairs={{0,8},{8,0},{16,24},{24,16},{1,9},{9,1},{17,25},{25,17},{2,10},{10... | collective-permute-start | bytes 294920 | tf_op jit(solution)/shard_map/ppermute | solution.py:239
  5.1 5.7 %collective-permute-start.1 = (bf16[24,2048]{1,0:T(8,128)(2,1)S(1)}, bf16[24,2048]{1,0:T(8,128)(2,1)S(1)}, u32[]{:S(2)}, u32[]{:S(2)}) collective-permute-start(bf16[24,2048]{1,0:T(8,128)(2,1)S(1)} %get-tuple-element.39), channel_id=1, source_target_pairs={{0,16},{8,24},{16,0},{24,8},{1,17},{9,25},{17,1},{25,9},{2,18},{10... | collective-permute-start | bytes 294920 | tf_op jit(solution)/shard_map/ppermute | solution.py:239
  6.6 5.5 %collective-permute-start.2 = (bf16[24,2048]{1,0:T(8,128)(2,1)S(1)}, bf16[24,2048]{1,0:T(8,128)(2,1)S(1)}, u32[]{:S(2)}, u32[]{:S(2)}) collective-permute-start(bf16[24,2048]{1,0:T(8,128)(2,1)S(1)} %get-tuple-element.40), channel_id=1, source_target_pairs={{0,24},{8,16},{16,8},{24,0},{1,25},{9,17},{17,9},{25,1},{2,26},{10... | collective-permute-start | bytes 294920 | tf_op jit(solution)/shard_map/ppermute | solution.py:239
  12.2 6.9 %collective-permute-start.5 = (bf16[96,1024]{1,0:T(8,128)(2,1)S(1)}, bf16[96,1024]{1,0:T(8,128)(2,1)S(1)}, u32[]{:S(2)}, u32[]{:S(2)}) collective-permute-start(bf16[96,1024]{1,0:T(8,128)(2,1)S(1)} %shard_map.105.after.d_ref), channel_id=1, source_target_pairs={{0,2},{1,3},{2,0},{3,1},{4,6},{5,7},{6,4},{7,5},{8,10},{9,11},{10,... | collective-permute-start | bytes 589832 | tf_op jit(solution)/shard_map/ppermute | solution.py:239
  14.7 4.4 %collective-permute-start.4 = (bf16[288,128]{1,0:T(8,128)(2,1)S(1)}, bf16[288,128]{1,0:T(8,128)(2,1)S(1)}, u32[]{:S(2)}, u32[]{:S(2)}) collective-permute-start(bf16[288,128]{1,0:T(8,128)(2,1)S(1)} %get-tuple-element.50), channel_id=1, source_target_pairs={{0,2},{1,3},{2,0},{3,1},{4,6},{5,7},{6,4},{7,5},{8,10},{9,11},{10,... | collective-permute-start | bytes 221192 | tf_op jit(solution)/shard_map/ppermute | solution.py:239
  19.2 1.9 %collective-permute-start.6 = (bf16[240,1024]{1,0:T(8,128)(2,1)S(1)}, bf16[240,1024]{1,0:T(8,128)(2,1)S(1)}, u32[]{:S(2)}, u32[]{:S(2)}) collective-permute-start(bf16[240,1024]{1,0:T(8,128)(2,1)S(1)} %shard_map.108.own_ref), channel_id=1, source_target_pairs={{0,1},{1,0},{2,3},{3,2},{4,5},{5,4},{6,7},{7,6},{8,9},{9,8},{10,11... | collective-permute-start | bytes 1474568 | tf_op jit(solution)/shard_map/ppermute | solution.py:239
  19.3 8.9 %collective-permute-start.3 = (bf16[24,2048]{1,0:T(8,128)(2,1)S(1)}, bf16[24,2048]{1,0:T(8,128)(2,1)S(1)}, u32[]{:S(2)}, u32[]{:S(2)}) collective-permute-start(bf16[24,2048]{1,0:T(8,128)(2,1)S(1)} %get-tuple-element.48), channel_id=1, source_target_pairs={{0,8},{8,0},{16,24},{24,16},{1,9},{9,1},{17,25},{25,17},{2,10},{10... | collective-permute-start | bytes 294920 | tf_op jit(solution)/shard_map/ppermute | solution.py:239
  21.7 11.4 %collective-permute-start.9 = (bf16[96,1024]{1,0:T(8,128)(2,1)S(1)}, bf16[96,1024]{1,0:T(8,128)(2,1)S(1)}, u32[]{:S(2)}, u32[]{:S(2)}) collective-permute-start(bf16[96,1024]{1,0:T(8,128)(2,1)S(1)} %get-tuple-element.51.after), channel_id=1, source_target_pairs={{0,6},{1,7},{2,4},{3,5},{4,2},{5,3},{6,0},{7,1},{8,14},{9,15},{10,... | collective-permute-start | bytes 589832 | tf_op jit(solution)/shard_map/ppermute | solution.py:239
  25.1 6.8 %collective-permute-start.7 = (bf16[24,2048]{1,0:T(8,128)(2,1)S(1)}, bf16[24,2048]{1,0:T(8,128)(2,1)S(1)}, u32[]{:S(2)}, u32[]{:S(2)}) collective-permute-start(bf16[24,2048]{1,0:T(8,128)(2,1)S(1)} %get-tuple-element.54), channel_id=1, source_target_pairs={{0,16},{8,24},{16,0},{24,8},{1,17},{9,25},{17,1},{25,9},{2,18},{10... | collective-permute-start | bytes 294920 | tf_op jit(solution)/shard_map/ppermute | solution.py:239
  25.9 6.0 %collective-permute-start.8 = (bf16[24,2048]{1,0:T(8,128)(2,1)S(1)}, bf16[24,2048]{1,0:T(8,128)(2,1)S(1)}, u32[]{:S(2)}, u32[]{:S(2)}) collective-permute-start(bf16[24,2048]{1,0:T(8,128)(2,1)S(1)} %get-tuple-element.55), channel_id=1, source_target_pairs={{0,24},{8,16},{16,8},{24,0},{1,25},{9,17},{17,9},{25,1},{2,26},{10... | collective-permute-start | bytes 294920 | tf_op jit(solution)/shard_map/ppermute | solution.py:239

commit v5 on v4

--- a/solution.py
+++ b/solution.py
@@ -239,6 +239,8 @@
     return lax.ppermute(value, axis, [(i, partner(i, step, count)) for i in range(count)])
 
 
+HELD = (2,)
+
 CORE, FAR, EXCHANGE = 1, 2, 6
 NEAR_UNITS = (0, EXCHANGE, CORE, CORE ^ EXCHANGE)
 
@@ -350,7 +352,7 @@
         in_specs=[ANY] + [NEAR] * (experts + 2),
         scratch_shapes=[pltpu.VMEM((rows, width), BF16), pltpu.VMEM((hidden_width, rows), BF16)],
     )(d_out, *came, own_gate, own_up)
-    own_result, near_result, *results = call(
+    results = list(call(
         functools.partial(backward_kernel, experts, chunk),
         2.6,
         [block] * experts,
@@ -359,24 +361,25 @@
             pltpu.VMEM((rows, width), F32),
             pltpu.VMEM((rows, width), F32),
         ],
-    )(*came, own_gate, own_up, own_down, hidden, d_gate, silu)
+    )(*came, own_gate, own_up, own_down, hidden, d_gate, silu))
 
     if short:
-        keep, give = grad_by_rows(hts, d_out, own_result, groups)
+        keep, give = grad_by_rows(hts, d_out, results[0], groups)
         grad = keep + swap(give, "dp", groups, EXCHANGE).astype(F32)
-        results = call(
-            functools.partial(release_kernel, experts - 2),
+        freed = call(
+            functools.partial(release_kernel, len(HELD)),
             9.0,
-            [block] * (experts - 2),
-            in_specs=[ANY] + [NEAR] * (experts - 2),
-        )(give, *results)
+            [block] * len(HELD),
+            in_specs=[ANY] + [NEAR] * len(HELD),
+        )(give, *(results[s] for s in HELD))
+        for step, value in zip(HELD, freed):
+            results[step] = value
     else:
         grad = grad_by_sums(hts, d_out, groups)
 
     pairs = experts & (experts - 1) == 0
-    results = [near_result, *results]
-    home = [own_result] + [
-        swap(results[s - 1], "expert", experts, s if pairs else experts - s) for s in range(1, experts)
+    home = [results[0]] + [
+        swap(results[s], "expert", experts, s if pairs else experts - s) for s in range(1, experts)
     ]
     layer_out, grad_tokens = call(
         functools.partial(combine_kernel, experts),

time: 34 us -> 32.8 us (0.965); the launches traced: 33.8 us -> 32.2 us
  waiting for transfers between devices: 8.66 us -> 7.74 us
  starting transfers between devices: 14.5 us -> 13.8 us
    ppermute x10, waiting for transfers between devices: 8.66 us -> 7.74 us  [swap(): lax.ppermute(value, axis, [(i, partner(i, step, count)) for i in range(co...]
    ppermute x10, starting transfers between devices: 14.5 us -> 13.8 us  [swap(): lax.ppermute(value, axis, [(i, partner(i, step, count)) for i in range(co...]
  transfers between devices with their start and end apart: 10 -> 10, of which waited for: 5 -> 5; matrix products, arithmetic and copies ran while one was open for 0% -> 0% of each run, Pallas kernels for 22% -> 23%
where the time goes in v5:
time: 32.8 us; the launch traced here: 32.2 us
  starting transfers between devices  13.8 us (42%)
  Pallas kernels  9.13 us (28%)
  waiting for transfers between devices  7.74 us (24%)
  other arithmetic  0.79 us (2%)
  between operations  0.7 us (2%)
    ppermute x10, starting transfers between devices, swap(): lax.ppermute(value, axis, [(i, partner(i, step, count)) for i in range(co...  13.8 us
    ppermute x10, waiting for transfers between devices, swap(): lax.ppermute(value, axis, [(i, partner(i, step, count)) for i in range(co...  7.74 us
    pallas_call x1, Pallas kernels, on_device(): call(functools.partial(backward_kernel, experts, chunk), 2.6, [block] * e...  2.61 us
    pallas_call x1, Pallas kernels, on_device(): call(weights_kernel, 2.4, [jax.ShapeDtypeStruct((width, hidden_width), BF...  2.38 us
    pallas_call x1, Pallas kernels, on_device(): call(functools.partial(route_kernel, experts, choices), 1.4, [block] * ex...  1.46 us
    pallas_call x1, Pallas kernels, on_device(): call(functools.partial(combine_kernel, experts), 0.1, [jax.ShapeDtypeStru...  1.14 us
    pallas_call x1, Pallas kernels, on_device(): call(functools.partial(forward_kernel, experts, chunk, gathered_units if...  0.88 us
    broadcast_in_dim x1, other arithmetic, on_device(): return (layer_out, grad_tokens, grad[None])  0.79 us
  transfers between devices with their start and end apart: 10, of which 5 were waited for; matrix products, arithmetic and copies ran while one was open for 0% of the time, Pallas kernels for 23%

profile of v5, /device:TPU:0, one launch (start us, length us, event | category | flops | bytes accessed | tf_op | source)
XLA Modules:
  0.0 32.2 jit_solution(17666587399997455128)
XLA Ops:
  0.6 1.5 %shard_map.103 = (bf16[24,2048]{1,0:T(8,128)(2,1)S(1)}, bf16[24,2048]{1,0:T(8,128)(2,1)S(1)}, bf16[24,2048]{1,0:T(8,128)(2,1)S(1)}, bf16[24,2048]{1,0:T(8,128)(2...) custom-call(s32[6,128]{1,0:T(8,128)} %bitcast.5, s32[6,128]{1,0:T(8,128)} %bitcast.6, f32[6,128]{1,0:T(8,128)} %bitcast.7, ...), custom_call_target="tpu_custom_call" | custom-call | flops 1400000000 | bytes 4200000 | tf_op jit(solution)/shard_map/pallas_call | solution.py:301
  2.1 3.0 %collective-permute-start = (bf16[24,2048]{1,0:T(8,128)(2,1)S(1)}, bf16[24,2048]{1,0:T(8,128)(2,1)S(1)}, u32[]{:S(2)}, u32[]{:S(2)}) collective-permute-start(bf16[24,2048]{1,0:T(8,128)(2,1)S(1)} %get-tuple-element.36), channel_id=1, source_target_pairs={{0,8},{8,0},{16,24},{24,16},{1,9},{9,1},{17,25},{25,17},{2,10},{10... | collective-permute-start | bytes 294920 | tf_op jit(solution)/shard_map/ppermute | solution.py:239
  5.1 1.5 %collective-permute-start.1 = (bf16[24,2048]{1,0:T(8,128)(2,1)S(1)}, bf16[24,2048]{1,0:T(8,128)(2,1)S(1)}, u32[]{:S(2)}, u32[]{:S(2)}) collective-permute-start(bf16[24,2048]{1,0:T(8,128)(2,1)S(1)} %get-tuple-element.37), channel_id=1, source_target_pairs={{0,16},{8,24},{16,0},{24,8},{1,17},{9,25},{17,1},{25,9},{2,18},{10... | collective-permute-start | bytes 294920 | tf_op jit(solution)/shard_map/ppermute | solution.py:239
  6.6 0.0 collective-permute-start.2
  6.6 2.4 %shard_map.104 = (bf16[1024,768]{1,0:T(8,128)(2,1)S(1)}, bf16[1024,768]{1,0:T(8,128)(2,1)S(1)}, bf16[768,1024]{1,0:T(8,128)(2,1)S(1)}, bf16[128,96]{1,0:T(8,128)...) custom-call(f32[96,128]{1,0:T(8,128)S(1)} %get-tuple-element.29.sel_ref, ...), custom_call_target="tpu_custom_call" | custom-call | flops 2400000000 | bytes 7200000 | tf_op jit(solution)/shard_map/pallas_call | solution.py:316
  9.0 0.0 collective-permute-done.refs_1_
  9.0 1.7 %collective-permute-done.1.refs_2_ = bf16[24,2048]{1,0:T(8,128)(2,1)S(1)} collective-permute-done((bf16[24,2048]{1,0:T(8,128)(2,1)S(1)}, bf16[24,2048]{1,0:T(8,128)(2,1)S(1)}, u32[]{:S(2)}, u32[]{:S(2)}) %collective-permute-start.1) | collective-permute-done | bytes 98336 | tf_op jit(solution)/shard_map/ppermute | solution.py:239
  10.8 1.4 %collective-permute-done.2.refs_3_ = bf16[24,2048]{1,0:T(8,128)(2,1)S(1)} collective-permute-done((bf16[24,2048]{1,0:T(8,128)(2,1)S(1)}, bf16[24,2048]{1,0:T(8,128)(2,1)S(1)}, u32[]{:S(2)}, u32[]{:S(2)}) %collective-permute-start.2) | collective-permute-done | bytes 98336 | tf_op jit(solution)/shard_map/ppermute | solution.py:239
  12.2 1.6 %collective-permute-start.5 = (bf16[96,1024]{1,0:T(8,128)(2,1)S(1)}, bf16[96,1024]{1,0:T(8,128)(2,1)S(1)}, u32[]{:S(2)}, u32[]{:S(2)}) collective-permute-start(bf16[96,1024]{1,0:T(8,128)(2,1)S(1)} %shard_map.105.after.d_ref), channel_id=1, source_target_pairs={{0,2},{1,3},{2,0},{3,1},{4,6},{5,7},{6,4},{7,5},{8,10},{9,11},{10,... | collective-permute-start | bytes 589832 | tf_op jit(solution)/shard_map/ppermute | solution.py:239
  13.8 0.9 %shard_map.106 = (bf16[384,96]{1,0:T(8,128)(2,1)S(1)}, bf16[288,128]{1,0:T(8,128)(2,1)S(1)}, bf16[96,768]{1,0:T(8,128)(2,1)S(1)}, f32[96,768]{1,0:T(8,128)S(1)}, f32[96,768]{1,0:T(8,128)S(1)}) custom-call(bf16[96,1024]{1,0:T(8,128)(2,1)S(1)} %shard_map.105.after.d_ref, bf16[24,2048]{1,0:T(8,128)(2,1)S(1)} %get-tuple-element.35.refs_0_, ...), custom_call_target="tpu_custom_call" | custom-call | flops 900000000 | bytes 2700000 | tf_op jit(solution)/shard_map/pallas_call | solution.py:348
  14.7 0.5 %collective-permute-start.4 = (bf16[288,128]{1,0:T(8,128)(2,1)S(1)}, bf16[288,128]{1,0:T(8,128)(2,1)S(1)}, u32[]{:S(2)}, u32[]{:S(2)}) collective-permute-start(bf16[288,128]{1,0:T(8,128)(2,1)S(1)} %get-tuple-element.48), channel_id=1, source_target_pairs={{0,2},{1,3},{2,0},{3,1},{4,6},{5,7},{6,4},{7,5},{8,10},{9,11},{10,... | collective-permute-start | bytes 221192 | tf_op jit(solution)/shard_map/ppermute | solution.py:239
  15.2 2.6 %shard_map.107 = (bf16[24,2048]{1,0:T(8,128)(2,1)S(1)}, bf16[24,2048]{1,0:T(8,128)(2,1)S(1)}, bf16[24,2048]{1,0:T(8,128)(2,1)S(1)}, bf16[24,2048]{1,0:T(8,128)(2,1)S(1)}) custom-call(bf16[24,2048]{1,0:T(8,128)(2,1)S(1)} %get-tuple-element.35.refs_0_, bf16[24,2048]{1,0:T(8,128)(2,1)S(1)} %collective-permute-done.refs_1_, ...), custom_call_target="tpu_custom_call" | custom-call | flops 2600000000 | bytes 7800000 | tf_op jit(solution)/shard_map/pallas_call | solution.py:355
  17.8 1.3 %collective-permute-done.4.far_ht = bf16[288,128]{1,0:T(8,128)(2,1)S(1)} collective-permute-done((bf16[288,128]{1,0:T(8,128)(2,1)S(1)}, bf16[288,128]{1,0:T(8,128)(2,1)S(1)}, u32[]{:S(2)}, u32[]{:S(2)}) %collective-permute-start.4) | collective-permute-done | bytes 73760 | tf_op jit(solution)/shard_map/ppermute | solution.py:239
  19.1 0.0 collective-permute-done.5.far_ref
  19.1 0.1 shard_map.108.own_ref
  19.2 0.1 collective-permute-start.6
  19.3 1.3 %collective-permute-start.3 = (bf16[24,2048]{1,0:T(8,128)(2,1)S(1)}, bf16[24,2048]{1,0:T(8,128)(2,1)S(1)}, u32[]{:S(2)}, u32[]{:S(2)}) collective-permute-start(bf16[24,2048]{1,0:T(8,128)(2,1)S(1)} %get-tuple-element.46), channel_id=1, source_target_pairs={{0,8},{8,0},{16,24},{24,16},{1,9},{9,1},{17,25},{25,17},{2,10},{10... | collective-permute-start | bytes 294920 | tf_op jit(solution)/shard_map/ppermute | solution.py:239
  20.6 1.1 %collective-permute-start.8 = (bf16[24,2048]{1,0:T(8,128)(2,1)S(1)}, bf16[24,2048]{1,0:T(8,128)(2,1)S(1)}, u32[]{:S(2)}, u32[]{:S(2)}) collective-permute-start(bf16[24,2048]{1,0:T(8,128)(2,1)S(1)} %get-tuple-element.51), channel_id=1, source_target_pairs={{0,24},{8,16},{16,8},{24,0},{1,25},{9,17},{17,9},{25,1},{2,26},{10... | collective-permute-start | bytes 294920 | tf_op jit(solution)/shard_map/ppermute | solution.py:239
  21.7 0.0 collective-permute-done.6.pair_ref
  21.7 0.5 %shard_map.109 = (f32[96,1024]{1,0:T(8,128)S(1)}, bf16[96,1024]{1,0:T(8,128)(2,1)S(1)}) custom-call(bf16[384,96]{1,0:T(8,128)(2,1)S(1)} %get-tuple-element.47.near_ht, bf16[288,128]{1,0:T(8,128)(2,1)S(1)} %collective-permute-done.4.far_ht, bf16[240,1024]{1,0:T(8,128)(2,1)S(1)} %shard_map.108.own_ref, bf16[240,1024]{1,0:T(8,128)(2,1)S(1)} %collective-permute-done.6.pair_ref), custom_call_target="tpu_custom_call" | custom-call | flops 600000000 | bytes 1800000 | tf_op jit(solution)/shard_map/pallas_call | solution.py:271
  22.3 3.2 %collective-permute-start.9 = (bf16[96,1024]{1,0:T(8,128)(2,1)S(1)}, bf16[96,1024]{1,0:T(8,128)(2,1)S(1)}, u32[]{:S(2)}, u32[]{:S(2)}) collective-permute-start(bf16[96,1024]{1,0:T(8,128)(2,1)S(1)} %get-tuple-element.49.after), channel_id=1, source_target_pairs={{0,6},{1,7},{2,4},{3,5},{4,2},{5,3},{6,0},{7,1},{8,14},{9,15},{10,... | collective-permute-start | bytes 589832 | tf_op jit(solution)/shard_map/ppermute | solution.py:239
  25.5 1.3 %collective-permute-start.7 = (bf16[24,2048]{1,0:T(8,128)(2,1)S(1)}, bf16[24,2048]{1,0:T(8,128)(2,1)S(1)}, u32[]{:S(2)}, u32[]{:S(2)}) collective-permute-start(bf16[24,2048]{1,0:T(8,128)(2,1)S(1)} %shard_map.110), channel_id=1, source_target_pairs={{0,16},{8,24},{16,0},{24,8},{1,17},{9,25},{17,1},{25,9},{2,18},{10... | collective-permute-start | bytes 294920 | tf_op jit(solution)/shard_map/ppermute | solution.py:239
  26.9 0.0 collective-permute-done.3.refs_1_
  26.9 0.1 collective-permute-done.8.refs_3_
  27.0 3.3 %collective-permute-done.7.refs_2_ = bf16[24,2048]{1,0:T(8,128)(2,1)S(1)} collective-permute-done((bf16[24,2048]{1,0:T(8,128)(2,1)S(1)}, bf16[24,2048]{1,0:T(8,128)(2,1)S(1)}, u32[]{:S(2)}, u32[]{:S(2)}) %collective-permute-start.7) | collective-permute-done | bytes 98336 | tf_op jit(solution)/shard_map/ppermute | solution.py:239
  30.2 1.1 %shard_map.111 = (bf16[128,1024]{1,0:T(8,128)(2,1)}, bf16[128,1024]{1,0:T(8,128)(2,1)}) custom-call(bf16[128,96]{1,0:T(8,128)(2,1)S(1)} %get-tuple-element.31.pick_ref, bf16[128,96]{1,0:T(8,128)(2,1)S(1)} %get-tuple-element.32.high_ref, bf16[128,96]{1,0:T(8,128)(2,1)S(1)} %get-tuple-element.33.mid_ref, bf16[128,96]{1,0:T(8,128)(2,1)S(1)} %get-tuple-element.34.low_ref, ...), custom_call_target="tpu_custom_call" | custom-call | flops 100000000 | bytes 300000 | tf_op jit(solution)/shard_map/pallas_call | solution.py:384
  31.4 0.0 collective-permute-done.9
  31.4 0.8 %add_bitcast_fusion = f32[1,96,1024]{2,1,0:T(8,128)} fusion(f32[96,1024]{1,0:T(8,128)S(1)} %get-tuple-element.54, bf16[96,1024]{1,0:T(8,128)(2,1)S(1)} %collective-permute-done.9), kind=kLoop, calls=%fused_computation | loop fusion | flops 196608 | bytes 983040 | tf_op jit(solution)/shard_map/broadcast_in_dim | solution.py:389
  (2 shorter events, 0.0 us)
Async XLA Ops:
  2.1 6.9 %collective-permute-start = (bf16[24,2048]{1,0:T(8,128)(2,1)S(1)}, bf16[24,2048]{1,0:T(8,128)(2,1)S(1)}, u32[]{:S(2)}, u32[]{:S(2)}) collective-permute-start(bf16[24,2048]{1,0:T(8,128)(2,1)S(1)} %get-tuple-element.36), channel_id=1, source_target_pairs={{0,8},{8,0},{16,24},{24,16},{1,9},{9,1},{17,25},{25,17},{2,10},{10... | collective-permute-start | bytes 294920 | tf_op jit(solution)/shard_map/ppermute | solution.py:239
  5.1 5.7 %collective-permute-start.1 = (bf16[24,2048]{1,0:T(8,128)(2,1)S(1)}, bf16[24,2048]{1,0:T(8,128)(2,1)S(1)}, u32[]{:S(2)}, u32[]{:S(2)}) collective-permute-start(bf16[24,2048]{1,0:T(8,128)(2,1)S(1)} %get-tuple-element.37), channel_id=1, source_target_pairs={{0,16},{8,24},{16,0},{24,8},{1,17},{9,25},{17,1},{25,9},{2,18},{10... | collective-permute-start | bytes 294920 | tf_op jit(solution)/shard_map/ppermute | solution.py:239
  6.6 5.5 %collective-permute-start.2 = (bf16[24,2048]{1,0:T(8,128)(2,1)S(1)}, bf16[24,2048]{1,0:T(8,128)(2,1)S(1)}, u32[]{:S(2)}, u32[]{:S(2)}) collective-permute-start(bf16[24,2048]{1,0:T(8,128)(2,1)S(1)} %get-tuple-element.38), channel_id=1, source_target_pairs={{0,24},{8,16},{16,8},{24,0},{1,25},{9,17},{17,9},{25,1},{2,26},{10... | collective-permute-start | bytes 294920 | tf_op jit(solution)/shard_map/ppermute | solution.py:239
  12.2 6.9 %collective-permute-start.5 = (bf16[96,1024]{1,0:T(8,128)(2,1)S(1)}, bf16[96,1024]{1,0:T(8,128)(2,1)S(1)}, u32[]{:S(2)}, u32[]{:S(2)}) collective-permute-start(bf16[96,1024]{1,0:T(8,128)(2,1)S(1)} %shard_map.105.after.d_ref), channel_id=1, source_target_pairs={{0,2},{1,3},{2,0},{3,1},{4,6},{5,7},{6,4},{7,5},{8,10},{9,11},{10,... | collective-permute-start | bytes 589832 | tf_op jit(solution)/shard_map/ppermute | solution.py:239
  14.7 4.4 %collective-permute-start.4 = (bf16[288,128]{1,0:T(8,128)(2,1)S(1)}, bf16[288,128]{1,0:T(8,128)(2,1)S(1)}, u32[]{:S(2)}, u32[]{:S(2)}) collective-permute-start(bf16[288,128]{1,0:T(8,128)(2,1)S(1)} %get-tuple-element.48), channel_id=1, source_target_pairs={{0,2},{1,3},{2,0},{3,1},{4,6},{5,7},{6,4},{7,5},{8,10},{9,11},{10,... | collective-permute-start | bytes 221192 | tf_op jit(solution)/shard_map/ppermute | solution.py:239
  19.2 2.5 %collective-permute-start.6 = (bf16[240,1024]{1,0:T(8,128)(2,1)S(1)}, bf16[240,1024]{1,0:T(8,128)(2,1)S(1)}, u32[]{:S(2)}, u32[]{:S(2)}) collective-permute-start(bf16[240,1024]{1,0:T(8,128)(2,1)S(1)} %shard_map.108.own_ref), channel_id=1, source_target_pairs={{0,1},{1,0},{2,3},{3,2},{4,5},{5,4},{6,7},{7,6},{8,9},{9,8},{10,11... | collective-permute-start | bytes 1474568 | tf_op jit(solution)/shard_map/ppermute | solution.py:239
  19.3 7.6 %collective-permute-start.3 = (bf16[24,2048]{1,0:T(8,128)(2,1)S(1)}, bf16[24,2048]{1,0:T(8,128)(2,1)S(1)}, u32[]{:S(2)}, u32[]{:S(2)}) collective-permute-start(bf16[24,2048]{1,0:T(8,128)(2,1)S(1)} %get-tuple-element.46), channel_id=1, source_target_pairs={{0,8},{8,0},{16,24},{24,16},{1,9},{9,1},{17,25},{25,17},{2,10},{10... | collective-permute-start | bytes 294920 | tf_op jit(solution)/shard_map/ppermute | solution.py:239
  20.6 6.4 %collective-permute-start.8 = (bf16[24,2048]{1,0:T(8,128)(2,1)S(1)}, bf16[24,2048]{1,0:T(8,128)(2,1)S(1)}, u32[]{:S(2)}, u32[]{:S(2)}) collective-permute-start(bf16[24,2048]{1,0:T(8,128)(2,1)S(1)} %get-tuple-element.51), channel_id=1, source_target_pairs={{0,24},{8,16},{16,8},{24,0},{1,25},{9,17},{17,9},{25,1},{2,26},{10... | collective-permute-start | bytes 294920 | tf_op jit(solution)/shard_map/ppermute | solution.py:239
  22.3 9.1 %collective-permute-start.9 = (bf16[96,1024]{1,0:T(8,128)(2,1)S(1)}, bf16[96,1024]{1,0:T(8,128)(2,1)S(1)}, u32[]{:S(2)}, u32[]{:S(2)}) collective-permute-start(bf16[96,1024]{1,0:T(8,128)(2,1)S(1)} %get-tuple-element.49.after), channel_id=1, source_target_pairs={{0,6},{1,7},{2,4},{3,5},{4,2},{5,3},{6,0},{7,1},{8,14},{9,15},{10,... | collective-permute-start | bytes 589832 | tf_op jit(solution)/shard_map/ppermute | solution.py:239
  25.5 4.7 %collective-permute-start.7 = (bf16[24,2048]{1,0:T(8,128)(2,1)S(1)}, bf16[24,2048]{1,0:T(8,128)(2,1)S(1)}, u32[]{:S(2)}, u32[]{:S(2)}) collective-permute-start(bf16[24,2048]{1,0:T(8,128)(2,1)S(1)} %shard_map.110), channel_id=1, source_target_pairs={{0,16},{8,24},{16,0},{24,8},{1,17},{9,25},{17,1},{25,9},{2,18},{10... | collective-permute-start | bytes 294920 | tf_op jit(solution)/shard_map/ppermute | solution.py:239

commit v6 on v5

--- a/solution.py
+++ b/solution.py
@@ -84,31 +84,32 @@
     pick = select.astype(BF16)
     gate_of = jnp.sum(gated, axis=1, keepdims=True)
     copies[3].wait()
-    chosen = dot(pick, x_ref[...]).astype(BF16)
+    chosen = dot(pick, x_ref[...])
     copies[4].wait()
-    grads = (gate_of * dot(pick, dy_ref[...])).astype(BF16)
+    grads = gate_of * dot(pick, dy_ref[...])
     for step in range(experts):
         at = slice(step * PAIR, (step + 1) * PAIR)
-        sends[step][:, :width] = chosen[at]
-        sends[step][:, width:] = grads[at]
-
-
-def weights_kernel(sel_ref, gsel_ref, gate_hbm, up_hbm, down_hbm, *refs):
-    gate_ref, up_ref, down_ref, pick_ref, high_ref, mid_ref, low_ref, sems = refs
+        sends[step][:, :width] = chosen[at].astype(BF16)
+        sends[step][:, width:] = grads[at].astype(BF16)
+
+
+def weights_kernel(parts, own_ref, sel_ref, gsel_ref, gate_hbm, up_hbm, down_hbm, *refs):
+    (gate_ref, up_ref, down_ref, first_ref), factors, sems = refs[:4], refs[4:-1], refs[-1]
+    first_ref[...] = own_ref[:, first_ref.shape[1] :]
     pairs = ((gate_hbm, gate_ref), (up_hbm, up_ref), (down_hbm, down_ref))
     copies = [
         pltpu.make_async_copy(src.at[0, 0], dst, sems.at[i]) for i, (src, dst) in enumerate(pairs)
     ]
     for copy in copies:
         copy.start()
-    pick_ref[...] = sel_ref[...].T.astype(BF16)
-    weight = gsel_ref[...].T
-    high = weight.astype(BF16)
-    rest = weight - high.astype(F32)
-    mid = rest.astype(BF16)
-    high_ref[...] = high
-    mid_ref[...] = mid
-    low_ref[...] = (rest - mid.astype(F32)).astype(BF16)
+    for i, steps in enumerate(parts):
+        rows = [slice(step * PAIR, (step + 1) * PAIR) for step in steps]
+        factors[2 * i][...] = jnp.concatenate([sel_ref[r] for r in rows], axis=0).T.astype(BF16)
+        weight = jnp.concatenate([gsel_ref[r] for r in rows], axis=0)
+        high = weight.astype(BF16).astype(F32)
+        mid = (weight - high).astype(BF16).astype(F32)
+        terms = jnp.concatenate([high, mid, weight - high - mid], axis=0)
+        factors[2 * i + 1][...] = terms.T.astype(BF16)
     for copy in copies:
         copy.wait()
 
@@ -119,8 +120,10 @@
 
 def join_kernel(experts, after, *refs):
     del after
-    blocks, d_ref = refs[:experts], refs[experts]
-    d_ref[...] = joined([b[:, d_ref.shape[1] :] for b in blocks])
+    blocks, (d_ref, others_ref) = refs[:experts], refs[experts:]
+    rows = [b[:, d_ref.shape[1] :] for b in blocks]
+    others_ref[...] = joined(rows[1:])
+    d_ref[...] = joined(rows)
 
 
 def forward_kernel(experts, chunk, units_of, after, *refs):
@@ -178,26 +181,28 @@
         outs[step][:, width:] = grad_s[rows, :].astype(BF16)
 
 
-def combine_kernel(experts, pick_ref, high_ref, mid_ref, low_ref, *refs):
-    blocks, (out_ref, grad_ref) = refs[:experts], refs[experts:]
+def combine_kernel(sums, pick_ref, terms_ref, *refs):
+    blocks, (out_ref, grad_ref) = refs[sums:-2], refs[-2:]
     width = out_ref.shape[1]
-    back = joined([b[...] for b in blocks])
-    result, d_rows = back[:, :width], back[:, width:]
-    total = dot(mid_ref[...], result) + dot(low_ref[...], result)
-    out_ref[...] = (dot(high_ref[...], result) + total).astype(BF16)
-    grad_ref[...] = dot(pick_ref[...], d_rows).astype(BF16)
+    results = [b[:, :width] for b in blocks]
+    total = dot(terms_ref[...], joined(3 * results))
+    grads = dot(pick_ref[...], joined([b[:, width:] for b in blocks]))
+    if sums:
+        total, grads = refs[0][...] + total, refs[1][...] + grads
+    out_ref[...] = total.astype(out_ref.dtype)
+    grad_ref[...] = grads.astype(grad_ref.dtype)
 
 
 def beside(parts):
     return jnp.concatenate([p.astype(F32) for p in parts], axis=1).astype(BF16)
 
 
-def pack_kernel(d_ref, far_ref, near_ht, far_ht, after, pair_ref):
+def pack_kernel(d_ref, first_ref, others_ref, near_ht, far_ht, after, pair_ref):
     del after
     rows, width = d_ref.shape
     share = near_ht.shape[0] // 4
     pair_ref[:rows] = d_ref[...]
-    pair_ref[rows : 2 * rows] = far_ref[...]
+    pair_ref[rows : 2 * rows] = joined([first_ref[...], others_ref[...]])
     pair_ref[2 * rows :] = jnp.zeros_like(pair_ref[2 * rows :])
     step = pair_ref.shape[0] - 2 * rows
     lanes = width // (4 * share // step)
@@ -239,7 +244,7 @@
     return lax.ppermute(value, axis, [(i, partner(i, step, count)) for i in range(count)])
 
 
-HELD = (2,)
+HELD = (3,)
 
 CORE, FAR, EXCHANGE = 1, 2, 6
 NEAR_UNITS = (0, EXCHANGE, CORE, CORE ^ EXCHANGE)
@@ -254,19 +259,19 @@
     return [[0]]
 
 
-def grad_by_rows(hts, d_out, after, groups):
+def grad_by_rows(hts, d_out, first, others, after, groups):
     near_ht, far_ht = hts
     rows, width = d_out.shape
     share = near_ht.shape[0] // 4
-    far = swap(d_out, "dp", groups, FAR)
+    first, others = swap(first, "dp", groups, FAR), swap(others, "dp", groups, FAR)
     far_ht = swap(far_ht, "dp", groups, FAR)
     extra = near_ht.shape[0] * 128 // width
     own = call(
         pack_kernel,
         0.2,
         jax.ShapeDtypeStruct((2 * rows + extra, width), BF16),
-        in_specs=[NEAR] * 4 + [ANY],
-    )(d_out, far, near_ht, far_ht, after)
+        in_specs=[NEAR] * 5 + [ANY],
+    )(d_out, first, others, near_ht, far_ht, after)
     pair = swap(own, "dp", groups, CORE)
     return call(
         functools.partial(outer_kernel, 1.0 / groups),
@@ -313,42 +318,48 @@
         ],
     )(ids, picks, gates, tokens, cotangent)
 
-    own_gate, own_up, own_down, *factors = call(
-        weights_kernel,
+    parts = [[step for step in range(experts) if step not in HELD], list(HELD)]
+    own_gate, own_up, own_down, first, *factors = call(
+        functools.partial(weights_kernel, parts),
         2.4,
         [
             jax.ShapeDtypeStruct((width, hidden_width), BF16),
             jax.ShapeDtypeStruct((width, hidden_width), BF16),
             jax.ShapeDtypeStruct((hidden_width, width), BF16),
+            jax.ShapeDtypeStruct((PAIR, width), BF16),
         ]
-        + [jax.ShapeDtypeStruct((tok_rows, rows), BF16)] * 4,
-        in_specs=[NEAR] * 2 + [HBM] * 3,
+        + [
+            jax.ShapeDtypeStruct((tok_rows, terms * PAIR * len(steps)), BF16)
+            for steps in parts
+            for terms in (1, 3)
+        ],
+        in_specs=[NEAR] * 3 + [HBM] * 3,
         scratch_shapes=[pltpu.SemaphoreType.DMA((3,))],
-    )(sel, gsel, w_gate, w_up, w_down)
+    )(sends[0], sel, gsel, w_gate, w_up, w_down)
 
     came = [sends[0]] + [swap(sends[s], "expert", experts, s) for s in range(1, experts)]
-    d_out = call(
+    d_out, others = call(
         functools.partial(join_kernel, experts),
         0.2,
-        jax.ShapeDtypeStruct((rows, width), BF16),
+        [jax.ShapeDtypeStruct((n, width), BF16) for n in (rows, rows - PAIR)],
         in_specs=[ANY] + [NEAR] * experts,
     )(own_gate, *came)
 
     share = hidden_width // groups
     short = groups == 8 and experts == 4 and share % 32 == 0
     if short:
-        parts = [
+        units = [
             jax.ShapeDtypeStruct((4 * share, rows), BF16),
             jax.ShapeDtypeStruct((3 * share, rows + rows // 3), BF16),
         ]
     else:
-        parts = [jax.ShapeDtypeStruct((hidden_width, rows), BF16)]
+        units = [jax.ShapeDtypeStruct((hidden_width, rows), BF16)]
     chunk = 256 if hidden_width % 256 == 0 else hidden_width
     kept = [jax.ShapeDtypeStruct((rows, hidden_width), t) for t in (BF16, F32, F32)]
     *hts, hidden, d_gate, silu = call(
         functools.partial(forward_kernel, experts, chunk, gathered_units if short else all_units),
         0.9,
-        parts + kept,
+        units + kept,
         in_specs=[ANY] + [NEAR] * (experts + 2),
         scratch_shapes=[pltpu.VMEM((rows, width), BF16), pltpu.VMEM((hidden_width, rows), BF16)],
     )(d_out, *came, own_gate, own_up)
@@ -364,7 +375,7 @@
     )(*came, own_gate, own_up, own_down, hidden, d_gate, silu))
 
     if short:
-        keep, give = grad_by_rows(hts, d_out, results[0], groups)
+        keep, give = grad_by_rows(hts, d_out, first, others, results[0], groups)
         grad = keep + swap(give, "dp", groups, EXCHANGE).astype(F32)
         freed = call(
             functools.partial(release_kernel, len(HELD)),
@@ -381,11 +392,14 @@
     home = [results[0]] + [
         swap(results[s], "expert", experts, s if pairs else experts - s) for s in range(1, experts)
     ]
-    layer_out, grad_tokens = call(
-        functools.partial(combine_kernel, experts),
-        0.1,
-        [jax.ShapeDtypeStruct((tok_rows, width), BF16)] * 2,
-    )(*factors, *home)
+    sums = []
+    for i, steps in enumerate(parts):
+        sums = call(
+            functools.partial(combine_kernel, len(sums)),
+            0.1,
+            [jax.ShapeDtypeStruct((tok_rows, width), BF16 if i else F32)] * 2,
+        )(*factors[2 * i : 2 * i + 2], *sums, *(home[step] for step in steps))
+    layer_out, grad_tokens = sums
     return layer_out, grad_tokens, grad[None]
 
 

time: 32.8 us -> 32.4 us (0.988); the launches traced: 32.2 us -> 32.2 us
  waiting for transfers between devices: 7.74 us -> 6.05 us
  starting transfers between devices: 13.8 us -> 15.4 us
    ppermute x10 -> x11, waiting for transfers between devices: 7.74 us -> 6.05 us  [swap(): lax.ppermute(value, axis, [(i, partner(i, step, count)) for i in range(co...]
    ppermute x10 -> x11, starting transfers between devices: 13.8 us -> 15.4 us  [swap(): lax.ppermute(value, axis, [(i, partner(i, step, count)) for i in range(co...]
    pallas_call x3 -> x4, Pallas kernels: 3.53 us -> 3.7 us  [the longest x1 2.38 us: on_device(): call(functools.partial(weights_kernel, parts), 2.4, [jax.ShapeDtypeStruct...]
  transfers between devices with their start and end apart: 10 -> 11, of which waited for: 5 -> 3; matrix products, arithmetic and copies ran while one was open for 0% -> 0% of each run, Pallas kernels for 23% -> 24%
where the time goes in v6:
time: 32.4 us; the launch traced here: 32.2 us
  starting transfers between devices  15.4 us (48%)
  Pallas kernels  9.28 us (29%)
  waiting for transfers between devices  6.05 us (19%)
  other arithmetic  0.79 us (2%)
  between operations  0.71 us (2%)
    ppermute x11, starting transfers between devices, swap(): lax.ppermute(value, axis, [(i, partner(i, step, count)) for i in range(co...  15.4 us
    ppermute x11, waiting for transfers between devices, swap(): lax.ppermute(value, axis, [(i, partner(i, step, count)) for i in range(co...  6.05 us
    pallas_call x1, Pallas kernels, on_device(): call(functools.partial(backward_kernel, experts, chunk), 2.6, [block] * e...  2.61 us
    pallas_call x1, Pallas kernels, on_device(): call(functools.partial(weights_kernel, parts), 2.4, [jax.ShapeDtypeStruct...  2.38 us
    pallas_call x1, Pallas kernels, on_device(): call(functools.partial(route_kernel, experts, choices), 1.4, [block] * ex...  1.46 us
    pallas_call x2, Pallas kernels, on_device(): call(functools.partial(combine_kernel, len(sums)), 0.1, [jax.ShapeDtypeSt...  1.3 us
    pallas_call x1, Pallas kernels, on_device(): call(functools.partial(forward_kernel, experts, chunk, gathered_units if...  0.86 us
    broadcast_in_dim x1, other arithmetic, on_device(): return (layer_out, grad_tokens, grad[None])  0.79 us
  transfers between devices with their start and end apart: 11, of which 3 were waited for; matrix products, arithmetic and copies ran while one was open for 0% of the time, Pallas kernels for 24%

profile of v6, /device:TPU:0, one launch (start us, length us, event | category | flops | bytes accessed | tf_op | source)
XLA Modules:
  0.0 32.2 jit_solution(3073782778279086046)
XLA Ops:
  0.6 1.5 %shard_map.103 = (bf16[24,2048]{1,0:T(8,128)(2,1)S(1)}, bf16[24,2048]{1,0:T(8,128)(2,1)S(1)}, bf16[24,2048]{1,0:T(8,128)(2,1)S(1)}, bf16[24,2048]{1,0:T(8,128)(2...) custom-call(s32[6,128]{1,0:T(8,128)} %bitcast.5, s32[6,128]{1,0:T(8,128)} %bitcast.6, f32[6,128]{1,0:T(8,128)} %bitcast.7, ...), custom_call_target="tpu_custom_call" | custom-call | flops 1400000000 | bytes 4200000 | tf_op jit(solution)/shard_map/pallas_call | solution.py:306
  2.1 3.0 %collective-permute-start = (bf16[24,2048]{1,0:T(8,128)(2,1)S(1)}, bf16[24,2048]{1,0:T(8,128)(2,1)S(1)}, u32[]{:S(2)}, u32[]{:S(2)}) collective-permute-start(bf16[24,2048]{1,0:T(8,128)(2,1)S(1)} %get-tuple-element.41), channel_id=1, source_target_pairs={{0,8},{8,0},{16,24},{24,16},{1,9},{9,1},{17,25},{25,17},{2,10},{10... | collective-permute-start | bytes 294920 | tf_op jit(solution)/shard_map/ppermute | solution.py:244
  5.1 1.5 %collective-permute-start.1 = (bf16[24,2048]{1,0:T(8,128)(2,1)S(1)}, bf16[24,2048]{1,0:T(8,128)(2,1)S(1)}, u32[]{:S(2)}, u32[]{:S(2)}) collective-permute-start(bf16[24,2048]{1,0:T(8,128)(2,1)S(1)} %get-tuple-element.42), channel_id=1, source_target_pairs={{0,16},{8,24},{16,0},{24,8},{1,17},{9,25},{17,1},{25,9},{2,18},{10... | collective-permute-start | bytes 294920 | tf_op jit(solution)/shard_map/ppermute | solution.py:244
  6.6 0.0 collective-permute-start.2
  6.6 2.4 %shard_map.104 = (bf16[1024,768]{1,0:T(8,128)(2,1)S(1)}, bf16[1024,768]{1,0:T(8,128)(2,1)S(1)}, bf16[768,1024]{1,0:T(8,128)(2,1)S(1)}, bf16[24,1024]{1,0:T(8,128...) custom-call(bf16[24,2048]{1,0:T(8,128)(2,1)S(1)} %get-tuple-element., ...), custom_call_target="tpu_custom_call" | custom-call | flops 2400000000 | bytes 7200000 | tf_op jit(solution)/shard_map/pallas_call | solution.py:322
  9.0 2.1 %collective-permute-start.6 = (bf16[24,1024]{1,0:T(8,128)(2,1)S(1)}, bf16[24,1024]{1,0:T(8,128)(2,1)S(1)}, u32[]{:S(2)}, u32[]{:S(2)}) collective-permute-start(bf16[24,1024]{1,0:T(8,128)(2,1)S(1)} %get-tuple-element.58), channel_id=1, source_target_pairs={{0,2},{1,3},{2,0},{3,1},{4,6},{5,7},{6,4},{7,5},{8,10},{9,11},{10,... | collective-permute-start | bytes 147464 | tf_op jit(solution)/shard_map/ppermute | solution.py:244
  11.1 0.0 collective-permute-done.refs_1_
  11.1 0.0 collective-permute-done.1.refs_2_
  11.1 1.0 %collective-permute-done.2.refs_3_ = bf16[24,2048]{1,0:T(8,128)(2,1)S(1)} collective-permute-done((bf16[24,2048]{1,0:T(8,128)(2,1)S(1)}, bf16[24,2048]{1,0:T(8,128)(2,1)S(1)}, u32[]{:S(2)}, u32[]{:S(2)}) %collective-permute-start.2) | collective-permute-done | bytes 98336 | tf_op jit(solution)/shard_map/ppermute | solution.py:244
  12.2 1.6 %collective-permute-start.7 = (bf16[72,1024]{1,0:T(8,128)(2,1)S(1)}, bf16[72,1024]{1,0:T(8,128)(2,1)S(1)}, u32[]{:S(2)}, u32[]{:S(2)}) collective-permute-start(bf16[72,1024]{1,0:T(8,128)(2,1)S(1)} %get-tuple-element.59), channel_id=1, source_target_pairs={{0,2},{1,3},{2,0},{3,1},{4,6},{5,7},{6,4},{7,5},{8,10},{9,11},{10,... | collective-permute-start | bytes 442376 | tf_op jit(solution)/shard_map/ppermute | solution.py:244
  13.8 0.9 %shard_map.106 = (bf16[384,96]{1,0:T(8,128)(2,1)S(1)}, bf16[288,128]{1,0:T(8,128)(2,1)S(1)}, bf16[96,768]{1,0:T(8,128)(2,1)S(1)}, f32[96,768]{1,0:T(8,128)S(1)}, f32[96,768]{1,0:T(8,128)S(1)}) custom-call(bf16[96,1024]{1,0:T(8,128)(2,1)S(1)} %get-tuple-element.47.after.d_ref, bf16[24,2048]{1,0:T(8,128)(2,1)S(1)} %get-tuple-element.34.own_ref.refs_0_, ...), custom_call_target="tpu_custom_call" | custom-call | flops 900000000 | bytes 2700000 | tf_op jit(solution)/shard_map/pallas_call | solution.py:359
  14.7 0.5 %collective-permute-start.5 = (bf16[288,128]{1,0:T(8,128)(2,1)S(1)}, bf16[288,128]{1,0:T(8,128)(2,1)S(1)}, u32[]{:S(2)}, u32[]{:S(2)}) collective-permute-start(bf16[288,128]{1,0:T(8,128)(2,1)S(1)} %get-tuple-element.57), channel_id=1, source_target_pairs={{0,2},{1,3},{2,0},{3,1},{4,6},{5,7},{6,4},{7,5},{8,10},{9,11},{10,... | collective-permute-start | bytes 221192 | tf_op jit(solution)/shard_map/ppermute | solution.py:244
  15.2 2.6 %shard_map.107 = (bf16[24,2048]{1,0:T(8,128)(2,1)S(1)}, bf16[24,2048]{1,0:T(8,128)(2,1)S(1)}, bf16[24,2048]{1,0:T(8,128)(2,1)S(1)}, bf16[24,2048]{1,0:T(8,128)(2,1)S(1)}) custom-call(bf16[24,2048]{1,0:T(8,128)(2,1)S(1)} %get-tuple-element.34.own_ref.refs_0_, bf16[24,2048]{1,0:T(8,128)(2,1)S(1)} %collective-permute-done.refs_1_, ...), custom_call_target="tpu_custom_call" | custom-call | flops 2600000000 | bytes 7800000 | tf_op jit(solution)/shard_map/pallas_call | solution.py:366
  17.8 0.0 collective-permute-done.6.first_ref
  17.8 1.3 %collective-permute-done.5.far_ht = bf16[288,128]{1,0:T(8,128)(2,1)S(1)} collective-permute-done((bf16[288,128]{1,0:T(8,128)(2,1)S(1)}, bf16[288,128]{1,0:T(8,128)(2,1)S(1)}, u32[]{:S(2)}, u32[]{:S(2)}) %collective-permute-start.5) | collective-permute-done | bytes 73760 | tf_op jit(solution)/shard_map/ppermute | solution.py:244
  19.1 0.0 collective-permute-done.7.others_ref
  19.1 0.1 shard_map.109.own_ref
  19.2 0.1 collective-permute-start.8
  19.3 0.8 %collective-permute-start.3 = (bf16[24,2048]{1,0:T(8,128)(2,1)S(1)}, bf16[24,2048]{1,0:T(8,128)(2,1)S(1)}, u32[]{:S(2)}, u32[]{:S(2)}) collective-permute-start(bf16[24,2048]{1,0:T(8,128)(2,1)S(1)} %get-tuple-element.52), channel_id=1, source_target_pairs={{0,8},{8,0},{16,24},{24,16},{1,9},{9,1},{17,25},{25,17},{2,10},{10... | collective-permute-start | bytes 294920 | tf_op jit(solution)/shard_map/ppermute | solution.py:244
  20.1 1.0 %collective-permute-start.4 = (bf16[24,2048]{1,0:T(8,128)(2,1)S(1)}, bf16[24,2048]{1,0:T(8,128)(2,1)S(1)}, u32[]{:S(2)}, u32[]{:S(2)}) collective-permute-start(bf16[24,2048]{1,0:T(8,128)(2,1)S(1)} %get-tuple-element.53), channel_id=1, source_target_pairs={{0,16},{8,24},{16,0},{24,8},{1,17},{9,25},{17,1},{25,9},{2,18},{10... | collective-permute-start | bytes 294920 | tf_op jit(solution)/shard_map/ppermute | solution.py:244
  21.1 0.0 collective-permute-done.8.pair_ref
  21.1 0.5 %shard_map.110 = (f32[96,1024]{1,0:T(8,128)S(1)}, bf16[96,1024]{1,0:T(8,128)(2,1)S(1)}) custom-call(bf16[384,96]{1,0:T(8,128)(2,1)S(1)} %get-tuple-element.56.near_ht, bf16[288,128]{1,0:T(8,128)(2,1)S(1)} %collective-permute-done.5.far_ht, bf16[240,1024]{1,0:T(8,128)(2,1)S(1)} %shard_map.109.own_ref, bf16[240,1024]{1,0:T(8,128)(2,1)S(1)} %collective-permute-done.8.pair_ref), custom_call_target="tpu_custom_call" | custom-call | flops 600000000 | bytes 1800000 | tf_op jit(solution)/shard_map/pallas_call | solution.py:276
  21.7 3.1 %collective-permute-start.10 = (bf16[96,1024]{1,0:T(8,128)(2,1)S(1)}, bf16[96,1024]{1,0:T(8,128)(2,1)S(1)}, u32[]{:S(2)}, u32[]{:S(2)}) collective-permute-start(bf16[96,1024]{1,0:T(8,128)(2,1)S(1)} %get-tuple-element.60.after), channel_id=1, source_target_pairs={{0,6},{1,7},{2,4},{3,5},{4,2},{5,3},{6,0},{7,1},{8,14},{9,15},{10,... | collective-permute-start | bytes 589832 | tf_op jit(solution)/shard_map/ppermute | solution.py:244
  24.8 1.5 %collective-permute-start.9 = (bf16[24,2048]{1,0:T(8,128)(2,1)S(1)}, bf16[24,2048]{1,0:T(8,128)(2,1)S(1)}, u32[]{:S(2)}, u32[]{:S(2)}) collective-permute-start(bf16[24,2048]{1,0:T(8,128)(2,1)S(1)} %shard_map.111), channel_id=1, source_target_pairs={{0,24},{8,16},{16,8},{24,0},{1,25},{9,17},{17,9},{25,1},{2,26},{10... | collective-permute-start | bytes 294920 | tf_op jit(solution)/shard_map/ppermute | solution.py:244
  26.3 0.0 collective-permute-done.3.refs_1_
  26.4 0.0 collective-permute-done.4.refs_2_
  26.4 0.3 shard_map.108
  26.7 3.7 %collective-permute-done.9.refs_2_ = bf16[24,2048]{1,0:T(8,128)(2,1)S(1)} collective-permute-done((bf16[24,2048]{1,0:T(8,128)(2,1)S(1)}, bf16[24,2048]{1,0:T(8,128)(2,1)S(1)}, u32[]{:S(2)}, u32[]{:S(2)}) %collective-permute-start.9) | collective-permute-done | bytes 98336 | tf_op jit(solution)/shard_map/ppermute | solution.py:244
  30.4 1.0 %shard_map.112 = (bf16[128,1024]{1,0:T(8,128)(2,1)}, bf16[128,1024]{1,0:T(8,128)(2,1)}) custom-call(bf16[128,24]{1,0:T(8,128)(2,1)S(1)} %get-tuple-element.37.pick_ref, bf16[128,72]{1,0:T(8,128)(2,1)S(1)} %get-tuple-element.38.terms_ref, f32[128,1024]{1,0:T(8,128)S(1)} %get-tuple-element.54.refs_0_, f32[128,1024]{1,0:T(8,128)S(1)} %get-tuple-element.55.refs_1_, ...), custom_call_target="tpu_custom_call" | custom-call | flops 100000000 | bytes 300000 | tf_op jit(solution)/shard_map/pallas_call | solution.py:397
  31.4 0.0 collective-permute-done.10
  31.4 0.8 %add_bitcast_fusion = f32[1,96,1024]{2,1,0:T(8,128)} fusion(f32[96,1024]{1,0:T(8,128)S(1)} %get-tuple-element.64, bf16[96,1024]{1,0:T(8,128)(2,1)S(1)} %collective-permute-done.10), kind=kLoop, calls=%fused_computation | loop fusion | flops 196608 | bytes 983040 | tf_op jit(solution)/shard_map/broadcast_in_dim | solution.py:403
  (2 shorter events, 0.0 us)
Async XLA Ops:
  2.1 9.0 %collective-permute-start = (bf16[24,2048]{1,0:T(8,128)(2,1)S(1)}, bf16[24,2048]{1,0:T(8,128)(2,1)S(1)}, u32[]{:S(2)}, u32[]{:S(2)}) collective-permute-start(bf16[24,2048]{1,0:T(8,128)(2,1)S(1)} %get-tuple-element.41), channel_id=1, source_target_pairs={{0,8},{8,0},{16,24},{24,16},{1,9},{9,1},{17,25},{25,17},{2,10},{10... | collective-permute-start | bytes 294920 | tf_op jit(solution)/shard_map/ppermute | solution.py:244
  5.1 6.0 %collective-permute-start.1 = (bf16[24,2048]{1,0:T(8,128)(2,1)S(1)}, bf16[24,2048]{1,0:T(8,128)(2,1)S(1)}, u32[]{:S(2)}, u32[]{:S(2)}) collective-permute-start(bf16[24,2048]{1,0:T(8,128)(2,1)S(1)} %get-tuple-element.42), channel_id=1, source_target_pairs={{0,16},{8,24},{16,0},{24,8},{1,17},{9,25},{17,1},{25,9},{2,18},{10... | collective-permute-start | bytes 294920 | tf_op jit(solution)/shard_map/ppermute | solution.py:244
  6.6 5.5 %collective-permute-start.2 = (bf16[24,2048]{1,0:T(8,128)(2,1)S(1)}, bf16[24,2048]{1,0:T(8,128)(2,1)S(1)}, u32[]{:S(2)}, u32[]{:S(2)}) collective-permute-start(bf16[24,2048]{1,0:T(8,128)(2,1)S(1)} %get-tuple-element.43), channel_id=1, source_target_pairs={{0,24},{8,16},{16,8},{24,0},{1,25},{9,17},{17,9},{25,1},{2,26},{10... | collective-permute-start | bytes 294920 | tf_op jit(solution)/shard_map/ppermute | solution.py:244
  9.0 8.8 %collective-permute-start.6 = (bf16[24,1024]{1,0:T(8,128)(2,1)S(1)}, bf16[24,1024]{1,0:T(8,128)(2,1)S(1)}, u32[]{:S(2)}, u32[]{:S(2)}) collective-permute-start(bf16[24,1024]{1,0:T(8,128)(2,1)S(1)} %get-tuple-element.58), channel_id=1, source_target_pairs={{0,2},{1,3},{2,0},{3,1},{4,6},{5,7},{6,4},{7,5},{8,10},{9,11},{10,... | collective-permute-start | bytes 147464 | tf_op jit(solution)/shard_map/ppermute | solution.py:244
  12.2 6.9 %collective-permute-start.7 = (bf16[72,1024]{1,0:T(8,128)(2,1)S(1)}, bf16[72,1024]{1,0:T(8,128)(2,1)S(1)}, u32[]{:S(2)}, u32[]{:S(2)}) collective-permute-start(bf16[72,1024]{1,0:T(8,128)(2,1)S(1)} %get-tuple-element.59), channel_id=1, source_target_pairs={{0,2},{1,3},{2,0},{3,1},{4,6},{5,7},{6,4},{7,5},{8,10},{9,11},{10,... | collective-permute-start | bytes 442376 | tf_op jit(solution)/shard_map/ppermute | solution.py:244
  14.7 4.4 %collective-permute-start.5 = (bf16[288,128]{1,0:T(8,128)(2,1)S(1)}, bf16[288,128]{1,0:T(8,128)(2,1)S(1)}, u32[]{:S(2)}, u32[]{:S(2)}) collective-permute-start(bf16[288,128]{1,0:T(8,128)(2,1)S(1)} %get-tuple-element.57), channel_id=1, source_target_pairs={{0,2},{1,3},{2,0},{3,1},{4,6},{5,7},{6,4},{7,5},{8,10},{9,11},{10,... | collective-permute-start | bytes 221192 | tf_op jit(solution)/shard_map/ppermute | solution.py:244
  19.2 1.9 %collective-permute-start.8 = (bf16[240,1024]{1,0:T(8,128)(2,1)S(1)}, bf16[240,1024]{1,0:T(8,128)(2,1)S(1)}, u32[]{:S(2)}, u32[]{:S(2)}) collective-permute-start(bf16[240,1024]{1,0:T(8,128)(2,1)S(1)} %shard_map.109.own_ref), channel_id=1, source_target_pairs={{0,1},{1,0},{2,3},{3,2},{4,5},{5,4},{6,7},{7,6},{8,9},{9,8},{10,11... | collective-permute-start | bytes 1474568 | tf_op jit(solution)/shard_map/ppermute | solution.py:244
  19.3 7.1 %collective-permute-start.3 = (bf16[24,2048]{1,0:T(8,128)(2,1)S(1)}, bf16[24,2048]{1,0:T(8,128)(2,1)S(1)}, u32[]{:S(2)}, u32[]{:S(2)}) collective-permute-start(bf16[24,2048]{1,0:T(8,128)(2,1)S(1)} %get-tuple-element.52), channel_id=1, source_target_pairs={{0,8},{8,0},{16,24},{24,16},{1,9},{9,1},{17,25},{25,17},{2,10},{10... | collective-permute-start | bytes 294920 | tf_op jit(solution)/shard_map/ppermute | solution.py:244
  20.1 6.3 %collective-permute-start.4 = (bf16[24,2048]{1,0:T(8,128)(2,1)S(1)}, bf16[24,2048]{1,0:T(8,128)(2,1)S(1)}, u32[]{:S(2)}, u32[]{:S(2)}) collective-permute-start(bf16[24,2048]{1,0:T(8,128)(2,1)S(1)} %get-tuple-element.53), channel_id=1, source_target_pairs={{0,16},{8,24},{16,0},{24,8},{1,17},{9,25},{17,1},{25,9},{2,18},{10... | collective-permute-start | bytes 294920 | tf_op jit(solution)/shard_map/ppermute | solution.py:244
  21.7 9.7 %collective-permute-start.10 = (bf16[96,1024]{1,0:T(8,128)(2,1)S(1)}, bf16[96,1024]{1,0:T(8,128)(2,1)S(1)}, u32[]{:S(2)}, u32[]{:S(2)}) collective-permute-start(bf16[96,1024]{1,0:T(8,128)(2,1)S(1)} %get-tuple-element.60.after), channel_id=1, source_target_pairs={{0,6},{1,7},{2,4},{3,5},{4,2},{5,3},{6,0},{7,1},{8,14},{9,15},{10,... | collective-permute-start | bytes 589832 | tf_op jit(solution)/shard_map/ppermute | solution.py:244
  24.8 5.6 %collective-permute-start.9 = (bf16[24,2048]{1,0:T(8,128)(2,1)S(1)}, bf16[24,2048]{1,0:T(8,128)(2,1)S(1)}, u32[]{:S(2)}, u32[]{:S(2)}) collective-permute-start(bf16[24,2048]{1,0:T(8,128)(2,1)S(1)} %shard_map.111), channel_id=1, source_target_pairs={{0,24},{8,16},{16,8},{24,0},{1,25},{9,17},{17,9},{25,1},{2,26},{10... | collective-permute-start | bytes 294920 | tf_op jit(solution)/shard_map/ppermute | solution.py:244

commit v7 on v6

--- a/solution.py
+++ b/solution.py
@@ -22,7 +22,12 @@
     return lax.dot_general(a, b, (contract, ((), ())), preferred_element_type=F32)
 
 
+ORDER = (0, 3, 2, 1)
+
+
 def partner(index, step, count):
+    if count == 4:
+        step = ORDER[step]
     if count & (count - 1) == 0:
         return index ^ step
     return (index + step) % count
@@ -244,7 +249,7 @@
     return lax.ppermute(value, axis, [(i, partner(i, step, count)) for i in range(count)])
 
 
-HELD = (3,)
+HELD = (1,)
 
 CORE, FAR, EXCHANGE = 1, 2, 6
 NEAR_UNITS = (0, EXCHANGE, CORE, CORE ^ EXCHANGE)

time: 32.4 us -> 32.3 us (level)
  waiting for transfers between devices: 6.05 us -> 5.1 us
  starting transfers between devices: 15.4 us -> 16.3 us
    ppermute x11, waiting for transfers between devices: 6.05 us -> 5.1 us  [swap(): lax.ppermute(value, axis, [(i, partner(i, step, count)) for i in range(co...]
    ppermute x11, starting transfers between devices: 15.4 us -> 16.3 us  [swap(): lax.ppermute(value, axis, [(i, partner(i, step, count)) for i in range(co...]
where the time goes in v7:
time: 32.3 us; the launch traced here: 32.2 us
  starting transfers between devices  16.3 us (50%)
  Pallas kernels  9.28 us (29%)
  waiting for transfers between devices  5.1 us (16%)
  other arithmetic  0.79 us (2%)
  between operations  0.71 us (2%)
    ppermute x11, starting transfers between devices, swap(): lax.ppermute(value, axis, [(i, partner(i, step, count)) for i in range(co...  16.3 us
    ppermute x11, waiting for transfers between devices, swap(): lax.ppermute(value, axis, [(i, partner(i, step, count)) for i in range(co...  5.1 us
    pallas_call x1, Pallas kernels, on_device(): call(functools.partial(backward_kernel, experts, chunk), 2.6, [block] * e...  2.61 us
    pallas_call x1, Pallas kernels, on_device(): call(functools.partial(weights_kernel, parts), 2.4, [jax.ShapeDtypeStruct...  2.38 us
    pallas_call x1, Pallas kernels, on_device(): call(functools.partial(route_kernel, experts, choices), 1.4, [block] * ex...  1.46 us
    pallas_call x2, Pallas kernels, on_device(): call(functools.partial(combine_kernel, len(sums)), 0.1, [jax.ShapeDtypeSt...  1.3 us
    pallas_call x1, Pallas kernels, on_device(): call(functools.partial(forward_kernel, experts, chunk, gathered_units if...  0.86 us
    broadcast_in_dim x1, other arithmetic, on_device(): return (layer_out, grad_tokens, grad[None])  0.79 us
  transfers between devices with their start and end apart: 11, of which 3 were waited for; matrix products, arithmetic and copies ran while one was open for 0% of the time, Pallas kernels for 24%

profile of v7, /device:TPU:0, one launch (start us, length us, event | category | flops | bytes accessed | tf_op | source)
XLA Modules:
  0.0 32.2 jit_solution(14941813783006776125)
XLA Ops:
  0.6 1.5 %shard_map.103 = (bf16[24,2048]{1,0:T(8,128)(2,1)S(1)}, bf16[24,2048]{1,0:T(8,128)(2,1)S(1)}, bf16[24,2048]{1,0:T(8,128)(2,1)S(1)}, bf16[24,2048]{1,0:T(8,128)(2...) custom-call(s32[6,128]{1,0:T(8,128)} %bitcast.5, s32[6,128]{1,0:T(8,128)} %bitcast.6, f32[6,128]{1,0:T(8,128)} %bitcast.7, ...), custom_call_target="tpu_custom_call" | custom-call | flops 1400000000 | bytes 4200000 | tf_op jit(solution)/shard_map/pallas_call | solution.py:311
  2.1 4.0 %collective-permute-start = (bf16[24,2048]{1,0:T(8,128)(2,1)S(1)}, bf16[24,2048]{1,0:T(8,128)(2,1)S(1)}, u32[]{:S(2)}, u32[]{:S(2)}) collective-permute-start(bf16[24,2048]{1,0:T(8,128)(2,1)S(1)} %get-tuple-element.41), channel_id=1, source_target_pairs={{0,24},{8,16},{16,8},{24,0},{1,25},{9,17},{17,9},{25,1},{2,26},{10... | collective-permute-start | bytes 294920 | tf_op jit(solution)/shard_map/ppermute | solution.py:249
  6.1 0.5 %collective-permute-start.1 = (bf16[24,2048]{1,0:T(8,128)(2,1)S(1)}, bf16[24,2048]{1,0:T(8,128)(2,1)S(1)}, u32[]{:S(2)}, u32[]{:S(2)}) collective-permute-start(bf16[24,2048]{1,0:T(8,128)(2,1)S(1)} %get-tuple-element.42), channel_id=1, source_target_pairs={{0,16},{8,24},{16,0},{24,8},{1,17},{9,25},{17,1},{25,9},{2,18},{10... | collective-permute-start | bytes 294920 | tf_op jit(solution)/shard_map/ppermute | solution.py:249
  6.6 0.1 collective-permute-start.2
  6.7 2.4 %shard_map.104 = (bf16[1024,768]{1,0:T(8,128)(2,1)S(1)}, bf16[1024,768]{1,0:T(8,128)(2,1)S(1)}, bf16[768,1024]{1,0:T(8,128)(2,1)S(1)}, bf16[24,1024]{1,0:T(8,128...) custom-call(bf16[24,2048]{1,0:T(8,128)(2,1)S(1)} %get-tuple-element., ...), custom_call_target="tpu_custom_call" | custom-call | flops 2400000000 | bytes 7200000 | tf_op jit(solution)/shard_map/pallas_call | solution.py:327
  9.1 2.0 %collective-permute-start.6 = (bf16[24,1024]{1,0:T(8,128)(2,1)S(1)}, bf16[24,1024]{1,0:T(8,128)(2,1)S(1)}, u32[]{:S(2)}, u32[]{:S(2)}) collective-permute-start(bf16[24,1024]{1,0:T(8,128)(2,1)S(1)} %get-tuple-element.58), channel_id=1, source_target_pairs={{0,2},{1,3},{2,0},{3,1},{4,6},{5,7},{6,4},{7,5},{8,10},{9,11},{10,... | collective-permute-start | bytes 147464 | tf_op jit(solution)/shard_map/ppermute | solution.py:249
  11.1 0.0 collective-permute-done.refs_1_
  11.1 0.0 collective-permute-done.1.refs_2_
  11.1 0.2 collective-permute-done.2.refs_3_
  11.3 1.6 %collective-permute-start.7 = (bf16[72,1024]{1,0:T(8,128)(2,1)S(1)}, bf16[72,1024]{1,0:T(8,128)(2,1)S(1)}, u32[]{:S(2)}, u32[]{:S(2)}) collective-permute-start(bf16[72,1024]{1,0:T(8,128)(2,1)S(1)} %get-tuple-element.59), channel_id=1, source_target_pairs={{0,2},{1,3},{2,0},{3,1},{4,6},{5,7},{6,4},{7,5},{8,10},{9,11},{10,... | collective-permute-start | bytes 442376 | tf_op jit(solution)/shard_map/ppermute | solution.py:249
  13.0 0.9 %shard_map.106 = (bf16[384,96]{1,0:T(8,128)(2,1)S(1)}, bf16[288,128]{1,0:T(8,128)(2,1)S(1)}, bf16[96,768]{1,0:T(8,128)(2,1)S(1)}, f32[96,768]{1,0:T(8,128)S(1)}, f32[96,768]{1,0:T(8,128)S(1)}) custom-call(bf16[96,1024]{1,0:T(8,128)(2,1)S(1)} %get-tuple-element.47.after.d_ref, bf16[24,2048]{1,0:T(8,128)(2,1)S(1)} %get-tuple-element.34.own_ref.refs_0_, ...), custom_call_target="tpu_custom_call" | custom-call | flops 900000000 | bytes 2700000 | tf_op jit(solution)/shard_map/pallas_call | solution.py:364
  13.8 0.5 %collective-permute-start.5 = (bf16[288,128]{1,0:T(8,128)(2,1)S(1)}, bf16[288,128]{1,0:T(8,128)(2,1)S(1)}, u32[]{:S(2)}, u32[]{:S(2)}) collective-permute-start(bf16[288,128]{1,0:T(8,128)(2,1)S(1)} %get-tuple-element.57), channel_id=1, source_target_pairs={{0,2},{1,3},{2,0},{3,1},{4,6},{5,7},{6,4},{7,5},{8,10},{9,11},{10,... | collective-permute-start | bytes 221192 | tf_op jit(solution)/shard_map/ppermute | solution.py:249
  14.3 2.6 %shard_map.107 = (bf16[24,2048]{1,0:T(8,128)(2,1)S(1)}, bf16[24,2048]{1,0:T(8,128)(2,1)S(1)}, bf16[24,2048]{1,0:T(8,128)(2,1)S(1)}, bf16[24,2048]{1,0:T(8,128)(2,1)S(1)}) custom-call(bf16[24,2048]{1,0:T(8,128)(2,1)S(1)} %get-tuple-element.34.own_ref.refs_0_, bf16[24,2048]{1,0:T(8,128)(2,1)S(1)} %collective-permute-done.refs_1_, ...), custom_call_target="tpu_custom_call" | custom-call | flops 2600000000 | bytes 7800000 | tf_op jit(solution)/shard_map/pallas_call | solution.py:371
  17.0 0.0 collective-permute-done.6.first_ref
  17.0 1.3 %collective-permute-done.5.far_ht = bf16[288,128]{1,0:T(8,128)(2,1)S(1)} collective-permute-done((bf16[288,128]{1,0:T(8,128)(2,1)S(1)}, bf16[288,128]{1,0:T(8,128)(2,1)S(1)}, u32[]{:S(2)}, u32[]{:S(2)}) %collective-permute-start.5) | collective-permute-done | bytes 73760 | tf_op jit(solution)/shard_map/ppermute | solution.py:249
  18.2 0.0 collective-permute-done.7.others_ref
  18.2 0.1 shard_map.109.own_ref
  18.3 0.1 collective-permute-start.8
  18.4 1.8 %collective-permute-start.3 = (bf16[24,2048]{1,0:T(8,128)(2,1)S(1)}, bf16[24,2048]{1,0:T(8,128)(2,1)S(1)}, u32[]{:S(2)}, u32[]{:S(2)}) collective-permute-start(bf16[24,2048]{1,0:T(8,128)(2,1)S(1)} %get-tuple-element.52), channel_id=1, source_target_pairs={{0,16},{8,24},{16,0},{24,8},{1,17},{9,25},{17,1},{25,9},{2,18},{10... | collective-permute-start | bytes 294920 | tf_op jit(solution)/shard_map/ppermute | solution.py:249
  20.3 0.8 %collective-permute-start.4 = (bf16[24,2048]{1,0:T(8,128)(2,1)S(1)}, bf16[24,2048]{1,0:T(8,128)(2,1)S(1)}, u32[]{:S(2)}, u32[]{:S(2)}) collective-permute-start(bf16[24,2048]{1,0:T(8,128)(2,1)S(1)} %get-tuple-element.53), channel_id=1, source_target_pairs={{0,8},{8,0},{16,24},{24,16},{1,9},{9,1},{17,25},{25,17},{2,10},{10... | collective-permute-start | bytes 294920 | tf_op jit(solution)/shard_map/ppermute | solution.py:249
  21.1 0.0 collective-permute-done.8.pair_ref
  21.1 0.6 %shard_map.110 = (f32[96,1024]{1,0:T(8,128)S(1)}, bf16[96,1024]{1,0:T(8,128)(2,1)S(1)}) custom-call(bf16[384,96]{1,0:T(8,128)(2,1)S(1)} %get-tuple-element.56.near_ht, bf16[288,128]{1,0:T(8,128)(2,1)S(1)} %collective-permute-done.5.far_ht, bf16[240,1024]{1,0:T(8,128)(2,1)S(1)} %shard_map.109.own_ref, bf16[240,1024]{1,0:T(8,128)(2,1)S(1)} %collective-permute-done.8.pair_ref), custom_call_target="tpu_custom_call" | custom-call | flops 600000000 | bytes 1800000 | tf_op jit(solution)/shard_map/pallas_call | solution.py:281
  21.7 3.1 %collective-permute-start.10 = (bf16[96,1024]{1,0:T(8,128)(2,1)S(1)}, bf16[96,1024]{1,0:T(8,128)(2,1)S(1)}, u32[]{:S(2)}, u32[]{:S(2)}) collective-permute-start(bf16[96,1024]{1,0:T(8,128)(2,1)S(1)} %get-tuple-element.60.after), channel_id=1, source_target_pairs={{0,6},{1,7},{2,4},{3,5},{4,2},{5,3},{6,0},{7,1},{8,14},{9,15},{10,... | collective-permute-start | bytes 589832 | tf_op jit(solution)/shard_map/ppermute | solution.py:249
  24.8 1.6 %collective-permute-start.9 = (bf16[24,2048]{1,0:T(8,128)(2,1)S(1)}, bf16[24,2048]{1,0:T(8,128)(2,1)S(1)}, u32[]{:S(2)}, u32[]{:S(2)}) collective-permute-start(bf16[24,2048]{1,0:T(8,128)(2,1)S(1)} %shard_map.111), channel_id=1, source_target_pairs={{0,24},{8,16},{16,8},{24,0},{1,25},{9,17},{17,9},{25,1},{2,26},{10... | collective-permute-start | bytes 294920 | tf_op jit(solution)/shard_map/ppermute | solution.py:249
  26.4 0.0 collective-permute-done.3.refs_1_
  26.4 0.0 collective-permute-done.4.refs_2_
  26.4 0.3 shard_map.108
  26.7 3.6 %collective-permute-done.9.refs_2_ = bf16[24,2048]{1,0:T(8,128)(2,1)S(1)} collective-permute-done((bf16[24,2048]{1,0:T(8,128)(2,1)S(1)}, bf16[24,2048]{1,0:T(8,128)(2,1)S(1)}, u32[]{:S(2)}, u32[]{:S(2)}) %collective-permute-start.9) | collective-permute-done | bytes 98336 | tf_op jit(solution)/shard_map/ppermute | solution.py:249
  30.4 1.0 %shard_map.112 = (bf16[128,1024]{1,0:T(8,128)(2,1)}, bf16[128,1024]{1,0:T(8,128)(2,1)}) custom-call(bf16[128,24]{1,0:T(8,128)(2,1)S(1)} %get-tuple-element.37.pick_ref, bf16[128,72]{1,0:T(8,128)(2,1)S(1)} %get-tuple-element.38.terms_ref, f32[128,1024]{1,0:T(8,128)S(1)} %get-tuple-element.54.refs_0_, f32[128,1024]{1,0:T(8,128)S(1)} %get-tuple-element.55.refs_1_, ...), custom_call_target="tpu_custom_call" | custom-call | flops 100000000 | bytes 300000 | tf_op jit(solution)/shard_map/pallas_call | solution.py:402
  31.4 0.0 collective-permute-done.10
  31.4 0.8 %add_bitcast_fusion = f32[1,96,1024]{2,1,0:T(8,128)} fusion(f32[96,1024]{1,0:T(8,128)S(1)} %get-tuple-element.64, bf16[96,1024]{1,0:T(8,128)(2,1)S(1)} %collective-permute-done.10), kind=kLoop, calls=%fused_computation | loop fusion | flops 196608 | bytes 983040 | tf_op jit(solution)/shard_map/broadcast_in_dim | solution.py:408
  (2 shorter events, 0.0 us)
Async XLA Ops:
  2.1 9.0 %collective-permute-start = (bf16[24,2048]{1,0:T(8,128)(2,1)S(1)}, bf16[24,2048]{1,0:T(8,128)(2,1)S(1)}, u32[]{:S(2)}, u32[]{:S(2)}) collective-permute-start(bf16[24,2048]{1,0:T(8,128)(2,1)S(1)} %get-tuple-element.41), channel_id=1, source_target_pairs={{0,24},{8,16},{16,8},{24,0},{1,25},{9,17},{17,9},{25,1},{2,26},{10... | collective-permute-start | bytes 294920 | tf_op jit(solution)/shard_map/ppermute | solution.py:249
  6.1 5.1 %collective-permute-start.1 = (bf16[24,2048]{1,0:T(8,128)(2,1)S(1)}, bf16[24,2048]{1,0:T(8,128)(2,1)S(1)}, u32[]{:S(2)}, u32[]{:S(2)}) collective-permute-start(bf16[24,2048]{1,0:T(8,128)(2,1)S(1)} %get-tuple-element.42), channel_id=1, source_target_pairs={{0,16},{8,24},{16,0},{24,8},{1,17},{9,25},{17,1},{25,9},{2,18},{10... | collective-permute-start | bytes 294920 | tf_op jit(solution)/shard_map/ppermute | solution.py:249
  6.6 4.7 %collective-permute-start.2 = (bf16[24,2048]{1,0:T(8,128)(2,1)S(1)}, bf16[24,2048]{1,0:T(8,128)(2,1)S(1)}, u32[]{:S(2)}, u32[]{:S(2)}) collective-permute-start(bf16[24,2048]{1,0:T(8,128)(2,1)S(1)} %get-tuple-element.43), channel_id=1, source_target_pairs={{0,8},{8,0},{16,24},{24,16},{1,9},{9,1},{17,25},{25,17},{2,10},{10... | collective-permute-start | bytes 294920 | tf_op jit(solution)/shard_map/ppermute | solution.py:249
  9.1 7.9 %collective-permute-start.6 = (bf16[24,1024]{1,0:T(8,128)(2,1)S(1)}, bf16[24,1024]{1,0:T(8,128)(2,1)S(1)}, u32[]{:S(2)}, u32[]{:S(2)}) collective-permute-start(bf16[24,1024]{1,0:T(8,128)(2,1)S(1)} %get-tuple-element.58), channel_id=1, source_target_pairs={{0,2},{1,3},{2,0},{3,1},{4,6},{5,7},{6,4},{7,5},{8,10},{9,11},{10,... | collective-permute-start | bytes 147464 | tf_op jit(solution)/shard_map/ppermute | solution.py:249
  11.3 6.9 %collective-permute-start.7 = (bf16[72,1024]{1,0:T(8,128)(2,1)S(1)}, bf16[72,1024]{1,0:T(8,128)(2,1)S(1)}, u32[]{:S(2)}, u32[]{:S(2)}) collective-permute-start(bf16[72,1024]{1,0:T(8,128)(2,1)S(1)} %get-tuple-element.59), channel_id=1, source_target_pairs={{0,2},{1,3},{2,0},{3,1},{4,6},{5,7},{6,4},{7,5},{8,10},{9,11},{10,... | collective-permute-start | bytes 442376 | tf_op jit(solution)/shard_map/ppermute | solution.py:249
  13.8 4.4 %collective-permute-start.5 = (bf16[288,128]{1,0:T(8,128)(2,1)S(1)}, bf16[288,128]{1,0:T(8,128)(2,1)S(1)}, u32[]{:S(2)}, u32[]{:S(2)}) collective-permute-start(bf16[288,128]{1,0:T(8,128)(2,1)S(1)} %get-tuple-element.57), channel_id=1, source_target_pairs={{0,2},{1,3},{2,0},{3,1},{4,6},{5,7},{6,4},{7,5},{8,10},{9,11},{10,... | collective-permute-start | bytes 221192 | tf_op jit(solution)/shard_map/ppermute | solution.py:249
  18.3 2.8 %collective-permute-start.8 = (bf16[240,1024]{1,0:T(8,128)(2,1)S(1)}, bf16[240,1024]{1,0:T(8,128)(2,1)S(1)}, u32[]{:S(2)}, u32[]{:S(2)}) collective-permute-start(bf16[240,1024]{1,0:T(8,128)(2,1)S(1)} %shard_map.109.own_ref), channel_id=1, source_target_pairs={{0,1},{1,0},{2,3},{3,2},{4,5},{5,4},{6,7},{7,6},{8,9},{9,8},{10,11... | collective-permute-start | bytes 1474568 | tf_op jit(solution)/shard_map/ppermute | solution.py:249
  18.4 8.0 %collective-permute-start.3 = (bf16[24,2048]{1,0:T(8,128)(2,1)S(1)}, bf16[24,2048]{1,0:T(8,128)(2,1)S(1)}, u32[]{:S(2)}, u32[]{:S(2)}) collective-permute-start(bf16[24,2048]{1,0:T(8,128)(2,1)S(1)} %get-tuple-element.52), channel_id=1, source_target_pairs={{0,16},{8,24},{16,0},{24,8},{1,17},{9,25},{17,1},{25,9},{2,18},{10... | collective-permute-start | bytes 294920 | tf_op jit(solution)/shard_map/ppermute | solution.py:249
  20.3 6.2 %collective-permute-start.4 = (bf16[24,2048]{1,0:T(8,128)(2,1)S(1)}, bf16[24,2048]{1,0:T(8,128)(2,1)S(1)}, u32[]{:S(2)}, u32[]{:S(2)}) collective-permute-start(bf16[24,2048]{1,0:T(8,128)(2,1)S(1)} %get-tuple-element.53), channel_id=1, source_target_pairs={{0,8},{8,0},{16,24},{24,16},{1,9},{9,1},{17,25},{25,17},{2,10},{10... | collective-permute-start | bytes 294920 | tf_op jit(solution)/shard_map/ppermute | solution.py:249
  21.7 9.7 %collective-permute-start.10 = (bf16[96,1024]{1,0:T(8,128)(2,1)S(1)}, bf16[96,1024]{1,0:T(8,128)(2,1)S(1)}, u32[]{:S(2)}, u32[]{:S(2)}) collective-permute-start(bf16[96,1024]{1,0:T(8,128)(2,1)S(1)} %get-tuple-element.60.after), channel_id=1, source_target_pairs={{0,6},{1,7},{2,4},{3,5},{4,2},{5,3},{6,0},{7,1},{8,14},{9,15},{10,... | collective-permute-start | bytes 589832 | tf_op jit(solution)/shard_map/ppermute | solution.py:249
  24.8 5.6 %collective-permute-start.9 = (bf16[24,2048]{1,0:T(8,128)(2,1)S(1)}, bf16[24,2048]{1,0:T(8,128)(2,1)S(1)}, u32[]{:S(2)}, u32[]{:S(2)}) collective-permute-start(bf16[24,2048]{1,0:T(8,128)(2,1)S(1)} %shard_map.111), channel_id=1, source_target_pairs={{0,24},{8,16},{16,8},{24,0},{1,25},{9,17},{17,9},{25,1},{2,26},{10... | collective-permute-start | bytes 294920 | tf_op jit(solution)/shard_map/ppermute | solution.py:249

commit v8 on v6

--- a/solution.py
+++ b/solution.py
@@ -120,10 +120,8 @@
 
 def join_kernel(experts, after, *refs):
     del after
-    blocks, (d_ref, others_ref) = refs[:experts], refs[experts:]
-    rows = [b[:, d_ref.shape[1] :] for b in blocks]
-    others_ref[...] = joined(rows[1:])
-    d_ref[...] = joined(rows)
+    blocks, others_ref = refs[: experts - 1], refs[experts - 1]
+    others_ref[...] = joined([b[:, others_ref.shape[1] :] for b in blocks])
 
 
 def forward_kernel(experts, chunk, units_of, after, *refs):
@@ -338,12 +336,12 @@
     )(sends[0], sel, gsel, w_gate, w_up, w_down)
 
     came = [sends[0]] + [swap(sends[s], "expert", experts, s) for s in range(1, experts)]
-    d_out, others = call(
+    others = call(
         functools.partial(join_kernel, experts),
         0.2,
-        [jax.ShapeDtypeStruct((n, width), BF16) for n in (rows, rows - PAIR)],
-        in_specs=[ANY] + [NEAR] * experts,
-    )(own_gate, *came)
+        jax.ShapeDtypeStruct((rows - PAIR, width), BF16),
+        in_specs=[ANY] + [NEAR] * (experts - 1),
+    )(own_gate, *came[1:])
 
     share = hidden_width // groups
     short = groups == 8 and experts == 4 and share % 32 == 0
@@ -362,17 +360,17 @@
         units + kept,
         in_specs=[ANY] + [NEAR] * (experts + 2),
         scratch_shapes=[pltpu.VMEM((rows, width), BF16), pltpu.VMEM((hidden_width, rows), BF16)],
-    )(d_out, *came, own_gate, own_up)
+    )(others, *came, own_gate, own_up)
     results = list(call(
         functools.partial(backward_kernel, experts, chunk),
         2.6,
-        [block] * experts,
+        [block] * experts + [jax.ShapeDtypeStruct((rows, width), BF16)],
         scratch_shapes=[
-            pltpu.VMEM((rows, width), BF16),
             pltpu.VMEM((rows, width), F32),
             pltpu.VMEM((rows, width), F32),
         ],
     )(*came, own_gate, own_up, own_down, hidden, d_gate, silu))
+    d_out = results.pop()
 
     if short:
         keep, give = grad_by_rows(hts, d_out, first, others, results[0], groups)

time: 32.4 us -> 32.4 us (level)
  no operation moved by 1% of the time
where the time goes in v8:
time: 32.4 us; the launch traced here: 32.2 us
  starting transfers between devices  15.4 us (48%)
  Pallas kernels  9.28 us (29%)
  waiting for transfers between devices  6.05 us (19%)
  other arithmetic  0.8 us (2%)
  between operations  0.71 us (2%)
    ppermute x11, starting transfers between devices, swap(): lax.ppermute(value, axis, [(i, partner(i, step, count)) for i in range(co...  15.4 us
    ppermute x11, waiting for transfers between devices, swap(): lax.ppermute(value, axis, [(i, partner(i, step, count)) for i in range(co...  6.05 us
    pallas_call x1, Pallas kernels, on_device(): call(functools.partial(backward_kernel, experts, chunk), 2.6, [block] * e...  2.63 us
    pallas_call x1, Pallas kernels, on_device(): call(functools.partial(weights_kernel, parts), 2.4, [jax.ShapeDtypeStruct...  2.38 us
    pallas_call x1, Pallas kernels, on_device(): call(functools.partial(route_kernel, experts, choices), 1.4, [block] * ex...  1.46 us
    pallas_call x2, Pallas kernels, on_device(): call(functools.partial(combine_kernel, len(sums)), 0.1, [jax.ShapeDtypeSt...  1.3 us
    pallas_call x1, Pallas kernels, on_device(): call(functools.partial(forward_kernel, experts, chunk, gathered_units if...  0.86 us
    broadcast_in_dim x1, other arithmetic, on_device(): return (layer_out, grad_tokens, grad[None])  0.8 us
  transfers between devices with their start and end apart: 11, of which 3 were waited for; matrix products, arithmetic and copies ran while one was open for 0% of the time, Pallas kernels for 24%

profile of v8, /device:TPU:0, one launch (start us, length us, event | category | flops | bytes accessed | tf_op | source)
XLA Modules:
  0.0 32.2 jit_solution(16825133791308855502)
XLA Ops:
  0.6 1.5 %shard_map.103 = (bf16[24,2048]{1,0:T(8,128)(2,1)S(1)}, bf16[24,2048]{1,0:T(8,128)(2,1)S(1)}, bf16[24,2048]{1,0:T(8,128)(2,1)S(1)}, bf16[24,2048]{1,0:T(8,128)(2...) custom-call(s32[6,128]{1,0:T(8,128)} %bitcast.5, s32[6,128]{1,0:T(8,128)} %bitcast.6, f32[6,128]{1,0:T(8,128)} %bitcast.7, ...), custom_call_target="tpu_custom_call" | custom-call | flops 1400000000 | bytes 4200000 | tf_op jit(solution)/shard_map/pallas_call | solution.py:304
  2.1 3.0 %collective-permute-start = (bf16[24,2048]{1,0:T(8,128)(2,1)S(1)}, bf16[24,2048]{1,0:T(8,128)(2,1)S(1)}, u32[]{:S(2)}, u32[]{:S(2)}) collective-permute-start(bf16[24,2048]{1,0:T(8,128)(2,1)S(1)} %get-tuple-element.40), channel_id=1, source_target_pairs={{0,8},{8,0},{16,24},{24,16},{1,9},{9,1},{17,25},{25,17},{2,10},{10... | collective-permute-start | bytes 294920 | tf_op jit(solution)/shard_map/ppermute | solution.py:242
  5.1 1.5 %collective-permute-start.1 = (bf16[24,2048]{1,0:T(8,128)(2,1)S(1)}, bf16[24,2048]{1,0:T(8,128)(2,1)S(1)}, u32[]{:S(2)}, u32[]{:S(2)}) collective-permute-start(bf16[24,2048]{1,0:T(8,128)(2,1)S(1)} %get-tuple-element.41), channel_id=1, source_target_pairs={{0,16},{8,24},{16,0},{24,8},{1,17},{9,25},{17,1},{25,9},{2,18},{10... | collective-permute-start | bytes 294920 | tf_op jit(solution)/shard_map/ppermute | solution.py:242
  6.6 0.0 collective-permute-start.2
  6.6 2.4 %shard_map.104 = (bf16[1024,768]{1,0:T(8,128)(2,1)S(1)}, bf16[1024,768]{1,0:T(8,128)(2,1)S(1)}, bf16[768,1024]{1,0:T(8,128)(2,1)S(1)}, bf16[24,1024]{1,0:T(8,128...) custom-call(bf16[24,2048]{1,0:T(8,128)(2,1)S(1)} %get-tuple-element., ...), custom_call_target="tpu_custom_call" | custom-call | flops 2400000000 | bytes 7200000 | tf_op jit(solution)/shard_map/pallas_call | solution.py:320
  9.0 2.1 %collective-permute-start.6 = (bf16[24,1024]{1,0:T(8,128)(2,1)S(1)}, bf16[24,1024]{1,0:T(8,128)(2,1)S(1)}, u32[]{:S(2)}, u32[]{:S(2)}) collective-permute-start(bf16[24,1024]{1,0:T(8,128)(2,1)S(1)} %get-tuple-element.57), channel_id=1, source_target_pairs={{0,2},{1,3},{2,0},{3,1},{4,6},{5,7},{6,4},{7,5},{8,10},{9,11},{10,... | collective-permute-start | bytes 147464 | tf_op jit(solution)/shard_map/ppermute | solution.py:242
  11.1 0.0 collective-permute-done.refs_0_.refs_1_
  11.1 0.0 collective-permute-done.1.refs_1_.refs_2_
  11.1 1.0 %collective-permute-done.2.refs_2_.refs_3_ = bf16[24,2048]{1,0:T(8,128)(2,1)S(1)} collective-permute-done((bf16[24,2048]{1,0:T(8,128)(2,1)S(1)}, bf16[24,2048]{1,0:T(8,128)(2,1)S(1)}, u32[]{:S(2)}, u32[]{:S(2)}) %collective-permute-start.2) | collective-permute-done | bytes 98336 | tf_op jit(solution)/shard_map/ppermute | solution.py:242
  12.2 1.6 %collective-permute-start.7 = (bf16[72,1024]{1,0:T(8,128)(2,1)S(1)}, bf16[72,1024]{1,0:T(8,128)(2,1)S(1)}, u32[]{:S(2)}, u32[]{:S(2)}) collective-permute-start(bf16[72,1024]{1,0:T(8,128)(2,1)S(1)} %shard_map.105.after), channel_id=1, source_target_pairs={{0,2},{1,3},{2,0},{3,1},{4,6},{5,7},{6,4},{7,5},{8,10},{9,11},{10,... | collective-permute-start | bytes 442376 | tf_op jit(solution)/shard_map/ppermute | solution.py:242
  13.8 0.9 %shard_map.106 = (bf16[384,96]{1,0:T(8,128)(2,1)S(1)}, bf16[288,128]{1,0:T(8,128)(2,1)S(1)}, bf16[96,768]{1,0:T(8,128)(2,1)S(1)}, f32[96,768]{1,0:T(8,128)S(1)}, f32[96,768]{1,0:T(8,128)S(1)}) custom-call(bf16[72,1024]{1,0:T(8,128)(2,1)S(1)} %shard_map.105.after, bf16[24,2048]{1,0:T(8,128)(2,1)S(1)} %get-tuple-element.33.own_ref.refs_0_, ...), custom_call_target="tpu_custom_call" | custom-call | flops 900000000 | bytes 2700000 | tf_op jit(solution)/shard_map/pallas_call | solution.py:357
  14.7 0.5 %collective-permute-start.5 = (bf16[288,128]{1,0:T(8,128)(2,1)S(1)}, bf16[288,128]{1,0:T(8,128)(2,1)S(1)}, u32[]{:S(2)}, u32[]{:S(2)}) collective-permute-start(bf16[288,128]{1,0:T(8,128)(2,1)S(1)} %get-tuple-element.55), channel_id=1, source_target_pairs={{0,2},{1,3},{2,0},{3,1},{4,6},{5,7},{6,4},{7,5},{8,10},{9,11},{10,... | collective-permute-start | bytes 221192 | tf_op jit(solution)/shard_map/ppermute | solution.py:242
  15.2 2.6 %shard_map.107 = (bf16[24,2048]{1,0:T(8,128)(2,1)S(1)}, bf16[24,2048]{1,0:T(8,128)(2,1)S(1)}, bf16[24,2048]{1,0:T(8,128)(2,1)S(1)}, bf16[24,2048]{1,0:T(8,128)(2,1)S(1)}, bf16[96,1024]{1,0:T(8,128)(2,1)S(1)}) custom-call(bf16[24,2048]{1,0:T(8,128)(2,1)S(1)} %get-tuple-element.33.own_ref.refs_0_, bf16[24,2048]{1,0:T(8,128)(2,1)S(1)} %collective-permute-done.refs_0_.refs_1_, ...), custom_call_target="tpu_custom_call" | custom-call | flops 2600000000 | bytes 7800000 | tf_op jit(solution)/shard_map/pallas_call | solution.py:364
  17.8 0.0 collective-permute-done.6.first_ref
  17.8 1.2 %collective-permute-done.5.far_ht = bf16[288,128]{1,0:T(8,128)(2,1)S(1)} collective-permute-done((bf16[288,128]{1,0:T(8,128)(2,1)S(1)}, bf16[288,128]{1,0:T(8,128)(2,1)S(1)}, u32[]{:S(2)}, u32[]{:S(2)}) %collective-permute-start.5) | collective-permute-done | bytes 73760 | tf_op jit(solution)/shard_map/ppermute | solution.py:242
  19.1 0.0 collective-permute-done.7.others_ref
  19.1 0.1 shard_map.109.own_ref
  19.2 0.1 collective-permute-start.8
  19.3 0.8 %collective-permute-start.3 = (bf16[24,2048]{1,0:T(8,128)(2,1)S(1)}, bf16[24,2048]{1,0:T(8,128)(2,1)S(1)}, u32[]{:S(2)}, u32[]{:S(2)}) collective-permute-start(bf16[24,2048]{1,0:T(8,128)(2,1)S(1)} %get-tuple-element.50), channel_id=1, source_target_pairs={{0,8},{8,0},{16,24},{24,16},{1,9},{9,1},{17,25},{25,17},{2,10},{10... | collective-permute-start | bytes 294920 | tf_op jit(solution)/shard_map/ppermute | solution.py:242
  20.1 1.0 %collective-permute-start.4 = (bf16[24,2048]{1,0:T(8,128)(2,1)S(1)}, bf16[24,2048]{1,0:T(8,128)(2,1)S(1)}, u32[]{:S(2)}, u32[]{:S(2)}) collective-permute-start(bf16[24,2048]{1,0:T(8,128)(2,1)S(1)} %get-tuple-element.51), channel_id=1, source_target_pairs={{0,16},{8,24},{16,0},{24,8},{1,17},{9,25},{17,1},{25,9},{2,18},{10... | collective-permute-start | bytes 294920 | tf_op jit(solution)/shard_map/ppermute | solution.py:242
  21.1 0.0 collective-permute-done.8.pair_ref
  21.1 0.5 %shard_map.110 = (f32[96,1024]{1,0:T(8,128)S(1)}, bf16[96,1024]{1,0:T(8,128)(2,1)S(1)}) custom-call(bf16[384,96]{1,0:T(8,128)(2,1)S(1)} %get-tuple-element.54.near_ht, bf16[288,128]{1,0:T(8,128)(2,1)S(1)} %collective-permute-done.5.far_ht, bf16[240,1024]{1,0:T(8,128)(2,1)S(1)} %shard_map.109.own_ref, bf16[240,1024]{1,0:T(8,128)(2,1)S(1)} %collective-permute-done.8.pair_ref), custom_call_target="tpu_custom_call" | custom-call | flops 600000000 | bytes 1800000 | tf_op jit(solution)/shard_map/pallas_call | solution.py:274
  21.7 3.1 %collective-permute-start.10 = (bf16[96,1024]{1,0:T(8,128)(2,1)S(1)}, bf16[96,1024]{1,0:T(8,128)(2,1)S(1)}, u32[]{:S(2)}, u32[]{:S(2)}) collective-permute-start(bf16[96,1024]{1,0:T(8,128)(2,1)S(1)} %get-tuple-element.58.after), channel_id=1, source_target_pairs={{0,6},{1,7},{2,4},{3,5},{4,2},{5,3},{6,0},{7,1},{8,14},{9,15},{10,... | collective-permute-start | bytes 589832 | tf_op jit(solution)/shard_map/ppermute | solution.py:242
  24.8 1.5 %collective-permute-start.9 = (bf16[24,2048]{1,0:T(8,128)(2,1)S(1)}, bf16[24,2048]{1,0:T(8,128)(2,1)S(1)}, u32[]{:S(2)}, u32[]{:S(2)}) collective-permute-start(bf16[24,2048]{1,0:T(8,128)(2,1)S(1)} %shard_map.111), channel_id=1, source_target_pairs={{0,24},{8,16},{16,8},{24,0},{1,25},{9,17},{17,9},{25,1},{2,26},{10... | collective-permute-start | bytes 294920 | tf_op jit(solution)/shard_map/ppermute | solution.py:242
  26.3 0.0 collective-permute-done.3.refs_1_
  26.3 0.0 collective-permute-done.4.refs_2_
  26.4 0.3 shard_map.108
  26.7 3.7 %collective-permute-done.9.refs_2_ = bf16[24,2048]{1,0:T(8,128)(2,1)S(1)} collective-permute-done((bf16[24,2048]{1,0:T(8,128)(2,1)S(1)}, bf16[24,2048]{1,0:T(8,128)(2,1)S(1)}, u32[]{:S(2)}, u32[]{:S(2)}) %collective-permute-start.9) | collective-permute-done | bytes 98336 | tf_op jit(solution)/shard_map/ppermute | solution.py:242
  30.4 1.0 %shard_map.112 = (bf16[128,1024]{1,0:T(8,128)(2,1)}, bf16[128,1024]{1,0:T(8,128)(2,1)}) custom-call(bf16[128,24]{1,0:T(8,128)(2,1)S(1)} %get-tuple-element.36.pick_ref, bf16[128,72]{1,0:T(8,128)(2,1)S(1)} %get-tuple-element.37.terms_ref, f32[128,1024]{1,0:T(8,128)S(1)} %get-tuple-element.52.refs_0_, f32[128,1024]{1,0:T(8,128)S(1)} %get-tuple-element.53.refs_1_, ...), custom_call_target="tpu_custom_call" | custom-call | flops 100000000 | bytes 300000 | tf_op jit(solution)/shard_map/pallas_call | solution.py:395
  31.4 0.0 collective-permute-done.10
  31.4 0.8 %add_bitcast_fusion = f32[1,96,1024]{2,1,0:T(8,128)} fusion(f32[96,1024]{1,0:T(8,128)S(1)} %get-tuple-element.62, bf16[96,1024]{1,0:T(8,128)(2,1)S(1)} %collective-permute-done.10), kind=kLoop, calls=%fused_computation | loop fusion | flops 196608 | bytes 983040 | tf_op jit(solution)/shard_map/broadcast_in_dim | solution.py:401
  (2 shorter events, 0.0 us)
Async XLA Ops:
  2.1 9.0 %collective-permute-start = (bf16[24,2048]{1,0:T(8,128)(2,1)S(1)}, bf16[24,2048]{1,0:T(8,128)(2,1)S(1)}, u32[]{:S(2)}, u32[]{:S(2)}) collective-permute-start(bf16[24,2048]{1,0:T(8,128)(2,1)S(1)} %get-tuple-element.40), channel_id=1, source_target_pairs={{0,8},{8,0},{16,24},{24,16},{1,9},{9,1},{17,25},{25,17},{2,10},{10... | collective-permute-start | bytes 294920 | tf_op jit(solution)/shard_map/ppermute | solution.py:242
  5.1 6.0 %collective-permute-start.1 = (bf16[24,2048]{1,0:T(8,128)(2,1)S(1)}, bf16[24,2048]{1,0:T(8,128)(2,1)S(1)}, u32[]{:S(2)}, u32[]{:S(2)}) collective-permute-start(bf16[24,2048]{1,0:T(8,128)(2,1)S(1)} %get-tuple-element.41), channel_id=1, source_target_pairs={{0,16},{8,24},{16,0},{24,8},{1,17},{9,25},{17,1},{25,9},{2,18},{10... | collective-permute-start | bytes 294920 | tf_op jit(solution)/shard_map/ppermute | solution.py:242
  6.6 5.5 %collective-permute-start.2 = (bf16[24,2048]{1,0:T(8,128)(2,1)S(1)}, bf16[24,2048]{1,0:T(8,128)(2,1)S(1)}, u32[]{:S(2)}, u32[]{:S(2)}) collective-permute-start(bf16[24,2048]{1,0:T(8,128)(2,1)S(1)} %get-tuple-element.42), channel_id=1, source_target_pairs={{0,24},{8,16},{16,8},{24,0},{1,25},{9,17},{17,9},{25,1},{2,26},{10... | collective-permute-start | bytes 294920 | tf_op jit(solution)/shard_map/ppermute | solution.py:242
  9.0 8.8 %collective-permute-start.6 = (bf16[24,1024]{1,0:T(8,128)(2,1)S(1)}, bf16[24,1024]{1,0:T(8,128)(2,1)S(1)}, u32[]{:S(2)}, u32[]{:S(2)}) collective-permute-start(bf16[24,1024]{1,0:T(8,128)(2,1)S(1)} %get-tuple-element.57), channel_id=1, source_target_pairs={{0,2},{1,3},{2,0},{3,1},{4,6},{5,7},{6,4},{7,5},{8,10},{9,11},{10,... | collective-permute-start | bytes 147464 | tf_op jit(solution)/shard_map/ppermute | solution.py:242
  12.2 6.9 %collective-permute-start.7 = (bf16[72,1024]{1,0:T(8,128)(2,1)S(1)}, bf16[72,1024]{1,0:T(8,128)(2,1)S(1)}, u32[]{:S(2)}, u32[]{:S(2)}) collective-permute-start(bf16[72,1024]{1,0:T(8,128)(2,1)S(1)} %shard_map.105.after), channel_id=1, source_target_pairs={{0,2},{1,3},{2,0},{3,1},{4,6},{5,7},{6,4},{7,5},{8,10},{9,11},{10,... | collective-permute-start | bytes 442376 | tf_op jit(solution)/shard_map/ppermute | solution.py:242
  14.7 4.4 %collective-permute-start.5 = (bf16[288,128]{1,0:T(8,128)(2,1)S(1)}, bf16[288,128]{1,0:T(8,128)(2,1)S(1)}, u32[]{:S(2)}, u32[]{:S(2)}) collective-permute-start(bf16[288,128]{1,0:T(8,128)(2,1)S(1)} %get-tuple-element.55), channel_id=1, source_target_pairs={{0,2},{1,3},{2,0},{3,1},{4,6},{5,7},{6,4},{7,5},{8,10},{9,11},{10,... | collective-permute-start | bytes 221192 | tf_op jit(solution)/shard_map/ppermute | solution.py:242
  19.2 1.9 %collective-permute-start.8 = (bf16[240,1024]{1,0:T(8,128)(2,1)S(1)}, bf16[240,1024]{1,0:T(8,128)(2,1)S(1)}, u32[]{:S(2)}, u32[]{:S(2)}) collective-permute-start(bf16[240,1024]{1,0:T(8,128)(2,1)S(1)} %shard_map.109.own_ref), channel_id=1, source_target_pairs={{0,1},{1,0},{2,3},{3,2},{4,5},{5,4},{6,7},{7,6},{8,9},{9,8},{10,11... | collective-permute-start | bytes 1474568 | tf_op jit(solution)/shard_map/ppermute | solution.py:242
  19.3 7.1 %collective-permute-start.3 = (bf16[24,2048]{1,0:T(8,128)(2,1)S(1)}, bf16[24,2048]{1,0:T(8,128)(2,1)S(1)}, u32[]{:S(2)}, u32[]{:S(2)}) collective-permute-start(bf16[24,2048]{1,0:T(8,128)(2,1)S(1)} %get-tuple-element.50), channel_id=1, source_target_pairs={{0,8},{8,0},{16,24},{24,16},{1,9},{9,1},{17,25},{25,17},{2,10},{10... | collective-permute-start | bytes 294920 | tf_op jit(solution)/shard_map/ppermute | solution.py:242
  20.1 6.3 %collective-permute-start.4 = (bf16[24,2048]{1,0:T(8,128)(2,1)S(1)}, bf16[24,2048]{1,0:T(8,128)(2,1)S(1)}, u32[]{:S(2)}, u32[]{:S(2)}) collective-permute-start(bf16[24,2048]{1,0:T(8,128)(2,1)S(1)} %get-tuple-element.51), channel_id=1, source_target_pairs={{0,16},{8,24},{16,0},{24,8},{1,17},{9,25},{17,1},{25,9},{2,18},{10... | collective-permute-start | bytes 294920 | tf_op jit(solution)/shard_map/ppermute | solution.py:242
  21.7 9.7 %collective-permute-start.10 = (bf16[96,1024]{1,0:T(8,128)(2,1)S(1)}, bf16[96,1024]{1,0:T(8,128)(2,1)S(1)}, u32[]{:S(2)}, u32[]{:S(2)}) collective-permute-start(bf16[96,1024]{1,0:T(8,128)(2,1)S(1)} %get-tuple-element.58.after), channel_id=1, source_target_pairs={{0,6},{1,7},{2,4},{3,5},{4,2},{5,3},{6,0},{7,1},{8,14},{9,15},{10,... | collective-permute-start | bytes 589832 | tf_op jit(solution)/shard_map/ppermute | solution.py:242
  24.8 5.6 %collective-permute-start.9 = (bf16[24,2048]{1,0:T(8,128)(2,1)S(1)}, bf16[24,2048]{1,0:T(8,128)(2,1)S(1)}, u32[]{:S(2)}, u32[]{:S(2)}) collective-permute-start(bf16[24,2048]{1,0:T(8,128)(2,1)S(1)} %shard_map.111), channel_id=1, source_target_pairs={{0,24},{8,16},{16,8},{24,0},{1,25},{9,17},{17,9},{25,1},{2,26},{10... | collective-permute-start | bytes 294920 | tf_op jit(solution)/shard_map/ppermute | solution.py:242
